TPU v7x, 32 devices: a whole 2x2x4 slice. The times are simulated.
32 devices in a mesh: dp: 8 (over z, x), fsdp: 4 (over y, core).
Axes of the slice: x: 2, y: 2, z: 4, core: 2. Of those that a mesh axis runs over, the one named last changes fastest.
Arguments:
- tokens: bfloat16 [32768, 512], P(('dp', 'fsdp')), may hold values from -6 to 6
- cotangent: bfloat16 [32768, 512], P(('dp', 'fsdp')), may hold values from -6 to 6
- attention_params: bfloat16 [1048576], P(('dp', 'fsdp')), may hold values from -0.25 to 0.25
- feedforward_params: bfloat16 [2097152], P(('dp', 'fsdp')), may hold values from -0.25 to 0.25
- bias_params: bfloat16 [4096], P(('dp', 'fsdp')), may hold values from -3 to 3
- branch_gates: float32 [2], replicated, may hold values from 0.5 to 2
- bucket_counts: int32 [32, 3], P(('dp', 'fsdp')), may hold values from 0 to 8, as said below
- valid_lengths: int32 [32, 8], P(('dp', 'fsdp')), may hold values from 0 to 1024, as said below
Outputs:
- layer_output: bfloat16 [32768, 512], P(('dp', 'fsdp'))
- input_grad: float32 [32768, 512], P(('dp', 'fsdp'))
- attention_grad: float32 [1048576], P(('dp', 'fsdp'))
- feedforward_grad: float32 [2097152], P(('dp', 'fsdp'))
- bias_grad: float32 [4096], P(('dp', 'fsdp'))
- gate_grad: float32 [2], replicated
Inputs may be any that keep to these rules, and one draw needn't show every extreme that they name: `bucket_counts`: row r counts slots of 128, 512 and 1024 rows in that order; the slots fill exactly 1024 rows. `valid_lengths`: entry (r, s) lies between half the size of slot s of buffer r (rounded up) and that size, and is 0 for slots beyond the buffer's count.
All inputs are finite; a program needn't handle non-finite values.
Results may differ from a plain program's by a relative error of at most 0.012.
The roundings to bfloat16 on the way count: a program that leaves them out, or rounds other values in their place, can miss the bound.
Values may be sent and summed in bfloat16 or wider, within the bound.
No kernel may reach another device: no remote copies, remote signals or barrier semaphores. Data moves between devices by JAX's collectives and lax.ppermute only.
A program may use at most 128 MiB of HBM per device.

v0:
```python
from functools import partial

import jax
import jax.numpy as jnp
from jax import lax
from jax.experimental import pallas as pl
from jax.experimental.pallas import tpu as pltpu
from jax.sharding import PartitionSpec as P

D = 512
H = 8
HD = 64
FF = 2048
ROWS = 1024
SLOTS = 8
SHORT = 128
MID = 512
LONG = 1024
AXES = ("dp", "fsdp")
PARTS = 32
A_TILES = 17
F_TILES = 32
G_TILES = 33
BF = jnp.bfloat16
F32 = jnp.float32
CHUNK = 64
SHARE = 6 * 64
BIG = 512
VMEM = pl.BlockSpec(memory_space=pltpu.VMEM)
SMEM = pl.BlockSpec(memory_space=pltpu.SMEM)
ANY = pl.BlockSpec(memory_space=pl.ANY)
DMA = pltpu.SemaphoreType.DMA


def nn(a, b):
    return lax.dot_general(a, b, (((1,), (0,)), ((), ())), preferred_element_type=F32)


def nt(a, b):
    return lax.dot_general(a, b, (((1,), (1,)), ((), ())), preferred_element_type=F32)


def call(body, outs, ins, scratch, flops, moved, limit, grid=None):
    return pl.pallas_call(
        body,
        out_shape=[jax.ShapeDtypeStruct(o[0], o[1]) for o in outs],
        grid=grid or (),
        in_specs=ins,
        out_specs=[o[2] if len(o) > 2 else VMEM for o in outs],
        scratch_shapes=[pltpu.VMEM(*s) if isinstance(s, tuple) else s for s in scratch],
        compiler_params=pltpu.CompilerParams(vmem_limit_bytes=limit << 20),
        cost_estimate=pl.CostEstimate(flops=flops, bytes_accessed=moved, transcendentals=0),
    )


def slot_masks(counts, lengths, keys_out, rows_out):
    lane = lax.broadcasted_iota(jnp.int32, (1, 128), 1)
    slot = lane & 63
    longs, mids, shorts = counts[0, 2], counts[0, 1], counts[0, 0]
    in_long = jnp.minimum(slot, longs)
    in_mid = jnp.clip(slot - longs, 0, mids)
    in_short = jnp.clip(slot - longs - mids, 0, shorts)
    start = in_long * LONG + in_mid * MID + in_short * SHORT
    size = jnp.where(
        slot < longs,
        LONG,
        jnp.where(slot < longs + mids, MID, jnp.where(slot < longs + mids + shorts, SHORT, 0)),
    )
    valid = jnp.zeros((1, 128), jnp.int32)
    for s in range(SLOTS):
        valid = jnp.where(slot == s, lengths[0, s], valid)
    row = lax.broadcasted_iota(jnp.int32, (ROWS, 128), 0)
    member = (row >= start) & (row < start + size)
    usable = (row >= start) & (row < start + valid)
    for parity in range(2):
        here = (slot < SLOTS) & ((lane >= 64) if parity == 0 else (lane < 64))
        rows_out[parity] = jnp.where(here & member, 1.0, 0.0).astype(BF)
        keys_out[parity] = jnp.where(here & jnp.logical_not(usable), -1e30, 0.0).astype(BF)


def prepare_body(counts, lengths, tok, keys_mask, rows_mask, x_t):
    slot_masks(counts, lengths, keys_mask, rows_mask)
    x_t[:D] = tok[...].T
    x_t[D:] = jnp.ones((16, ROWS), BF)


def half_of(parity, shape):
    lane = lax.broadcasted_iota(jnp.int32, shape, len(shape) - 1)
    return (lane < 64) if parity == 0 else (lane >= 64)


def assemble(pieces, dest, me):
    for c in range(2):
        for xy in range(4):
            for z in range(4):
                dest[(8 * z + 2 * xy + c) ^ me] = pieces[4 * c + xy][z]


def columns(ref, owners, tiles, each):
    parts = []
    for t in range(tiles.start, tiles.stop, each):
        part = ref[owners, t : t + each]
        parts.append(part.reshape(part.shape[0] * each * 16, 128))
    return jnp.concatenate(parts, axis=1)


def square(ref, index):
    return columns(ref, slice(8 * index, 8 * index + 8), slice(0, 16), 4)


def project_body(place, tok, keys_mask, rows_mask, *refs):
    pieces, (q_out, k_out, v_out, w_out, bias_out) = refs[:8], refs[8:]
    assemble(pieces, w_out, place[0])
    for o in range(PARTS):
        bias_out[0:1, 128 * o : 128 * o + 128] = w_out[o, A_TILES - 1].astype(F32)[0:1]
    for r in range(4):
        at = slice(256 * r, 256 * r + 256)
        x = tok[at, :]
        q = (nn(x, square(w_out, 0)) + bias_out[0:1, 0:D]).astype(BF)
        q = (q.astype(F32) * 0.125).astype(BF)
        k = nn(x, square(w_out, 1)).astype(BF)
        v_out[at, :] = (nn(x, square(w_out, 2)) + bias_out[0:1, D : 2 * D]).astype(BF)
        for h in range(H):
            mine = half_of(h % 2, (256, 128))
            lanes = slice(h // 2 * 128, h // 2 * 128 + 128)
            q_out[h, at] = jnp.where(mine, q[:, lanes], rows_mask[h % 2, at])
            k_out[h, at] = jnp.where(mine, k[:, lanes], keys_mask[h % 2, at])


def attend_body(q_all, k_all, v_all, ctx_out, ctx_t_out, lse_out, values_t, ctx_t, s0, s1, p0, p1):
    def pair(p, _):
        attend_pair(
            p, q_all.at[pl.ds(2 * p, 2)], k_all.at[pl.ds(2 * p, 2)], v_all, ctx_out, ctx_t_out, lse_out, values_t, ctx_t,
            s0, s1, p0, p1,
        )
        return 0

    lax.fori_loop(0, 4, pair, 0)
    ctx_t_out[D:] = jnp.ones((16, ROWS), BF)


def attend_pair(p, q_in, k_in, v_all, ctx_out, ctx_t_out, lse_out, values_t, ctx_t, s0, s1, p0, p1):
    lanes = pl.ds(pl.multiple_of(p * 128, 128), 128)
    scores, probs = (s0, s1), (p0, p1)
    values_t[...] = v_all[:, lanes].T
    steps = [(parity, r) for parity in range(2) for r in range(4)]

    def score(i):
        parity, r = steps[i]

        def part(c):
            scores[i % 2][c : c + 256] = nt(k_in[parity, c : c + 256], q_in[parity, r * 256 : r * 256 + 256])

        return [partial(part, c) for c in range(0, ROWS, 256)]

    def collect(i):
        parity, r = steps[i]
        rows = slice(64 * parity, 64 * parity + 64)
        total = []

        def part(c):
            total.append(nn(values_t[rows, c : c + 256], probs[i % 2][c : c + 256]))
            if c == ROWS - 256:
                ctx_t[rows, r * 256 : r * 256 + 256] = (total[0] + total[1]) + (total[2] + total[3])

        return [partial(part, c) for c in range(0, ROWS, 256)]

    def soften(i):
        parity, r = steps[i]
        s, out = scores[i % 2], probs[i % 2]
        state = {}

        def peak(c):
            part = jnp.max(s[c : c + CHUNK].reshape(-1, 8, 256), axis=0)
            state["top"] = jnp.maximum(state["top"], part) if c else part
            if c == ROWS - CHUNK:
                state["top"] = jnp.max(state["top"], axis=0, keepdims=True)

        def power(c):
            e = jnp.exp(s[c : c + CHUNK] - state["top"])
            s[c : c + CHUNK] = e
            part = jnp.sum(e.reshape(-1, 8, 256), axis=0)
            state["mass"] = state["mass"] + part if c else part
            if c == ROWS - CHUNK:
                mass = jnp.sum(state["mass"], axis=0, keepdims=True)
                lse_out[pl.ds(2 * p + parity, 1), r * 256 : r * 256 + 256] = state["top"] + jnp.log(mass)
                state["share"] = 1.0 / mass

        def share(c):
            out[c : c + CHUNK] = (s[c : c + CHUNK] * state["share"]).astype(BF)

        at = range(0, ROWS, CHUNK)
        return [(1, partial(peak, c)) for c in at] + [(3, partial(power, c)) for c in at] + [
            (1.5, partial(share, c)) for c in at
        ]

    for task in score(0):
        task()
    for i in range(9):
        later = (score(i + 1) if i < 7 else []) + (collect(i - 1) if i else [])
        mix(soften(i) if i < 8 else [], later)
    low = ctx_t[...].astype(BF)
    ctx_t_out[lanes, :] = low
    ctx_out[:, lanes] = low.T


def mix(vector, matrix):
    whole = sum(weight for weight, _ in vector) or 1
    done, given = 0, 0
    for weight, task in vector:
        while given < len(matrix) and given * whole <= done * len(matrix):
            matrix[given]()
            given += 1
        task()
        done += weight
    for task in matrix[given:]:
        task()


def feed_body(place, gates, tok, cot, ctx, ctx_t, w_in, bias, *refs):
    pieces, refs = refs[:8], refs[8:]
    (layer_out, gm, gctx, keep_out, send_out, wo_keep, wo_send) = refs[:7]
    (w, low_t, gbr, gs_all, active_t, gh_all, v0, v1, b0, b1, active, second, gmid, sums) = refs[7:21]
    (layer, both, sems) = refs[21:]
    values, backs = (v0, v1), (b0, b1)
    wo = w_in.at[24:32]
    assemble(pieces, w, place[0])

    def rows_of(r):
        return pl.ds(pl.multiple_of(r * 256, 256), 256)

    ga, gf = gates[0], gates[1]
    c1 = 0.7978845608028654
    c2 = 0.044715
    ones = jnp.ones((16, ROWS), BF)
    low_t[D:] = ones
    active_t[FF:] = ones

    def w_up(j):
        return columns(w, slice(0, 16), slice(8 * j, 8 * j + 8), 2)

    def w_down(j):
        return columns(w, slice(16 + 4 * j, 20 + 4 * j), slice(0, 32), 8)

    def rows(r, carry):
        attend_sum, feed_sum = carry
        at = rows_of(r)
        br = nn(ctx[at, :], square(wo, 0)) + bias[0:1, 2 * D : 3 * D]
        middle = tok[at, :].astype(F32) + ga * br
        low = middle.astype(BF)
        low_t[:D, at] = low.T
        ct = cot[at, :].astype(F32)
        gs = (gf * ct).astype(BF)
        gs_all[at, :] = gs

        def first(j):
            up, down = w_up(j), w_down(j)

            def value(n):
                values[j % 2][:, n : n + 256] = nn(low, up[:, n : n + 256])

            def back(n):
                backs[j % 2][:, n : n + 256] = nt(gs, down[n : n + 256])

            return [partial(f, n) for n in (0, 256) for f in (value, back)]

        def bend(j):
            def part(c):
                lines = slice(c, c + 32)
                cols = slice(4 * D + 512 * j, 4 * D + 512 * j + 512)
                v = values[j % 2][lines] + bias[0:1, cols]
                v2 = v * v
                t = jnp.tanh(v * (c1 + (c1 * c2) * v2))
                half = 0.5 + 0.5 * t
                act = v * half
                slope = half * (1.0 + (v - act) * (2.0 * c1 + (6.0 * c1 * c2) * v2))
                active[lines, 512 * j : 512 * j + 512] = act.astype(BF)
                gh_all[pl.ds(r * 256 + c, 32), 512 * j : 512 * j + 512] = (slope * backs[j % 2][lines]).astype(BF)

            return [(1, partial(part, c)) for c in range(0, 256, 32)]

        def then(j):
            up, down = w_up(j), w_down(j)
            cols = slice(512 * j, 512 * j + 512)

            def forward(n):
                val = nn(active[:, cols], down[:, n : n + 256])
                second[:, n : n + 256] = second[:, n : n + 256] + val if j else val

            def backward(n):
                val = nt(gh_all[at, cols], up[n : n + 256])
                gmid[:, n : n + 256] = gmid[:, n : n + 256] + val if j else val

            def turn():
                active_t[cols, at] = active[:, cols].T

            return [turn] + [partial(f, n) for n in (0, 256) for f in (forward, backward)]

        for task in first(0):
            task()
        for j in range(5):
            mix(bend(j) if j < 4 else [], (first(j + 1) if j < 3 else []) + (then(j - 1) if j else []))
        out = second[...] + bias[0:1, 3 * D : 4 * D]
        layer[at, :] = (middle + gf * out).astype(BF)
        grad = ct + gmid[...]
        gm[at, :] = grad
        gb = (ga * grad).astype(BF)
        gbr[at, :] = gb
        gctx[at, :] = nt(gb, square(wo, 0)).astype(BF)
        pltpu.make_async_copy(layer.at[at], layer_out.at[at], sems.at[0]).start()
        attend_sum = attend_sum + jnp.sum(br * grad, axis=0, keepdims=True)
        feed_sum = feed_sum + jnp.sum(out * ct, axis=0, keepdims=True)
        return attend_sum, feed_sum

    zero = jnp.zeros((1, D), F32)
    attend_sum, feed_sum = lax.fori_loop(0, 4, rows, (zero, zero))
    odd = place[1]

    def send(slots, sem):
        copies = [
            pltpu.make_async_copy(both.at[0, slots], keep_out.at[slots], sems.at[sem]),
            pltpu.make_async_copy(both.at[1, slots], send_out.at[slots], sems.at[sem + 1]),
        ]
        for copy in copies:
            copy.start()
        return copies

    for j in range(4):
        val = nn(low_t[...], gh_all[:, 512 * j : 512 * j + 512])
        sums[0:1, 4 * D + 512 * j : 4 * D + 512 * j + 512] = val[D : D + 1]
        for o in range(16):
            for jj in range(4):
                for i in range(2):
                    top, col = 32 * o + 16 * i, slice(128 * jj, 128 * jj + 128)
                    both[(o % 2) ^ odd, o // 2, 2 * (4 * j + jj) + i] = val[top : top + 16, col]
    val = nn(ctx_t[...], gbr[...])
    sums[0:1, 2 * D : 3 * D] = val[D : D + 1]
    for o in range(0, 8, 2):
        for j in range(4):
            for i in range(4):
                top, col = 64 * o + 16 * i, slice(128 * j, 128 * j + 128)
                even, other = val[top : top + 16, col], val[top + 64 : top + 80, col]
                wo_keep[o // 2, 4 * j + i] = jnp.where(odd == 1, other, even)
                wo_send[o // 2, 4 * j + i] = jnp.where(odd == 1, even, other)
    copies = []
    lane = lax.broadcasted_iota(jnp.int32, (1, 128), 1)
    gate = jnp.where(lane == 2 * place[2], jnp.sum(attend_sum), 0.0)
    gate = jnp.where(lane == 2 * place[2] + 1, jnp.sum(feed_sum), gate)
    high = gate.astype(BF).astype(F32)
    rest = gate - high
    mid = rest.astype(BF).astype(F32)
    last = (rest - mid).astype(BF).astype(F32)
    row = lax.broadcasted_iota(jnp.int32, (16, 128), 0)
    base = jnp.where(row == 1, high, jnp.where(row == 2, mid, jnp.where(row == 3, last, 0.0)))
    sums[0:1, 0 : 2 * D] = jnp.zeros((1, 2 * D), F32)

    def tail(o):
        both[(o % 2) ^ odd, o // 2, G_TILES - 1] = jnp.where(row == 0, sums[0:1, 128 * o : 128 * o + 128], base)

    for j in (3, 2, 1, 0):
        val = nn(active_t[512 * j : 512 * j + (528 if j == 3 else 512)], gs_all[...])
        if j == 3:
            sums[0:1, 3 * D : 4 * D] = val[D : D + 1]
            for o in range(16):
                tail(o)
            copies += send(pl.ds(0, 8), 5)
        for o in range(4):
            tail(16 + 4 * j + o)
            for jj in range(4):
                for i in range(8):
                    top, col = 128 * o + 16 * i, slice(128 * jj, 128 * jj + 128)
                    both[(o % 2) ^ odd, 8 + 2 * j + o // 2, 8 * jj + i] = val[top : top + 16, col]
        copies += send(pl.ds(8 + 2 * j, 2), 7 + 2 * j)
    pltpu.make_async_copy(layer, layer_out, sems.at[0]).wait()
    for copy in copies:
        copy.wait()


def back_body(first, place, q_all, k_all, v_all, g_all, lse, x_t, *refs):
    if first:
        before, *refs = refs
    dq_out, dk_out, dv_out, *refs = refs
    if first:
        keeps, sends, refs, sums = refs[:2], refs[2:4], refs[4:-1], refs[-1]
    else:
        keep, send, sums, *refs = refs
        keeps, sends = [(ref.at[:SHARE], ref.at[SHARE:]) for ref in (keep, send)]
    k_t, dq_t, dk_acc, dv_acc, s0, s1, g0, g1, p0, p1, d0, d1 = refs
    scores, grads, probs, diffs = (s0, s1), (g0, g1), (p0, p1), (d0, d1)
    steps = [(parity, r) for parity in range(2) for r in range(4)]
    odd = place[1] == 1
    sums[...] = before[...] if first else jnp.zeros_like(sums)

    def pair(turn, _):
        p = turn + first
        lanes = pl.ds(pl.multiple_of(p * 128, 128), 128)
        out = pl.ds(pl.multiple_of(turn * 128, 128), 128)
        q_in, k_in = q_all.at[pl.ds(2 * p, 2)], k_all.at[pl.ds(2 * p, 2)]
        for parity in range(2):
            k_t[parity] = k_in[parity].T

        def mine(block, i):
            return jnp.where(half_of(steps[i][0], (256, 128)), block, jnp.zeros_like(block))

        def score(i):
            parity, r = steps[i]
            qa = q_in[parity, r * 256 : r * 256 + 256]
            ga = mine(g_all[r * 256 : r * 256 + 256, lanes], i)

            def part(c):
                scores[i % 2][c : c + BIG] = nt(k_in[parity, c : c + BIG], qa)

            def grad(c):
                grads[i % 2][c : c + BIG] = nt(v_all[c : c + BIG, lanes], ga)

            return [task for c in range(0, ROWS, BIG) for task in (partial(part, c), partial(grad, c))]

        def soften(i):
            parity, r = steps[i]
            s, g, out, diff = scores[i % 2], grads[i % 2], probs[i % 2], diffs[i % 2]
            logs = lse[pl.ds(2 * p + parity, 1), r * 256 : r * 256 + 256]
            state = {}

            def power(c):
                e = jnp.exp(s[c : c + CHUNK] - logs)
                s[c : c + CHUNK] = e
                out[c : c + CHUNK] = e.astype(BF)
                part = jnp.sum((e * g[c : c + CHUNK]).reshape(-1, 8, 256), axis=0)
                state["inner"] = state["inner"] + part if c else part
                if c == ROWS - CHUNK:
                    state["inner"] = jnp.sum(state["inner"], axis=0, keepdims=True)

            def minus(c):
                diff[c : c + CHUNK] = (s[c : c + CHUNK] * (g[c : c + CHUNK] - state["inner"])).astype(BF)

            at = range(0, ROWS, CHUNK)
            return [(5.5, partial(power, c)) for c in at] + [(2.5, partial(minus, c)) for c in at]

        def collect(i):
            parity, r = steps[i]
            rows = slice(64 * parity, 64 * parity + 64)
            at = slice(r * 256, r * 256 + 256)
            qz, gz = mine(q_in[parity, at], i), mine(g_all[at, lanes], i)
            total = []

            def part(c):
                total.append(nn(k_t[parity, rows, c : c + 256], diffs[i % 2][c : c + 256]))
                if c == ROWS - 256:
                    dq_t[rows, r * 256 : r * 256 + 256] = ((total[0] + total[1]) + (total[2] + total[3])) * 0.125

            def add(acc, ref, z, c):
                val = nn(ref[c : c + BIG], z)
                acc[c : c + BIG] = acc[c : c + BIG] + val if i else val

            tasks = []
            for c in range(0, ROWS, 256):
                if c % BIG == 0:
                    tasks += [partial(add, dv_acc, probs[i % 2], gz, c), partial(add, dk_acc, diffs[i % 2], qz, c)]
                tasks += [partial(part, c)]
            return tasks

        for task in score(0):
            task()
        for i in range(9):
            later = (score(i + 1) if i < 7 else []) + (collect(i - 1) if i else [])
            mix(soften(i) if i < 8 else [], later)
        dq = dq_t[...].astype(BF).T
        dk = dk_acc[...].astype(BF)
        dv = dv_acc[...].astype(BF)
        dq_out[:, out] = dq
        dk_out[:, out] = dk
        dv_out[:, out] = dv
        val = nn(x_t[...], jnp.concatenate([dq, dk, dv, dv], axis=1))
        sums[pl.ds(p, 1), :] = val[D : D + 1, 0:128]
        sums[pl.ds(4 + p, 1), :] = val[D : D + 1, 256:384]
        for index in range(3):
            for o in range(0, 8, 2):
                for i in range(4):
                    col, top = slice(128 * index, 128 * index + 128), 64 * o + 16 * i
                    even, other = val[top : top + 16, col], val[top + 64 : top + 80, col]
                    part, at = part_of(index, o // 2)
                    at = pl.ds(pl.multiple_of(SHARE * turn + 64 * at + 16 * i, 16), 16)
                    keeps[part][at] = jnp.where(odd, other, even)
                    sends[part][at] = jnp.where(odd, even, other)
        return 0

    lax.fori_loop(0, dq_out.shape[1] // 128, pair, 0)
    if first:
        row = lax.broadcasted_iota(jnp.int32, (8, 128), 0)
        even, other = jnp.zeros((8, 128), F32), jnp.zeros((8, 128), F32)
        for o in range(0, 8, 2):
            even = jnp.where(row == o // 2, sums[o : o + 1, :], even)
            other = jnp.where(row == o // 2, sums[o + 1 : o + 2, :], other)
        keeps[1][3 * SHARE :] = jnp.where(odd, other, even)
        sends[1][3 * SHARE :] = jnp.where(odd, even, other)


def part_of(index, slot):
    return (index, slot) if index < 2 else (slot // 2, 4 + slot % 2)


def split_row(tile):
    row = lax.broadcasted_iota(jnp.int32, tile.shape, 0)
    rest = tile[0:1] - tile[0:1].astype(BF).astype(F32)
    return jnp.where(row == 4, rest, tile)


def join_row(tile):
    row = lax.broadcasted_iota(jnp.int32, tile.shape, 0)
    whole = tile[0:1] + tile[4:5]
    return jnp.where(row == 0, whole, jnp.where(row == 4, 0.0, tile))


def feed_xy_body(place, keep, got, wo_keep, wo_got, *outs):
    size = keep.shape[1]
    for t in range(4):
        here = place[3] ^ t
        out = outs[t]
        for z in range(4):
            total = keep[4 * z + here] + got[4 * z + here]
            out[size * z : size * z + size - 1] = total[: size - 1].astype(out.dtype)
            out[size * z + size - 1] = (split_row(total[size - 1]) if t else total[size - 1]).astype(out.dtype)
        out[4 * size :] = (wo_keep[here] + wo_got[here]).astype(out.dtype)


def feed_z_body(place, keep, g1, g2, g3, out0, out1, out2, out3, wo_out):
    size = out0.shape[0]
    for t, out in enumerate((out0, out1, out2, out3)):
        at = pl.ds((place[4] ^ t) * size, size - 1)
        total = keep[at] + g1[at].astype(F32) + g2[at].astype(F32) + g3[at].astype(F32)
        out[: size - 1] = total.astype(out.dtype)
        at = (place[4] ^ t) * size + size - 1
        total = keep[at]
        for g in (g1, g2, g3):
            total = total + join_row(g[at].astype(F32))
        out[size - 1] = (split_row(total) if t else total).astype(out.dtype)
    at = slice(4 * size, 4 * size + 16)
    wo_out[...] = keep[at] + g1[at].astype(F32) + g2[at].astype(F32) + g3[at].astype(F32)


def square_xy_body(place, first, first_got, a, b, a_got, b_got, *outs):
    def added(p, part, at):
        rows = pl.ds(pl.multiple_of(at * 64, 64), 64)
        if p == 0:
            rows = pl.ds(pl.multiple_of(SHARE * part + at * 64, 64), 64)
            return first[rows] + first_got[rows]
        rows = pl.ds(pl.multiple_of(SHARE * (p - 1) + at * 64, 64), 64)
        return ((a, b)[part])[rows] + ((a_got, b_got)[part])[rows]

    for t in range(4):
        here = place[3] ^ t
        out = outs[t]
        for z in range(3):
            for p in range(4):
                if z < 2:
                    total = added(p, z, here)
                else:
                    total = jnp.where(here < 2, added(p, 0, 4 + here % 2), added(p, 1, 4 + here % 2))
                out[16 * z + 4 * p : 16 * z + 4 * p + 4] = total.reshape(4, 16, 128).astype(out.dtype)
        row = lax.broadcasted_iota(jnp.int32, (16, 128), 0)
        total = b[pl.ds(3 * SHARE + here, 1)] + b_got[pl.ds(3 * SHARE + here, 1)]
        total = jnp.where(row == 0, total, 0.0)
        out[48] = (split_row(total) if t else total).astype(out.dtype)


def square_z_body(place, keep, g1, g2, g3, wo, out0, out1, out2, out3, whole):
    for z in range(3):
        at = slice(16 * z, 16 * z + 16)
        whole[z, :16] = keep[at] + g1[at].astype(F32) + g2[at].astype(F32) + g3[at].astype(F32)
        whole[z + 1, 16] = jnp.zeros((16, 128), F32)
    whole[3, :16] = wo[...]
    total = keep[48]
    for g in (g1, g2, g3):
        total = total + join_row(g[48].astype(F32))
    whole[0, 16] = total
    for t, out in enumerate((out0, out1, out2, out3)):
        at = place[4] ^ t
        out[:16] = whole[at, :16].astype(out.dtype)
        out[16] = (split_row(whole[at, 16]) if t else whole[at, 16]).astype(out.dtype)


def input_body(gm, *refs):
    w, out = refs[6:]
    for r in range(4):
        at = slice(256 * r, 256 * r + 256)
        total = gm[at, :]
        for index in range(3):
            total = total + nt(jnp.concatenate([ref[at, :] for ref in refs[index:6:3]], axis=1), square(w, index))
        out[at, :] = total


def to_columns(flat, rows):
    return flat.reshape(rows // 16, 16, -1, 128).transpose(2, 0, 1, 3).reshape(-1, 16, 128)


def from_columns(tiles, rows):
    return tiles.reshape(-1, rows // 16, 16, 128).transpose(1, 2, 0, 3).reshape(-1)


def swap(x, n, bit):
    return lax.ppermute(x, AXES, [(i, i ^ bit) for i in range(n)])


def small(body, outs, args, scratch=()):
    ins = [SMEM if arg.dtype == jnp.int32 else VMEM for arg in args]
    size = sum(arg.size for arg in args)
    return call(body, outs, ins, scratch, 2 * size, 6 * size, 16)(*args)


def blocks_of(*shape):
    return [(shape + (16, 128), F32)] + [(shape + (16, 128), BF)] * 3


def hop(parts, n, step):
    return [parts[0]] + [swap(part, n, step * t) for t, part in enumerate(parts) if t]


def tie(values, after):
    return lax.optimization_barrier((values, after))[0]


def along_z(own, n):
    return jnp.stack([own] + [swap(own, n, 8 * z) for z in (1, 2, 3)])


def along_xy(stack, n):
    return [stack] + [swap(stack, n, 2 * xy) for xy in (1, 2, 3)]


def across(chips, n):
    return chips + [swap(part, n, 1) for part in chips]


def pack_square_body(flat, biases, out, wide):
    wide[...] = flat[...].astype(F32)
    for j in range(4):
        for i in range(4):
            out[4 * j + i] = wide[pl.ds(64 * i + j, 16, stride=4), :].astype(BF)
    row = lax.broadcasted_iota(jnp.int32, (16, 128), 0)
    out[16] = jnp.where(row == 0, biases[...].astype(F32), 0.0).astype(BF)


def pack_feed_body(place, flat, out, wide):
    wide[...] = flat[...].astype(F32)

    @pl.when(place[0] < PARTS // 2)
    def _():
        for j in range(16):
            for i in range(2):
                out[2 * j + i] = wide[pl.ds(256 * i + j, 16, stride=16), :].astype(BF)

    @pl.when(place[0] >= PARTS // 2)
    def _():
        for j in range(4):
            for i in range(8):
                out[8 * j + i] = wide[pl.ds(64 * i + j, 16, stride=4), :].astype(BF)


def finish_body(place, keep_f, f1, f2, f3, keep_a, a1, a2, a3, att, ff, bias, gate):
    def added(keep, gots, at):
        total = keep[at]
        for g in gots:
            total = total + g[at].astype(F32)
        return total

    def added_tail(keep, gots, at):
        total = keep[at]
        for g in gots:
            total = total + join_row(g[at].astype(F32))
        return total

    for j in range(4):
        for i in range(4):
            att[pl.ds(64 * i + j, 16, stride=4), :] = added(keep_a, (a1, a2, a3), 4 * j + i)
    gots = (f1, f2, f3)

    @pl.when(place[0] < PARTS // 2)
    def _():
        for j in range(16):
            for i in range(2):
                ff[pl.ds(256 * i + j, 16, stride=16), :] = added(keep_f, gots, 2 * j + i)

    @pl.when(place[0] >= PARTS // 2)
    def _():
        for j in range(4):
            for i in range(8):
                ff[pl.ds(64 * i + j, 16, stride=4), :] = added(keep_f, gots, 8 * j + i)

    tail = added_tail(keep_f, gots, F_TILES)
    own = added_tail(keep_a, (a1, a2, a3), 16)
    bias[...] = jnp.where(place[0] < 8, own[0:1], tail[0:1])
    gates = tail[1:2] + tail[2:3] + tail[3:4]
    lane = lax.broadcasted_iota(jnp.int32, (1, 128), 1)
    for g in range(2):
        gate[g] = jnp.sum(jnp.where((lane < 2 * PARTS) & (lane % 2 == g), gates, 0.0))


def own_pieces(attention, feedforward, biases, upper, parts):
    tail = jnp.pad(biases.reshape(1, 1, 128), ((0, 0), (0, 15), (0, 0)))
    own_a = jnp.concatenate([to_columns(attention, 4 * D // parts), tail], axis=0)
    up = to_columns(feedforward, 2 * D // parts)
    down = to_columns(feedforward, 2 * FF // parts)
    return own_a, jnp.where(upper, up, down)


def pieces_any(attention, feedforward, biases):
    full = [lax.all_gather(x, AXES, axis=0, tiled=True).reshape(PARTS, -1) for x in (attention, feedforward, biases)]
    upper = jnp.arange(PARTS) < PARTS // 2
    a, f = jax.vmap(lambda *x: own_pieces(*x, PARTS))(*full, upper)
    a, f = a.reshape((4, 4, 2) + a.shape[1:]), f.reshape((4, 4, 2) + f.shape[1:])

    return [[x[:, xy, c] for c in range(2) for xy in range(4)] for x in (a, f)]


def local(direct, tokens, cotangent, attention, feedforward, biases, gates, counts, lengths):
    me = lax.axis_index(AXES)
    n = PARTS
    *masks, x_t = call(
        prepare_body,
        [((2, ROWS, 128), BF), ((2, ROWS, 128), BF), ((D + 16, ROWS), BF)],
        [SMEM, SMEM, VMEM], [], 1 << 20, 3 << 20, 16,
    )(counts, lengths, tokens)
    if direct:
        place = jnp.stack([me, me % 2, me, (me // 2) % 4, me // 8]).astype(jnp.int32)
        (own_a,) = small(
            pack_square_body, [((A_TILES, 16, 128), BF)], (attention.reshape(-1, 128), biases.reshape(1, 128)), [((256, 128), F32)]
        )
        (own_f,) = small(
            pack_feed_body, [((F_TILES, 16, 128), BF)], (place, feedforward.reshape(-1, 128)), [((512, 128), F32)]
        )
        stack_a, masks = lax.optimization_barrier((along_z(own_a, n), masks))
        stack_f = along_z(own_f, n)
        chips_a = along_xy(stack_a, n)
        ga_all = across(chips_a, n)
        chips_f = along_xy(stack_f, n)
    else:
        ga_all, gf_all = pieces_any(attention, feedforward, biases)
        place = jnp.zeros((5,), jnp.int32)
    row = (ROWS, D)
    q, k, v, w, bias = call(
        project_body,
        [((H, ROWS, 128), BF)] * 2 + [(row, BF), ((PARTS, A_TILES, 16, 128), BF), ((1, 8 * D), F32)],
        [SMEM] + [VMEM] * 11, [], 2 << 30, 10 << 20, 20,
    )(place, tokens, *masks, *ga_all)
    ctx, ctx_t, lse = call(
        attend_body,
        [(row, BF), ((D + 16, ROWS), BF), ((8, ROWS), F32)],
        [VMEM] * 3,
        [((128, ROWS), BF), ((128, ROWS), F32)] + [((ROWS, 256), F32)] * 2 + [((ROWS, 256), BF)] * 2,
        12 << 30, 4 << 20, 20,
    )(q, k, v)
    if direct:
        chips_f, ctx = lax.optimization_barrier((chips_f, ctx))
        gf_all = across(chips_f, n)
    layer, gm, gctx, ff_keep, ff_send, wo_keep, wo_send = call(
        feed_body,
        [(row, BF, ANY), (row, F32), (row, BF)] + [((n // 2, G_TILES, 16, 128), F32, ANY)] * 2
        + [((4, 16, 16, 128), F32)] * 2,
        [SMEM, SMEM] + [VMEM] * 14,
        [((PARTS, F_TILES, 16, 128), BF), ((D + 16, ROWS), BF), (row, BF), (row, BF),
         ((FF + 16, ROWS), BF), ((ROWS, FF), BF)]
        + [((256, D), F32)] * 4 + [((256, FF), BF)] + [((256, D), F32)] * 2 + [((1, 8 * D), F32)]
        + [(row, BF), ((2, n // 2, G_TILES, 16, 128), F32), DMA((16,))],
        16 << 30, 30 << 20, 36,
    )(place, gates, tokens, cotangent, ctx, ctx_t, w, bias, *gf_all)

    def back(first, pairs, q, before):
        shares = [((3 * SHARE, 128), F32), ((3 * SHARE + 8, 128), F32)] * 2 if first else [((2 * SHARE, 128), F32)] * 2
        return call(
            partial(back_body, first),
            [((ROWS, 128 * pairs), BF)] * 3 + shares + ([] if first else [((8, 128), F32)]),
            [SMEM] + [VMEM] * (7 if first else 6),
            [((2, 128, ROWS), BF), ((128, ROWS), F32), ((ROWS, 128), F32), ((ROWS, 128), F32)]
            + [((ROWS, 256), F32)] * 4 + [((ROWS, 256), BF)] * 4 + ([((8, 128), F32)] if first else []),
            1000, 1000, 28,
        )(place, q, k, v, gctx, lse, x_t, *([before] if first else []))

    barrier = lax.optimization_barrier
    if direct:
        got, wo_got = swap(ff_send, n, 1), swap(wo_send, n, 1)
    *grads, keep, send, before = back(0, 1, q, None)
    if direct:
        got, wo_got, grads, send = barrier((got, wo_got, grads, send))
        parts = small(feed_xy_body, blocks_of(4 * G_TILES + 16), (place, ff_keep, got, wo_keep, wo_got))
        q, parts = barrier((q, parts))
        ff_got = hop(parts, n, 2)
        got = swap(send, n, 1)
    *parts, keep_a, keep_b, send_a, send_b = back(1, 3, q, before)
    grads += parts
    (input_grad,) = call(
        input_body, [(row, F32)], [VMEM] * 8, [], 1000, 1000, 24
    )(gm, *grads, w)
    if direct:
        gots = [got, swap(send_a, n, 1), swap(send_b, n, 1)]
        gots, input_grad, ff_got = barrier((gots, input_grad, ff_got))
        parts = small(square_xy_body, blocks_of(49), (place, keep, gots[0], keep_a, keep_b, *gots[1:]))
        ff_got, parts = barrier((ff_got, parts))
        got = hop(parts, n, 2)
        *ff_parts, wo = small(feed_z_body, blocks_of(G_TILES) + [((16, 16, 128), F32)], (place, *ff_got))
        ff_got = hop(ff_parts, n, 8)
        got, ff_parts = barrier((got, ff_parts))
    if direct:
        parts = small(square_z_body, blocks_of(17), (place, *got, wo), [((4, 17, 16, 128), F32)])
        got = hop(parts, n, 8)
        att_grad, ff_grad, bias_grad, gate_grad = call(
            finish_body,
            [((256, 128), F32), ((512, 128), F32), ((1, 128), F32), ((2,), F32, SMEM)],
            [SMEM] + [VMEM] * 8, [], 1 << 20, 1 << 20, 16,
        )(place, *ff_got, *got)
        att_grad, ff_grad, bias_grad = att_grad.reshape(-1), ff_grad.reshape(-1), bias_grad.reshape(-1)
        return layer, input_grad, att_grad, ff_grad, bias_grad, gate_grad

    def owners(keep, send):
        return jnp.stack([keep, send], axis=1).reshape((-1,) + keep.shape[1:])

    def reduce(flat):
        return lax.psum_scatter(flat.reshape(-1), AXES, scatter_dimension=0, tiled=True)

    both = owners(ff_keep, ff_send)
    up = jax.vmap(lambda t: from_columns(t, 2 * D // n))(both[: n // 2, :F_TILES]).reshape(-1)
    down = jax.vmap(lambda t: from_columns(t, 2 * FF // n))(both[n // 2 :, :F_TILES]).reshape(-1)
    ff_grad = reduce(jnp.concatenate([up, down]))
    tail = both[0, F_TILES]
    gate_grad = lax.psum((tail[1] + tail[2] + tail[3])[:2], AXES)
    bias_grad = owners(keep_b[3 * SHARE : 3 * SHARE + 4], send_b[3 * SHARE : 3 * SHARE + 4])
    bias_grad = jnp.concatenate([bias_grad, both[8:, F_TILES, 0]])
    both = []
    for own, x_a, x_b in ((keep, keep_a, keep_b), (send, send_a, send_b)):
        x_a, x_b = [jnp.concatenate(x).reshape(4, 6, 64, 128) for x in ((own[:SHARE], x_a), (own[SHARE:], x_b[: 3 * SHARE]))]
        both.append(jnp.concatenate([x_a[:, :4], x_b[:, :4], x_a[:, 4:], x_b[:, 4:]], axis=1))
    both = jnp.stack(both, axis=2).reshape(4, 24, 4, 16, 128).transpose(1, 0, 2, 3, 4)
    both = jnp.concatenate([both.reshape(24, 16, 16, 128), owners(wo_keep, wo_send)])
    att_grad = jax.vmap(lambda t: from_columns(t, 4 * D // n))(both)
    return layer, input_grad, reduce(att_grad), ff_grad, reduce(bias_grad), gate_grad


def solution(mesh):
    direct = dict(mesh.shape) == {"dp": 8, "fsdp": 4}
    both = P(AXES)
    rows = P(AXES, None)
    return jax.shard_map(
        partial(local, direct),
        mesh=mesh,
        in_specs=(rows, rows, both, both, both, P(), rows, rows),
        out_specs=(rows, rows, both, both, both, P()),
        check_vma=False,
    )
```

profile of v0, /device:TPU:0, one launch (start us, length us, event | category | flops | bytes accessed | tf_op | source)
XLA Modules:
  0.0 152.5 jit_solution(11387432252897053416)
XLA Ops:
  2.2 5.1 %collective-permute-start.8 = (bf16[17,16,128]{2,1,0:T(8,128)(2,1)S(1)}, bf16[17,16,128]{2,1,0:T(8,128)(2,1)S(1)}, u32[]{:S(2)}, u32[]{:S(2)}) collective-permute-start(bf16[17,16,128]{2,1,0:T(8,128)(2,1)S(1)} %shard_map.128), channel_id=1, source_target_pairs={{0,24},{1,25},{2,26},{3,27},{4,28},{5,29},{6,30},{7,31},{8,16},{9,... | collective-permute-start | bytes 208904 | tf_op jit(solution)/shard_map/ppermute | solution.py:601
  7.9 1.2 copy-done.1
  10.4 1.5 shard_map.129
  12.0 1.2 collective-permute-done.7
  13.2 2.5 %collective-permute-start.11 = (bf16[4,17,16,128]{3,2,1,0:T(8,128)(2,1)S(1)}, bf16[4,17,16,128]{3,2,1,0:T(8,128)(2,1)}, u32[]{:S(2)}, u32[]{:S(2)}) collective-permute-start(bf16[4,17,16,128]{3,2,1,0:T(8,128)(2,1)S(1)} %pad_maximum_fusion.1.refs_0_), channel_id=1, source_target_pairs={{0,6},{1,7},{2,4},{3,5},{4,2},{5,3},{6,0},{7,1},{8,14},{9,15},{10,... | collective-permute-start | bytes 835592 | tf_op jit(solution)/shard_map/ppermute | solution.py:601
  18.4 2.7 %collective-permute-start.2 = (bf16[32,16,128]{2,1,0:T(8,128)(2,1)S(1)}, bf16[32,16,128]{2,1,0:T(8,128)(2,1)S(1)}, u32[]{:S(2)}, u32[]{:S(2)}) collective-permute-start(bf16[32,16,128]{2,1,0:T(8,128)(2,1)S(1)} %shard_map.127), channel_id=1, source_target_pairs={{0,24},{1,25},{2,26},{3,27},{4,28},{5,29},{6,30},{7,31},{8,16},{9,... | collective-permute-start | bytes 393224 | tf_op jit(solution)/shard_map/ppermute | solution.py:601
  21.1 4.9 %collective-permute-done.2 = bf16[32,16,128]{2,1,0:T(8,128)(2,1)S(1)} collective-permute-done((bf16[32,16,128]{2,1,0:T(8,128)(2,1)S(1)}, bf16[32,16,128]{2,1,0:T(8,128)(2,1)S(1)}, u32[]{:S(2)}, u32[]{:S(2)}) %collective-permute-start.2) | collective-permute-done | bytes 131104 | tf_op jit(solution)/shard_map/ppermute | solution.py:601
  26.5 2.2 %collective-permute-done.10.refs_2_ = bf16[4,17,16,128]{3,2,1,0:T(8,128)(2,1)} collective-permute-done((bf16[4,17,16,128]{3,2,1,0:T(8,128)(2,1)S(1)}, bf16[4,17,16,128]{3,2,1,0:T(8,128)(2,1)}, u32[]{:S(2)}, u32[]{:S(2)}) %collective-permute-start.10) | collective-permute-done | bytes 278560 | tf_op jit(solution)/shard_map/ppermute | solution.py:601
  29.2 2.3 %collective-permute-done.1 = bf16[32,16,128]{2,1,0:T(8,128)(2,1)S(1)} collective-permute-done((bf16[32,16,128]{2,1,0:T(8,128)(2,1)S(1)}, bf16[32,16,128]{2,1,0:T(8,128)(2,1)S(1)}, u32[]{:S(2)}, u32[]{:S(2)}) %collective-permute-start.1) | collective-permute-done | bytes 131104 | tf_op jit(solution)/shard_map/ppermute | solution.py:601
  31.7 4.8 %collective-permute-done = bf16[32,16,128]{2,1,0:T(8,128)(2,1)S(1)} collective-permute-done((bf16[32,16,128]{2,1,0:T(8,128)(2,1)S(1)}, bf16[32,16,128]{2,1,0:T(8,128)(2,1)S(1)}, u32[]{:S(2)}, u32[]{:S(2)}) %collective-permute-start) | collective-permute-done | bytes 131104 | tf_op jit(solution)/shard_map/ppermute | solution.py:601
  36.6 2.6 %collective-permute-start.5 = (bf16[4,32,16,128]{3,2,1,0:T(8,128)(2,1)S(1)}, bf16[4,32,16,128]{3,2,1,0:T(8,128)(2,1)S(1)}, u32[]{:S(2)}, u32[]{:S(2)}) collective-permute-start(bf16[4,32,16,128]{3,2,1,0:T(8,128)(2,1)S(1)} %pad_maximum_fusion.refs_0_), channel_id=1, source_target_pairs={{0,6},{1,7},{2,4},{3,5},{4,2},{5,3},{6,0},{7,1},{8,14},{9,15},{10,... | collective-permute-start | bytes 1572872 | tf_op jit(solution)/shard_map/ppermute | solution.py:601
  40.2 3.2 %shard_map.130 = (bf16[8,1024,128]{2,1,0:T(8,128)(2,1)S(1)}, bf16[8,1024,128]{2,1,0:T(8,128)(2,1)S(1)}, bf16[1024,512]{1,0:T(8,128)(2,1)S(1)}, bf16[32,17,16,128]{3,2,1,0:T(8,128)(2,1)S(1)}, f32[1,4096]{1,0:T(1,128)S(1)}) custom-call(s32[5]{0:T(128)S(1)} %stack.50.place, bf16[1024,512]{1,0:T(8,128)(2,1)S(1)} %copy-done.2, ...), custom_call_target="tpu_custom_call" | custom-call | flops 2147483648 | bytes 10485760 | tf_op jit(solution)/shard_map/pallas_call | solution.py:740
  43.3 13.1 %shard_map.131 = (bf16[1024,512]{1,0:T(8,128)(2,1)S(1)}, bf16[528,1024]{1,0:T(8,128)(2,1)S(1)}, f32[8,1024]{1,0:T(8,128)S(1)}) custom-call(bf16[8,1024,128]{2,1,0:T(8,128)(2,1)S(1)} %get-tuple-element.133.q_all, bf16[8,1024,128]{2,1,0:T(8,128)(2,1)S(1)} %get-tuple-element.103.k_all, bf16[1024,512]{1,0:T(8,128)(2,1)S(1)} %get-tuple-element.104.v_all), custom_call_target="tpu_custom_call" | custom-call | flops 12884901888 | bytes 4194304 | tf_op jit(solution)/shard_map/pallas_call | solution.py:745
  56.5 3.8 %collective-permute-done.4.refs_2_ = bf16[4,32,16,128]{3,2,1,0:T(8,128)(2,1)S(1)} collective-permute-done((bf16[4,32,16,128]{3,2,1,0:T(8,128)(2,1)S(1)}, bf16[4,32,16,128]{3,2,1,0:T(8,128)(2,1)S(1)}, u32[]{:S(2)}, u32[]{:S(2)}) %collective-permute-start.4) | collective-permute-done | bytes 524320 | tf_op jit(solution)/shard_map/ppermute | solution.py:601
  64.5 20.5 %shard_map.132 = (bf16[1024,512]{1,0:T(8,128)(2,1)}, f32[1024,512]{1,0:T(8,128)S(1)}, bf16[1024,512]{1,0:T(8,128)(2,1)S(1)}, f32[16,33,16,128]{3,2,1,0:T(8,128)}...) custom-call(s32[5]{0:T(128)S(1)} %stack.50.place, f32[2]{0:T(128)S(1)} %copy-done.9, ...), custom_call_target="tpu_custom_call" | custom-call | flops 17179869184 | bytes 31457280 | tf_op jit(solution)/shard_map/pallas_call | solution.py:755
  85.5 7.1 %shard_map.133 = (bf16[1024,128]{1,0:T(8,128)(2,1)S(1)}, bf16[1024,128]{1,0:T(8,128)(2,1)S(1)}, bf16[1024,128]{1,0:T(8,128)(2,1)S(1)}, f32[768,128]{1,0:T(8,128)...) custom-call(s32[5]{0:T(128)S(1)} %stack.50.place, bf16[8,1024,128]{2,1,0:T(8,128)(2,1)S(1)} %get-tuple-element.133.q_all, ...), custom_call_target="tpu_custom_call" | custom-call | flops 1000 | bytes 1000 | tf_op jit(solution)/shard_map/pallas_call | solution.py:769
  93.5 1.0 shard_map.134
  94.5 1.5 collective-permute-start.25
  96.0 1.5 collective-permute-start.26
  98.0 20.3 %shard_map.135 = (bf16[1024,384]{1,0:T(8,128)(2,1)S(1)}, bf16[1024,384]{1,0:T(8,128)(2,1)S(1)}, bf16[1024,384]{1,0:T(8,128)(2,1)S(1)}, f32[1152,128]{1,0:T(8,128...) custom-call(s32[5]{0:T(128)S(1)} %stack.50.place, ...), custom_call_target="tpu_custom_call" | custom-call | flops 1000 | bytes 1000 | tf_op jit(solution)/shard_map/pallas_call | solution.py:769
  119.0 3.1 %shard_map.136 = f32[1024,512]{1,0:T(8,128)} custom-call(f32[1024,512]{1,0:T(8,128)S(1)} %get-tuple-element.137.gm, bf16[1024,128]{1,0:T(8,128)(2,1)S(1)} %get-tuple-element.138.refs_0_, bf16[1024,128]{1,0:T(8,128)(2,1)S(1)} %get-tuple-element.139.refs_1_, bf16[1024,128]{1,0:T(8,128)(2,1)S(1)} %get-tuple-element.140.refs_2_, ...), custom_call_target="tpu_custom_call" | custom-call | flops 1000 | bytes 1000 | tf_op jit(solution)/shard_map/pallas_call | solution.py:790
  122.1 2.5 %collective-permute-done.27.g3 = bf16[148,16,128]{2,1,0:T(8,128)(2,1)S(1)} collective-permute-done((bf16[148,16,128]{2,1,0:T(8,128)(2,1)S(1)}, bf16[148,16,128]{2,1,0:T(8,128)(2,1)S(1)}, u32[]{:S(2)}, u32[]{:S(2)}) %collective-permute-start.27) | collective-permute-done | bytes 606240 | tf_op jit(solution)/shard_map/ppermute | solution.py:601
  125.5 1.5 collective-permute-start.31
  126.9 1.5 collective-permute-start.32
  129.9 2.5 %collective-permute-start.28 = (bf16[33,16,128]{2,1,0:T(8,128)(2,1)S(1)}, bf16[33,16,128]{2,1,0:T(8,128)(2,1)S(1)}, u32[]{:S(2)}, u32[]{:S(2)}) collective-permute-start(bf16[33,16,128]{2,1,0:T(8,128)(2,1)S(1)} %get-tuple-element.168), channel_id=1, source_target_pairs={{0,8},{1,9},{2,10},{3,11},{4,12},{5,13},{6,14},{7,15},{8,0},{9,1},... | collective-permute-start | bytes 405512 | tf_op jit(solution)/shard_map/ppermute | solution.py:601
  132.7 2.2 %collective-permute-start.30 = (bf16[33,16,128]{2,1,0:T(8,128)(2,1)S(1)}, bf16[33,16,128]{2,1,0:T(8,128)(2,1)S(1)}, u32[]{:S(2)}, u32[]{:S(2)}) collective-permute-start(bf16[33,16,128]{2,1,0:T(8,128)(2,1)S(1)} %get-tuple-element.170), channel_id=1, source_target_pairs={{0,24},{1,25},{2,26},{3,27},{4,28},{5,29},{6,30},{7,31},{8,16},{9,... | collective-permute-start | bytes 405512 | tf_op jit(solution)/shard_map/ppermute | solution.py:601
  134.9 2.3 %collective-permute-done.33.g3 = bf16[49,16,128]{2,1,0:T(8,128)(2,1)S(1)} collective-permute-done((bf16[49,16,128]{2,1,0:T(8,128)(2,1)S(1)}, bf16[49,16,128]{2,1,0:T(8,128)(2,1)S(1)}, u32[]{:S(2)}, u32[]{:S(2)}) %collective-permute-start.33) | collective-permute-done | bytes 200736 | tf_op jit(solution)/shard_map/ppermute | solution.py:601
  137.8 2.5 %collective-permute-start.34 = (bf16[17,16,128]{2,1,0:T(8,128)(2,1)S(1)}, bf16[17,16,128]{2,1,0:T(8,128)(2,1)S(1)}, u32[]{:S(2)}, u32[]{:S(2)}) collective-permute-start(bf16[17,16,128]{2,1,0:T(8,128)(2,1)S(1)} %get-tuple-element.181), channel_id=1, source_target_pairs={{0,8},{1,9},{2,10},{3,11},{4,12},{5,13},{6,14},{7,15},{8,0},{9,1},... | collective-permute-start | bytes 208904 | tf_op jit(solution)/shard_map/ppermute | solution.py:601
  140.6 2.2 %collective-permute-start.36 = (bf16[17,16,128]{2,1,0:T(8,128)(2,1)S(1)}, bf16[17,16,128]{2,1,0:T(8,128)(2,1)S(1)}, u32[]{:S(2)}, u32[]{:S(2)}) collective-permute-start(bf16[17,16,128]{2,1,0:T(8,128)(2,1)S(1)} %get-tuple-element.183), channel_id=1, source_target_pairs={{0,24},{1,25},{2,26},{3,27},{4,28},{5,29},{6,30},{7,31},{8,16},{9,... | collective-permute-start | bytes 208904 | tf_op jit(solution)/shard_map/ppermute | solution.py:601
  142.8 3.3 %collective-permute-done.29.f2 = bf16[33,16,128]{2,1,0:T(8,128)(2,1)S(1)} collective-permute-done((bf16[33,16,128]{2,1,0:T(8,128)(2,1)S(1)}, bf16[33,16,128]{2,1,0:T(8,128)(2,1)S(1)}, u32[]{:S(2)}, u32[]{:S(2)}) %collective-permute-start.29) | collective-permute-done | bytes 135200 | tf_op jit(solution)/shard_map/ppermute | solution.py:601
  146.1 4.7 %collective-permute-done.35.a2 = bf16[17,16,128]{2,1,0:T(8,128)(2,1)S(1)} collective-permute-done((bf16[17,16,128]{2,1,0:T(8,128)(2,1)S(1)}, bf16[17,16,128]{2,1,0:T(8,128)(2,1)S(1)}, u32[]{:S(2)}, u32[]{:S(2)}) %collective-permute-start.35) | collective-permute-done | bytes 69664 | tf_op jit(solution)/shard_map/ppermute | solution.py:601
  150.8 1.5 shard_map.140
  (79 shorter events, 18.7 us)
Async XLA Ops:
  2.2 9.8 %collective-permute-start.8 = (bf16[17,16,128]{2,1,0:T(8,128)(2,1)S(1)}, bf16[17,16,128]{2,1,0:T(8,128)(2,1)S(1)}, u32[]{:S(2)}, u32[]{:S(2)}) collective-permute-start(bf16[17,16,128]{2,1,0:T(8,128)(2,1)S(1)} %shard_map.128), channel_id=1, source_target_pairs={{0,24},{1,25},{2,26},{3,27},{4,28},{5,29},{6,30},{7,31},{8,16},{9,... | collective-permute-start | bytes 208904 | tf_op jit(solution)/shard_map/ppermute | solution.py:601
  7.3 5.9 %collective-permute-start.7 = (bf16[17,16,128]{2,1,0:T(8,128)(2,1)S(1)}, bf16[17,16,128]{2,1,0:T(8,128)(2,1)S(1)}, u32[]{:S(2)}, u32[]{:S(2)}) collective-permute-start(bf16[17,16,128]{2,1,0:T(8,128)(2,1)S(1)} %shard_map.128), channel_id=1, source_target_pairs={{0,16},{1,17},{2,18},{3,19},{4,20},{5,21},{6,22},{7,23},{8,24},{9,... | collective-permute-start | bytes 208904 | tf_op jit(solution)/shard_map/ppermute | solution.py:601
  7.3 5.9 %collective-permute-start.6 = (bf16[17,16,128]{2,1,0:T(8,128)(2,1)S(1)}, bf16[17,16,128]{2,1,0:T(8,128)(2,1)S(1)}, u32[]{:S(2)}, u32[]{:S(2)}) collective-permute-start(bf16[17,16,128]{2,1,0:T(8,128)(2,1)S(1)} %shard_map.128), channel_id=1, source_target_pairs={{0,8},{1,9},{2,10},{3,11},{4,12},{5,13},{6,14},{7,15},{8,0},{9,1},... | collective-permute-start | bytes 208904 | tf_op jit(solution)/shard_map/ppermute | solution.py:601
  13.2 12.8 %collective-permute-start.11 = (bf16[4,17,16,128]{3,2,1,0:T(8,128)(2,1)S(1)}, bf16[4,17,16,128]{3,2,1,0:T(8,128)(2,1)}, u32[]{:S(2)}, u32[]{:S(2)}) collective-permute-start(bf16[4,17,16,128]{3,2,1,0:T(8,128)(2,1)S(1)} %pad_maximum_fusion.1.refs_0_), channel_id=1, source_target_pairs={{0,6},{1,7},{2,4},{3,5},{4,2},{5,3},{6,0},{7,1},{8,14},{9,15},{10,... | collective-permute-start | bytes 835592 | tf_op jit(solution)/shard_map/ppermute | solution.py:601
  15.7 13.0 %collective-permute-start.10 = (bf16[4,17,16,128]{3,2,1,0:T(8,128)(2,1)S(1)}, bf16[4,17,16,128]{3,2,1,0:T(8,128)(2,1)}, u32[]{:S(2)}, u32[]{:S(2)}) collective-permute-start(bf16[4,17,16,128]{3,2,1,0:T(8,128)(2,1)S(1)} %pad_maximum_fusion.1.refs_0_), channel_id=1, source_target_pairs={{0,4},{1,5},{2,6},{3,7},{4,0},{5,1},{6,2},{7,3},{8,12},{9,13},{10,... | collective-permute-start | bytes 835592 | tf_op jit(solution)/shard_map/ppermute | solution.py:601
  16.3 12.5 %collective-permute-start.9 = (bf16[4,17,16,128]{3,2,1,0:T(8,128)(2,1)S(1)}, bf16[4,17,16,128]{3,2,1,0:T(8,128)(2,1)}, u32[]{:S(2)}, u32[]{:S(2)}) collective-permute-start(bf16[4,17,16,128]{3,2,1,0:T(8,128)(2,1)S(1)} %pad_maximum_fusion.1.refs_0_), channel_id=1, source_target_pairs={{0,2},{1,3},{2,0},{3,1},{4,6},{5,7},{6,4},{7,5},{8,10},{9,11},{10,... | collective-permute-start | bytes 835592 | tf_op jit(solution)/shard_map/ppermute | solution.py:601
  18.4 7.6 %collective-permute-start.2 = (bf16[32,16,128]{2,1,0:T(8,128)(2,1)S(1)}, bf16[32,16,128]{2,1,0:T(8,128)(2,1)S(1)}, u32[]{:S(2)}, u32[]{:S(2)}) collective-permute-start(bf16[32,16,128]{2,1,0:T(8,128)(2,1)S(1)} %shard_map.127), channel_id=1, source_target_pairs={{0,24},{1,25},{2,26},{3,27},{4,28},{5,29},{6,30},{7,31},{8,16},{9,... | collective-permute-start | bytes 393224 | tf_op jit(solution)/shard_map/ppermute | solution.py:601
  21.1 10.4 %collective-permute-start.1 = (bf16[32,16,128]{2,1,0:T(8,128)(2,1)S(1)}, bf16[32,16,128]{2,1,0:T(8,128)(2,1)S(1)}, u32[]{:S(2)}, u32[]{:S(2)}) collective-permute-start(bf16[32,16,128]{2,1,0:T(8,128)(2,1)S(1)} %shard_map.127), channel_id=1, source_target_pairs={{0,16},{1,17},{2,18},{3,19},{4,20},{5,21},{6,22},{7,23},{8,24},{9,... | collective-permute-start | bytes 393224 | tf_op jit(solution)/shard_map/ppermute | solution.py:601
  26.0 13.2 %collective-permute-start.12 = (bf16[4,17,16,128]{3,2,1,0:T(8,128)(2,1)S(1)}, bf16[4,17,16,128]{3,2,1,0:T(8,128)(2,1)S(1)}, u32[]{:S(2)}, u32[]{:S(2)}) collective-permute-start(bf16[4,17,16,128]{3,2,1,0:T(8,128)(2,1)S(1)} %pad_maximum_fusion.1.refs_0_), channel_id=1, source_target_pairs={{0,1},{1,0},{2,3},{3,2},{4,5},{5,4},{6,7},{7,6},{8,9},{9,8},{10,11... | collective-permute-start | bytes 835592 | tf_op jit(solution)/shard_map/ppermute | solution.py:601
  26.0 13.7 %collective-permute-start.15 = (bf16[4,17,16,128]{3,2,1,0:T(8,128)(2,1)}, bf16[4,17,16,128]{3,2,1,0:T(8,128)(2,1)S(1)}, u32[]{:S(2)}, u32[]{:S(2)}) collective-permute-start(bf16[4,17,16,128]{3,2,1,0:T(8,128)(2,1)} %collective-permute-done.11.refs_3_), channel_id=1, source_target_pairs={{0,1},{1,0},{2,3},{3,2},{4,5},{5,4},{6,7},{7,6},{8,9},{9,8},{10,11... | collective-permute-start | bytes 835592 | tf_op jit(solution)/shard_map/ppermute | solution.py:601
  28.7 11.4 %collective-permute-start.14 = (bf16[4,17,16,128]{3,2,1,0:T(8,128)(2,1)}, bf16[4,17,16,128]{3,2,1,0:T(8,128)(2,1)S(1)}, u32[]{:S(2)}, u32[]{:S(2)}) collective-permute-start(bf16[4,17,16,128]{3,2,1,0:T(8,128)(2,1)} %collective-permute-done.10.refs_2_), channel_id=1, source_target_pairs={{0,1},{1,0},{2,3},{3,2},{4,5},{5,4},{6,7},{7,6},{8,9},{9,8},{10,11... | collective-permute-start | bytes 835592 | tf_op jit(solution)/shard_map/ppermute | solution.py:601
  28.7 11.4 %collective-permute-start.13 = (bf16[4,17,16,128]{3,2,1,0:T(8,128)(2,1)}, bf16[4,17,16,128]{3,2,1,0:T(8,128)(2,1)S(1)}, u32[]{:S(2)}, u32[]{:S(2)}) collective-permute-start(bf16[4,17,16,128]{3,2,1,0:T(8,128)(2,1)} %collective-permute-done.9.refs_1_), channel_id=1, source_target_pairs={{0,1},{1,0},{2,3},{3,2},{4,5},{5,4},{6,7},{7,6},{8,9},{9,8},{10,11... | collective-permute-start | bytes 835592 | tf_op jit(solution)/shard_map/ppermute | solution.py:601
  31.5 5.0 %collective-permute-start = (bf16[32,16,128]{2,1,0:T(8,128)(2,1)S(1)}, bf16[32,16,128]{2,1,0:T(8,128)(2,1)S(1)}, u32[]{:S(2)}, u32[]{:S(2)}) collective-permute-start(bf16[32,16,128]{2,1,0:T(8,128)(2,1)S(1)} %shard_map.127), channel_id=1, source_target_pairs={{0,8},{1,9},{2,10},{3,11},{4,12},{5,13},{6,14},{7,15},{8,0},{9,1},... | collective-permute-start | bytes 393224 | tf_op jit(solution)/shard_map/ppermute | solution.py:601
  36.6 19.9 %collective-permute-start.5 = (bf16[4,32,16,128]{3,2,1,0:T(8,128)(2,1)S(1)}, bf16[4,32,16,128]{3,2,1,0:T(8,128)(2,1)S(1)}, u32[]{:S(2)}, u32[]{:S(2)}) collective-permute-start(bf16[4,32,16,128]{3,2,1,0:T(8,128)(2,1)S(1)} %pad_maximum_fusion.refs_0_), channel_id=1, source_target_pairs={{0,6},{1,7},{2,4},{3,5},{4,2},{5,3},{6,0},{7,1},{8,14},{9,15},{10,... | collective-permute-start | bytes 1572872 | tf_op jit(solution)/shard_map/ppermute | solution.py:601
  39.2 21.1 %collective-permute-start.4 = (bf16[4,32,16,128]{3,2,1,0:T(8,128)(2,1)S(1)}, bf16[4,32,16,128]{3,2,1,0:T(8,128)(2,1)S(1)}, u32[]{:S(2)}, u32[]{:S(2)}) collective-permute-start(bf16[4,32,16,128]{3,2,1,0:T(8,128)(2,1)S(1)} %pad_maximum_fusion.refs_0_), channel_id=1, source_target_pairs={{0,4},{1,5},{2,6},{3,7},{4,0},{5,1},{6,2},{7,3},{8,12},{9,13},{10,... | collective-permute-start | bytes 1572872 | tf_op jit(solution)/shard_map/ppermute | solution.py:601
  39.8 20.5 %collective-permute-start.3 = (bf16[4,32,16,128]{3,2,1,0:T(8,128)(2,1)S(1)}, bf16[4,32,16,128]{3,2,1,0:T(8,128)(2,1)S(1)}, u32[]{:S(2)}, u32[]{:S(2)}) collective-permute-start(bf16[4,32,16,128]{3,2,1,0:T(8,128)(2,1)S(1)} %pad_maximum_fusion.refs_0_), channel_id=1, source_target_pairs={{0,2},{1,3},{2,0},{3,1},{4,6},{5,7},{6,4},{7,5},{8,10},{9,11},{10,... | collective-permute-start | bytes 1572872 | tf_op jit(solution)/shard_map/ppermute | solution.py:601
  85.0 8.4 %collective-permute-start.20 = (f32[16,33,16,128]{3,2,1,0:T(8,128)}, f32[16,33,16,128]{3,2,1,0:T(8,128)S(1)}, u32[]{:S(2)}, u32[]{:S(2)}) collective-permute-start(f32[16,33,16,128]{3,2,1,0:T(8,128)} %get-tuple-element.115), channel_id=1, source_target_pairs={{0,1},{1,0},{2,3},{3,2},{4,5},{5,4},{6,7},{7,6},{8,9},{9,8},{10,11... | collective-permute-start | bytes 12976136 | tf_op jit(solution)/shard_map/ppermute | solution.py:601
  85.2 7.4 %collective-permute-start.21 = (f32[4,16,16,128]{3,2,1,0:T(8,128)S(1)}, f32[4,16,16,128]{3,2,1,0:T(8,128)S(1)}, u32[]{:S(2)}, u32[]{:S(2)}) collective-permute-start(f32[4,16,16,128]{3,2,1,0:T(8,128)S(1)} %get-tuple-element.116), channel_id=1, source_target_pairs={{0,1},{1,0},{2,3},{3,2},{4,5},{5,4},{6,7},{7,6},{8,9},{9,8},{10,11... | collective-permute-start | bytes 1572872 | tf_op jit(solution)/shard_map/ppermute | solution.py:601
  93.3 25.1 %collective-permute-start.22 = (f32[768,128]{1,0:T(8,128)S(1)}, f32[768,128]{1,0:T(8,128)S(1)}, u32[]{:S(2)}, u32[]{:S(2)}) collective-permute-start(f32[768,128]{1,0:T(8,128)S(1)} %get-tuple-element.124), channel_id=1, source_target_pairs={{0,1},{1,0},{2,3},{3,2},{4,5},{5,4},{6,7},{7,6},{8,9},{9,8},{10,11... | collective-permute-start | bytes 1179656 | tf_op jit(solution)/shard_map/ppermute | solution.py:601
  94.5 27.7 %collective-permute-start.25 = (bf16[148,16,128]{2,1,0:T(8,128)(2,1)S(1)}, bf16[148,16,128]{2,1,0:T(8,128)(2,1)S(1)}, u32[]{:S(2)}, u32[]{:S(2)}) collective-permute-start(bf16[148,16,128]{2,1,0:T(8,128)(2,1)S(1)} %get-tuple-element.145), channel_id=1, source_target_pairs={{0,2},{1,3},{2,0},{3,1},{4,6},{5,7},{6,4},{7,5},{8,10},{9,11},{10,... | collective-permute-start | bytes 1818632 | tf_op jit(solution)/shard_map/ppermute | solution.py:601
  96.0 26.2 %collective-permute-start.26 = (bf16[148,16,128]{2,1,0:T(8,128)(2,1)S(1)}, bf16[148,16,128]{2,1,0:T(8,128)(2,1)S(1)}, u32[]{:S(2)}, u32[]{:S(2)}) collective-permute-start(bf16[148,16,128]{2,1,0:T(8,128)(2,1)S(1)} %get-tuple-element.146), channel_id=1, source_target_pairs={{0,4},{1,5},{2,6},{3,7},{4,0},{5,1},{6,2},{7,3},{8,12},{9,13},{10,... | collective-permute-start | bytes 1818632 | tf_op jit(solution)/shard_map/ppermute | solution.py:601
  97.5 27.2 %collective-permute-start.27 = (bf16[148,16,128]{2,1,0:T(8,128)(2,1)S(1)}, bf16[148,16,128]{2,1,0:T(8,128)(2,1)S(1)}, u32[]{:S(2)}, u32[]{:S(2)}) collective-permute-start(bf16[148,16,128]{2,1,0:T(8,128)(2,1)S(1)} %get-tuple-element.147), channel_id=1, source_target_pairs={{0,6},{1,7},{2,4},{3,5},{4,2},{5,3},{6,0},{7,1},{8,14},{9,15},{10,... | collective-permute-start | bytes 1818632 | tf_op jit(solution)/shard_map/ppermute | solution.py:601
  118.4 3.7 %collective-permute-start.24 = (f32[1160,128]{1,0:T(8,128)S(1)}, f32[1160,128]{1,0:T(8,128)S(1)}, u32[]{:S(2)}, u32[]{:S(2)}) collective-permute-start(f32[1160,128]{1,0:T(8,128)S(1)} %get-tuple-element.136), channel_id=1, source_target_pairs={{0,1},{1,0},{2,3},{3,2},{4,5},{5,4},{6,7},{7,6},{8,9},{9,8},{10,11... | collective-permute-start | bytes 1781768 | tf_op jit(solution)/shard_map/ppermute | solution.py:601
  125.5 7.2 %collective-permute-start.31 = (bf16[49,16,128]{2,1,0:T(8,128)(2,1)S(1)}, bf16[49,16,128]{2,1,0:T(8,128)(2,1)S(1)}, u32[]{:S(2)}, u32[]{:S(2)}) collective-permute-start(bf16[49,16,128]{2,1,0:T(8,128)(2,1)S(1)} %get-tuple-element.172), channel_id=1, source_target_pairs={{0,2},{1,3},{2,0},{3,1},{4,6},{5,7},{6,4},{7,5},{8,10},{9,11},{10,... | collective-permute-start | bytes 602120 | tf_op jit(solution)/shard_map/ppermute | solution.py:601
  126.9 7.9 %collective-permute-start.32 = (bf16[49,16,128]{2,1,0:T(8,128)(2,1)S(1)}, bf16[49,16,128]{2,1,0:T(8,128)(2,1)S(1)}, u32[]{:S(2)}, u32[]{:S(2)}) collective-permute-start(bf16[49,16,128]{2,1,0:T(8,128)(2,1)S(1)} %get-tuple-element.173), channel_id=1, source_target_pairs={{0,4},{1,5},{2,6},{3,7},{4,0},{5,1},{6,2},{7,3},{8,12},{9,13},{10,... | collective-permute-start | bytes 602120 | tf_op jit(solution)/shard_map/ppermute | solution.py:601
  128.4 8.7 %collective-permute-start.33 = (bf16[49,16,128]{2,1,0:T(8,128)(2,1)S(1)}, bf16[49,16,128]{2,1,0:T(8,128)(2,1)S(1)}, u32[]{:S(2)}, u32[]{:S(2)}) collective-permute-start(bf16[49,16,128]{2,1,0:T(8,128)(2,1)S(1)} %get-tuple-element.174), channel_id=1, source_target_pairs={{0,6},{1,7},{2,4},{3,5},{4,2},{5,3},{6,0},{7,1},{8,14},{9,15},{10,... | collective-permute-start | bytes 602120 | tf_op jit(solution)/shard_map/ppermute | solution.py:601
  129.9 10.8 %collective-permute-start.28 = (bf16[33,16,128]{2,1,0:T(8,128)(2,1)S(1)}, bf16[33,16,128]{2,1,0:T(8,128)(2,1)S(1)}, u32[]{:S(2)}, u32[]{:S(2)}) collective-permute-start(bf16[33,16,128]{2,1,0:T(8,128)(2,1)S(1)} %get-tuple-element.168), channel_id=1, source_target_pairs={{0,8},{1,9},{2,10},{3,11},{4,12},{5,13},{6,14},{7,15},{8,0},{9,1},... | collective-permute-start | bytes 405512 | tf_op jit(solution)/shard_map/ppermute | solution.py:601
  132.4 13.7 %collective-permute-start.29 = (bf16[33,16,128]{2,1,0:T(8,128)(2,1)S(1)}, bf16[33,16,128]{2,1,0:T(8,128)(2,1)S(1)}, u32[]{:S(2)}, u32[]{:S(2)}) collective-permute-start(bf16[33,16,128]{2,1,0:T(8,128)(2,1)S(1)} %get-tuple-element.169), channel_id=1, source_target_pairs={{0,16},{1,17},{2,18},{3,19},{4,20},{5,21},{6,22},{7,23},{8,24},{9,... | collective-permute-start | bytes 405512 | tf_op jit(solution)/shard_map/ppermute | solution.py:601
  132.7 13.4 %collective-permute-start.30 = (bf16[33,16,128]{2,1,0:T(8,128)(2,1)S(1)}, bf16[33,16,128]{2,1,0:T(8,128)(2,1)S(1)}, u32[]{:S(2)}, u32[]{:S(2)}) collective-permute-start(bf16[33,16,128]{2,1,0:T(8,128)(2,1)S(1)} %get-tuple-element.170), channel_id=1, source_target_pairs={{0,24},{1,25},{2,26},{3,27},{4,28},{5,29},{6,30},{7,31},{8,16},{9,... | collective-permute-start | bytes 405512 | tf_op jit(solution)/shard_map/ppermute | solution.py:601
  137.8 8.3 %collective-permute-start.34 = (bf16[17,16,128]{2,1,0:T(8,128)(2,1)S(1)}, bf16[17,16,128]{2,1,0:T(8,128)(2,1)S(1)}, u32[]{:S(2)}, u32[]{:S(2)}) collective-permute-start(bf16[17,16,128]{2,1,0:T(8,128)(2,1)S(1)} %get-tuple-element.181), channel_id=1, source_target_pairs={{0,8},{1,9},{2,10},{3,11},{4,12},{5,13},{6,14},{7,15},{8,0},{9,1},... | collective-permute-start | bytes 208904 | tf_op jit(solution)/shard_map/ppermute | solution.py:601
  140.4 10.4 %collective-permute-start.35 = (bf16[17,16,128]{2,1,0:T(8,128)(2,1)S(1)}, bf16[17,16,128]{2,1,0:T(8,128)(2,1)S(1)}, u32[]{:S(2)}, u32[]{:S(2)}) collective-permute-start(bf16[17,16,128]{2,1,0:T(8,128)(2,1)S(1)} %get-tuple-element.182), channel_id=1, source_target_pairs={{0,16},{1,17},{2,18},{3,19},{4,20},{5,21},{6,22},{7,23},{8,24},{9,... | collective-permute-start | bytes 208904 | tf_op jit(solution)/shard_map/ppermute | solution.py:601
  140.6 10.2 %collective-permute-start.36 = (bf16[17,16,128]{2,1,0:T(8,128)(2,1)S(1)}, bf16[17,16,128]{2,1,0:T(8,128)(2,1)S(1)}, u32[]{:S(2)}, u32[]{:S(2)}) collective-permute-start(bf16[17,16,128]{2,1,0:T(8,128)(2,1)S(1)} %get-tuple-element.183), channel_id=1, source_target_pairs={{0,24},{1,25},{2,26},{3,27},{4,28},{5,29},{6,30},{7,31},{8,16},{9,... | collective-permute-start | bytes 208904 | tf_op jit(solution)/shard_map/ppermute | solution.py:601
  (15 other events, 99.6 us)
where the time goes:
time: 153 us; the launch traced here: 152 us
  Pallas kernels  74.2 us (48%)
  starting transfers between devices  36.2 us (24%)
  waiting for transfers between devices  35.9 us (23%)
  local copies, waits for them, and re-layouts  5.03 us (3%)
    ppermute x37, starting transfers between devices, swap(): return lax.ppermute(x, AXES, [(i, i ^ bit) for i in range(n)])  36.2 us
    ppermute x37, waiting for transfers between devices, swap(): return lax.ppermute(x, AXES, [(i, i ^ bit) for i in range(n)])  35.9 us
    pallas_call x2, Pallas kernels, back(): call(partial(back_body, first), [((ROWS, 128 * pairs), BF)] * 3 + shares...  27.4 us
    pallas_call x1, Pallas kernels, local(): call(feed_body, [(row, BF, ANY), (row, F32), (row, BF)] + [((n // 2, G_TI...  20.5 us
    pallas_call x1, Pallas kernels, local(): call(attend_body, [(row, BF), ((D + 16, ROWS), BF), ((8, ROWS), F32)], [V...  13.1 us
    unnamed x20, local copies, waits for them, and re-layouts  4.95 us
    pallas_call x6, Pallas kernels, small(): return call(body, outs, ins, scratch, 2 * size, 6 * size, 16)(*args)  3.95 us
    pallas_call x1, Pallas kernels, local(): call(project_body, [((H, ROWS, 128), BF)] * 2 + [(row, BF), ((PARTS, A_TI...  3.15 us
  transfers between devices with their start and end apart: 37, of which 15 were waited for; matrix products, arithmetic and copies ran while one was open for 0% of the time, Pallas kernels for 34%

commit v1 on v0

--- a/solution.py
+++ b/solution.py
@@ -24,7 +24,7 @@
 BF = jnp.bfloat16
 F32 = jnp.float32
 CHUNK = 64
-SHARE = 6 * 64
+SHARE = 12 * 64
 BIG = 512
 VMEM = pl.BlockSpec(memory_space=pltpu.VMEM)
 SMEM = pl.BlockSpec(memory_space=pltpu.SMEM)
@@ -221,7 +221,7 @@
     pieces, refs = refs[:8], refs[8:]
     (layer_out, gm, gctx, keep_out, send_out, wo_keep, wo_send) = refs[:7]
     (w, low_t, gbr, gs_all, active_t, gh_all, v0, v1, b0, b1, active, second, gmid, sums) = refs[7:21]
-    (layer, both, sems) = refs[21:]
+    (layer, keep, send, sems) = refs[21:]
     values, backs = (v0, v1), (b0, b1)
     wo = w_in.at[24:32]
     assemble(pieces, w, place[0])
@@ -314,12 +314,17 @@
 
     zero = jnp.zeros((1, D), F32)
     attend_sum, feed_sum = lax.fori_loop(0, 4, rows, (zero, zero))
-    odd = place[1]
-
-    def send(slots, sem):
+    odd = place[1] == 1
+
+    def store(o, tile, even, other):
+        keep[o // 2, tile] = jnp.where(odd, other, even)
+        mail = jnp.where(odd, even, other)
+        send[o // 2, tile] = (split_row(mail) if tile == G_TILES - 1 else mail).astype(BF)
+
+    def post(slots, sem):
         copies = [
-            pltpu.make_async_copy(both.at[0, slots], keep_out.at[slots], sems.at[sem]),
-            pltpu.make_async_copy(both.at[1, slots], send_out.at[slots], sems.at[sem + 1]),
+            pltpu.make_async_copy(keep.at[slots], keep_out.at[slots], sems.at[sem]),
+            pltpu.make_async_copy(send.at[slots], send_out.at[slots], sems.at[sem + 1]),
         ]
         for copy in copies:
             copy.start()
@@ -328,11 +333,11 @@
     for j in range(4):
         val = nn(low_t[...], gh_all[:, 512 * j : 512 * j + 512])
         sums[0:1, 4 * D + 512 * j : 4 * D + 512 * j + 512] = val[D : D + 1]
-        for o in range(16):
+        for o in range(0, 16, 2):
             for jj in range(4):
                 for i in range(2):
                     top, col = 32 * o + 16 * i, slice(128 * jj, 128 * jj + 128)
-                    both[(o % 2) ^ odd, o // 2, 2 * (4 * j + jj) + i] = val[top : top + 16, col]
+                    store(o, 2 * (4 * j + jj) + i, val[top : top + 16, col], val[top + 32 : top + 48, col])
     val = nn(ctx_t[...], gbr[...])
     sums[0:1, 2 * D : 3 * D] = val[D : D + 1]
     for o in range(0, 8, 2):
@@ -340,8 +345,8 @@
             for i in range(4):
                 top, col = 64 * o + 16 * i, slice(128 * j, 128 * j + 128)
                 even, other = val[top : top + 16, col], val[top + 64 : top + 80, col]
-                wo_keep[o // 2, 4 * j + i] = jnp.where(odd == 1, other, even)
-                wo_send[o // 2, 4 * j + i] = jnp.where(odd == 1, even, other)
+                wo_keep[o // 2, 4 * j + i] = jnp.where(odd, other, even)
+                wo_send[o // 2, 4 * j + i] = jnp.where(odd, even, other)
     copies = []
     lane = lax.broadcasted_iota(jnp.int32, (1, 128), 1)
     gate = jnp.where(lane == 2 * place[2], jnp.sum(attend_sum), 0.0)
@@ -355,115 +360,118 @@
     sums[0:1, 0 : 2 * D] = jnp.zeros((1, 2 * D), F32)
 
     def tail(o):
-        both[(o % 2) ^ odd, o // 2, G_TILES - 1] = jnp.where(row == 0, sums[0:1, 128 * o : 128 * o + 128], base)
+        even = jnp.where(row == 0, sums[0:1, 128 * o : 128 * o + 128], base)
+        other = jnp.where(row == 0, sums[0:1, 128 * o + 128 : 128 * o + 256], base)
+        store(o, G_TILES - 1, even, other)
 
     for j in (3, 2, 1, 0):
         val = nn(active_t[512 * j : 512 * j + (528 if j == 3 else 512)], gs_all[...])
         if j == 3:
             sums[0:1, 3 * D : 4 * D] = val[D : D + 1]
-            for o in range(16):
+            for o in range(0, 16, 2):
                 tail(o)
-            copies += send(pl.ds(0, 8), 5)
-        for o in range(4):
+            copies += post(pl.ds(0, 8), 5)
+        for o in (0, 2):
             tail(16 + 4 * j + o)
             for jj in range(4):
                 for i in range(8):
                     top, col = 128 * o + 16 * i, slice(128 * jj, 128 * jj + 128)
-                    both[(o % 2) ^ odd, 8 + 2 * j + o // 2, 8 * jj + i] = val[top : top + 16, col]
-        copies += send(pl.ds(8 + 2 * j, 2), 7 + 2 * j)
+                    store(16 + 4 * j + o, 8 * jj + i, val[top : top + 16, col], val[top + 128 : top + 144, col])
+        copies += post(pl.ds(8 + 2 * j, 2), 7 + 2 * j)
     pltpu.make_async_copy(layer, layer_out, sems.at[0]).wait()
     for copy in copies:
         copy.wait()
 
 
-def back_body(first, place, q_all, k_all, v_all, g_all, lse, x_t, *refs):
-    if first:
-        before, *refs = refs
-    dq_out, dk_out, dv_out, *refs = refs
-    if first:
-        keeps, sends, refs, sums = refs[:2], refs[2:4], refs[4:-1], refs[-1]
-    else:
-        keep, send, sums, *refs = refs
-        keeps, sends = [(ref.at[:SHARE], ref.at[SHARE:]) for ref in (keep, send)]
-    k_t, dq_t, dk_acc, dv_acc, s0, s1, g0, g1, p0, p1, d0, d1 = refs
+def pair_back(p, parities, q_all, k_all, v_all, g_all, lse, dq_t, dk_acc, dv_acc, firsts, buffers):
+    k_t, s0, s1, g0, g1, p0, p1, d0, d1 = buffers
     scores, grads, probs, diffs = (s0, s1), (g0, g1), (p0, p1), (d0, d1)
-    steps = [(parity, r) for parity in range(2) for r in range(4)]
+    steps = [(parity, r) for parity in parities for r in range(4)]
+    lanes = pl.ds(pl.multiple_of(p * 128, 128), 128)
+    q_in, k_in = q_all.at[pl.ds(2 * p, 2)], k_all.at[pl.ds(2 * p, 2)]
+    for parity in parities:
+        k_t[parity] = k_in[parity].T
+
+    def mine(block, i):
+        return jnp.where(half_of(steps[i][0], (256, 128)), block, jnp.zeros_like(block))
+
+    def score(i):
+        parity, r = steps[i]
+        qa = q_in[parity, r * 256 : r * 256 + 256]
+        ga = mine(g_all[r * 256 : r * 256 + 256, lanes], i)
+
+        def part(c):
+            scores[i % 2][c : c + BIG] = nt(k_in[parity, c : c + BIG], qa)
+
+        def grad(c):
+            grads[i % 2][c : c + BIG] = nt(v_all[c : c + BIG, lanes], ga)
+
+        return [task for c in range(0, ROWS, BIG) for task in (partial(part, c), partial(grad, c))]
+
+    def soften(i):
+        parity, r = steps[i]
+        s, g, out, diff = scores[i % 2], grads[i % 2], probs[i % 2], diffs[i % 2]
+        logs = lse[pl.ds(2 * p + parity, 1), r * 256 : r * 256 + 256]
+        state = {}
+
+        def power(c):
+            e = jnp.exp(s[c : c + CHUNK] - logs)
+            s[c : c + CHUNK] = e
+            out[c : c + CHUNK] = e.astype(BF)
+            part = jnp.sum((e * g[c : c + CHUNK]).reshape(-1, 8, 256), axis=0)
+            state["inner"] = state["inner"] + part if c else part
+            if c == ROWS - CHUNK:
+                state["inner"] = jnp.sum(state["inner"], axis=0, keepdims=True)
+
+        def minus(c):
+            diff[c : c + CHUNK] = (s[c : c + CHUNK] * (g[c : c + CHUNK] - state["inner"])).astype(BF)
+
+        at = range(0, ROWS, CHUNK)
+        return [(5.5, partial(power, c)) for c in at] + [(2.5, partial(minus, c)) for c in at]
+
+    def collect(i):
+        parity, r = steps[i]
+        rows = slice(64 * parity, 64 * parity + 64)
+        at = slice(r * 256, r * 256 + 256)
+        qz, gz = mine(q_in[parity, at], i), mine(g_all[at, lanes], i)
+        total = []
+
+        def part(c):
+            total.append(nn(k_t[parity, rows, c : c + 256], diffs[i % 2][c : c + 256]))
+            if c == ROWS - 256:
+                dq_t[rows, r * 256 : r * 256 + 256] = ((total[0] + total[1]) + (total[2] + total[3])) * 0.125
+
+        def add(acc, first, ref, z, c):
+            val = nn(ref[c : c + BIG], z)
+            base = acc if i else first
+            acc[c : c + BIG] = val if base is None else base[c : c + BIG] + val
+
+        tasks = []
+        for c in range(0, ROWS, 256):
+            if c % BIG == 0:
+                tasks += [partial(add, dv_acc, firsts[1], probs[i % 2], gz, c), partial(add, dk_acc, firsts[0], diffs[i % 2], qz, c)]
+            tasks += [partial(part, c)]
+        return tasks
+
+    for task in score(0):
+        task()
+    last = len(steps) - 1
+    for i in range(last + 2):
+        later = (score(i + 1) if i < last else []) + (collect(i - 1) if i else [])
+        mix(soften(i) if i <= last else [], later)
+
+
+def back_first_body(q_all, k_all, v_all, g_all, lse, dq_t, dk_acc, dv_acc, *buffers):
+    pair_back(0, (0,), q_all, k_all, v_all, g_all, lse, dq_t, dk_acc, dv_acc, (None, None), buffers)
+
+
+def back_body(place, q_all, k_all, v_all, g_all, lse, x_t, dq_first, dk_first, dv_first, *refs):
+    (dq_out, dk_out, dv_out, keep, send), refs = refs[:5], refs[5:]
+    dq_t, dk_acc, dv_acc, sums, *buffers = refs
     odd = place[1] == 1
-    sums[...] = before[...] if first else jnp.zeros_like(sums)
-
-    def pair(turn, _):
-        p = turn + first
-        lanes = pl.ds(pl.multiple_of(p * 128, 128), 128)
-        out = pl.ds(pl.multiple_of(turn * 128, 128), 128)
-        q_in, k_in = q_all.at[pl.ds(2 * p, 2)], k_all.at[pl.ds(2 * p, 2)]
-        for parity in range(2):
-            k_t[parity] = k_in[parity].T
-
-        def mine(block, i):
-            return jnp.where(half_of(steps[i][0], (256, 128)), block, jnp.zeros_like(block))
-
-        def score(i):
-            parity, r = steps[i]
-            qa = q_in[parity, r * 256 : r * 256 + 256]
-            ga = mine(g_all[r * 256 : r * 256 + 256, lanes], i)
-
-            def part(c):
-                scores[i % 2][c : c + BIG] = nt(k_in[parity, c : c + BIG], qa)
-
-            def grad(c):
-                grads[i % 2][c : c + BIG] = nt(v_all[c : c + BIG, lanes], ga)
-
-            return [task for c in range(0, ROWS, BIG) for task in (partial(part, c), partial(grad, c))]
-
-        def soften(i):
-            parity, r = steps[i]
-            s, g, out, diff = scores[i % 2], grads[i % 2], probs[i % 2], diffs[i % 2]
-            logs = lse[pl.ds(2 * p + parity, 1), r * 256 : r * 256 + 256]
-            state = {}
-
-            def power(c):
-                e = jnp.exp(s[c : c + CHUNK] - logs)
-                s[c : c + CHUNK] = e
-                out[c : c + CHUNK] = e.astype(BF)
-                part = jnp.sum((e * g[c : c + CHUNK]).reshape(-1, 8, 256), axis=0)
-                state["inner"] = state["inner"] + part if c else part
-                if c == ROWS - CHUNK:
-                    state["inner"] = jnp.sum(state["inner"], axis=0, keepdims=True)
-
-            def minus(c):
-                diff[c : c + CHUNK] = (s[c : c + CHUNK] * (g[c : c + CHUNK] - state["inner"])).astype(BF)
-
-            at = range(0, ROWS, CHUNK)
-            return [(5.5, partial(power, c)) for c in at] + [(2.5, partial(minus, c)) for c in at]
-
-        def collect(i):
-            parity, r = steps[i]
-            rows = slice(64 * parity, 64 * parity + 64)
-            at = slice(r * 256, r * 256 + 256)
-            qz, gz = mine(q_in[parity, at], i), mine(g_all[at, lanes], i)
-            total = []
-
-            def part(c):
-                total.append(nn(k_t[parity, rows, c : c + 256], diffs[i % 2][c : c + 256]))
-                if c == ROWS - 256:
-                    dq_t[rows, r * 256 : r * 256 + 256] = ((total[0] + total[1]) + (total[2] + total[3])) * 0.125
-
-            def add(acc, ref, z, c):
-                val = nn(ref[c : c + BIG], z)
-                acc[c : c + BIG] = acc[c : c + BIG] + val if i else val
-
-            tasks = []
-            for c in range(0, ROWS, 256):
-                if c % BIG == 0:
-                    tasks += [partial(add, dv_acc, probs[i % 2], gz, c), partial(add, dk_acc, diffs[i % 2], qz, c)]
-                tasks += [partial(part, c)]
-            return tasks
-
-        for task in score(0):
-            task()
-        for i in range(9):
-            later = (score(i + 1) if i < 7 else []) + (collect(i - 1) if i else [])
-            mix(soften(i) if i < 8 else [], later)
+
+    def finish(p):
+        out = pl.ds(pl.multiple_of(p * 128, 128), 128)
         dq = dq_t[...].astype(BF).T
         dk = dk_acc[...].astype(BF)
         dv = dv_acc[...].astype(BF)
@@ -478,25 +486,26 @@
                 for i in range(4):
                     col, top = slice(128 * index, 128 * index + 128), 64 * o + 16 * i
                     even, other = val[top : top + 16, col], val[top + 64 : top + 80, col]
-                    part, at = part_of(index, o // 2)
-                    at = pl.ds(pl.multiple_of(SHARE * turn + 64 * at + 16 * i, 16), 16)
-                    keeps[part][at] = jnp.where(odd, other, even)
-                    sends[part][at] = jnp.where(odd, even, other)
+                    at = pl.ds(pl.multiple_of(SHARE * p + 64 * (4 * index + o // 2) + 16 * i, 16), 16)
+                    keep[at] = jnp.where(odd, other, even)
+                    send[at] = jnp.where(odd, even, other)
+
+    def pair(p, _):
+        pair_back(p, (0, 1), q_all, k_all, v_all, g_all, lse, dq_t, dk_acc, dv_acc, (None, None), buffers)
+        finish(p)
         return 0
 
-    lax.fori_loop(0, dq_out.shape[1] // 128, pair, 0)
-    if first:
-        row = lax.broadcasted_iota(jnp.int32, (8, 128), 0)
-        even, other = jnp.zeros((8, 128), F32), jnp.zeros((8, 128), F32)
-        for o in range(0, 8, 2):
-            even = jnp.where(row == o // 2, sums[o : o + 1, :], even)
-            other = jnp.where(row == o // 2, sums[o + 1 : o + 2, :], other)
-        keeps[1][3 * SHARE :] = jnp.where(odd, other, even)
-        sends[1][3 * SHARE :] = jnp.where(odd, even, other)
-
-
-def part_of(index, slot):
-    return (index, slot) if index < 2 else (slot // 2, 4 + slot % 2)
+    dq_t[:64] = dq_first[...]
+    pair_back(0, (1,), q_all, k_all, v_all, g_all, lse, dq_t, dk_acc, dv_acc, (dk_first, dv_first), buffers)
+    finish(0)
+    lax.fori_loop(1, 4, pair, 0)
+    row = lax.broadcasted_iota(jnp.int32, (8, 128), 0)
+    even, other = jnp.zeros((8, 128), F32), jnp.zeros((8, 128), F32)
+    for o in range(0, 8, 2):
+        even = jnp.where(row == o // 2, sums[o : o + 1, :], even)
+        other = jnp.where(row == o // 2, sums[o + 1 : o + 2, :], other)
+    keep[4 * SHARE :] = jnp.where(odd, other, even)
+    send[4 * SHARE :] = jnp.where(odd, even, other)
 
 
 def split_row(tile):
@@ -517,9 +526,10 @@
         here = place[3] ^ t
         out = outs[t]
         for z in range(4):
-            total = keep[4 * z + here] + got[4 * z + here]
-            out[size * z : size * z + size - 1] = total[: size - 1].astype(out.dtype)
-            out[size * z + size - 1] = (split_row(total[size - 1]) if t else total[size - 1]).astype(out.dtype)
+            at = 4 * z + here
+            out[size * z : size * z + size - 1] = (keep[at, : size - 1] + got[at, : size - 1].astype(F32)).astype(out.dtype)
+            total = keep[at, size - 1] + join_row(got[at, size - 1].astype(F32))
+            out[size * z + size - 1] = (split_row(total) if t else total).astype(out.dtype)
         out[4 * size :] = (wo_keep[here] + wo_got[here]).astype(out.dtype)
 
 
@@ -538,27 +548,17 @@
     wo_out[...] = keep[at] + g1[at].astype(F32) + g2[at].astype(F32) + g3[at].astype(F32)
 
 
-def square_xy_body(place, first, first_got, a, b, a_got, b_got, *outs):
-    def added(p, part, at):
-        rows = pl.ds(pl.multiple_of(at * 64, 64), 64)
-        if p == 0:
-            rows = pl.ds(pl.multiple_of(SHARE * part + at * 64, 64), 64)
-            return first[rows] + first_got[rows]
-        rows = pl.ds(pl.multiple_of(SHARE * (p - 1) + at * 64, 64), 64)
-        return ((a, b)[part])[rows] + ((a_got, b_got)[part])[rows]
-
+def square_xy_body(place, keep, got, *outs):
     for t in range(4):
         here = place[3] ^ t
         out = outs[t]
         for z in range(3):
             for p in range(4):
-                if z < 2:
-                    total = added(p, z, here)
-                else:
-                    total = jnp.where(here < 2, added(p, 0, 4 + here % 2), added(p, 1, 4 + here % 2))
+                rows = pl.ds(pl.multiple_of(SHARE * p + 64 * (4 * z + here), 64), 64)
+                total = keep[rows] + got[rows]
                 out[16 * z + 4 * p : 16 * z + 4 * p + 4] = total.reshape(4, 16, 128).astype(out.dtype)
         row = lax.broadcasted_iota(jnp.int32, (16, 128), 0)
-        total = b[pl.ds(3 * SHARE + here, 1)] + b_got[pl.ds(3 * SHARE + here, 1)]
+        total = keep[pl.ds(4 * SHARE + here, 1)] + got[pl.ds(4 * SHARE + here, 1)]
         total = jnp.where(row == 0, total, 0.0)
         out[48] = (split_row(total) if t else total).astype(out.dtype)
 
@@ -579,13 +579,12 @@
         out[16] = (split_row(whole[at, 16]) if t else whole[at, 16]).astype(out.dtype)
 
 
-def input_body(gm, *refs):
-    w, out = refs[6:]
+def input_body(gm, dq, dk, dv, w, out):
     for r in range(4):
         at = slice(256 * r, 256 * r + 256)
         total = gm[at, :]
         for index in range(3):
-            total = total + nt(jnp.concatenate([ref[at, :] for ref in refs[index:6:3]], axis=1), square(w, index))
+            total = total + nt((dq, dk, dv)[index][at, :], square(w, index))
         out[at, :] = total
 
 
@@ -654,6 +653,11 @@
         for j in range(4):
             for i in range(8):
                 out[8 * j + i] = wide[pl.ds(64 * i + j, 16, stride=4), :].astype(BF)
+
+
+def copy_body(ref, out):
+    for i in range(5):
+        out[i] = ref[i]
 
 
 def finish_body(place, keep_f, f1, f2, f3, keep_a, a1, a2, a3, att, ff, bias, gate):
@@ -729,10 +733,14 @@
             pack_feed_body, [((F_TILES, 16, 128), BF)], (place, feedforward.reshape(-1, 128)), [((512, 128), F32)]
         )
         stack_a, masks = lax.optimization_barrier((along_z(own_a, n), masks))
-        stack_f = along_z(own_f, n)
+        far = [swap(own_f, n, 16), swap(own_f, n, 24)]
         chips_a = along_xy(stack_a, n)
+        far, own_f, place = lax.optimization_barrier((far, own_f, place))
+        near = swap(own_f, n, 8)
+        (place,) = call(copy_body, [((5,), jnp.int32, SMEM)], [SMEM], [], 8 << 30, 1000, 16)(place)
+        chips_a, place = lax.optimization_barrier((chips_a, place))
         ga_all = across(chips_a, n)
-        chips_f = along_xy(stack_f, n)
+        chips_f = along_xy(jnp.stack([own_f, near] + far), n)
     else:
         ga_all, gf_all = pieces_any(attention, feedforward, biases)
         place = jnp.zeros((5,), jnp.int32)
@@ -740,60 +748,60 @@
     q, k, v, w, bias = call(
         project_body,
         [((H, ROWS, 128), BF)] * 2 + [(row, BF), ((PARTS, A_TILES, 16, 128), BF), ((1, 8 * D), F32)],
-        [SMEM] + [VMEM] * 11, [], 2 << 30, 10 << 20, 20,
+        [SMEM] + [VMEM] * 11, [], 1000, 1000, 20,
     )(place, tokens, *masks, *ga_all)
     ctx, ctx_t, lse = call(
         attend_body,
         [(row, BF), ((D + 16, ROWS), BF), ((8, ROWS), F32)],
         [VMEM] * 3,
         [((128, ROWS), BF), ((128, ROWS), F32)] + [((ROWS, 256), F32)] * 2 + [((ROWS, 256), BF)] * 2,
-        12 << 30, 4 << 20, 20,
+        1000, 1000, 20,
     )(q, k, v)
     if direct:
         chips_f, ctx = lax.optimization_barrier((chips_f, ctx))
         gf_all = across(chips_f, n)
     layer, gm, gctx, ff_keep, ff_send, wo_keep, wo_send = call(
         feed_body,
-        [(row, BF, ANY), (row, F32), (row, BF)] + [((n // 2, G_TILES, 16, 128), F32, ANY)] * 2
+        [(row, BF, ANY), (row, F32), (row, BF)]
+        + [((n // 2, G_TILES, 16, 128), F32, ANY), ((n // 2, G_TILES, 16, 128), BF, ANY)]
         + [((4, 16, 16, 128), F32)] * 2,
         [SMEM, SMEM] + [VMEM] * 14,
         [((PARTS, F_TILES, 16, 128), BF), ((D + 16, ROWS), BF), (row, BF), (row, BF),
          ((FF + 16, ROWS), BF), ((ROWS, FF), BF)]
         + [((256, D), F32)] * 4 + [((256, FF), BF)] + [((256, D), F32)] * 2 + [((1, 8 * D), F32)]
-        + [(row, BF), ((2, n // 2, G_TILES, 16, 128), F32), DMA((16,))],
+        + [(row, BF), ((n // 2, G_TILES, 16, 128), F32), ((n // 2, G_TILES, 16, 128), BF), DMA((16,))],
         16 << 30, 30 << 20, 36,
     )(place, gates, tokens, cotangent, ctx, ctx_t, w, bias, *gf_all)
 
-    def back(first, pairs, q, before):
-        shares = [((3 * SHARE, 128), F32), ((3 * SHARE + 8, 128), F32)] * 2 if first else [((2 * SHARE, 128), F32)] * 2
-        return call(
-            partial(back_body, first),
-            [((ROWS, 128 * pairs), BF)] * 3 + shares + ([] if first else [((8, 128), F32)]),
-            [SMEM] + [VMEM] * (7 if first else 6),
-            [((2, 128, ROWS), BF), ((128, ROWS), F32), ((ROWS, 128), F32), ((ROWS, 128), F32)]
-            + [((ROWS, 256), F32)] * 4 + [((ROWS, 256), BF)] * 4 + ([((8, 128), F32)] if first else []),
-            1000, 1000, 28,
-        )(place, q, k, v, gctx, lse, x_t, *([before] if first else []))
-
+    half, whole = (ROWS // 16, ROWS), (128, ROWS)
+    buffers = [((2, 128, ROWS), BF)] + [((ROWS, 256), F32)] * 4 + [((ROWS, 256), BF)] * 4
+    sums = [((ROWS, 128), F32)] * 2
     barrier = lax.optimization_barrier
     if direct:
         got, wo_got = swap(ff_send, n, 1), swap(wo_send, n, 1)
-    *grads, keep, send, before = back(0, 1, q, None)
+    begun = call(
+        back_first_body, [(half, F32)] + sums, [VMEM] * 5, buffers, 1000, 1000, 28
+    )(q, k, v, gctx, lse)
     if direct:
-        got, wo_got, grads, send = barrier((got, wo_got, grads, send))
+        got, wo_got, begun = barrier((got, wo_got, begun))
         parts = small(feed_xy_body, blocks_of(4 * G_TILES + 16), (place, ff_keep, got, wo_keep, wo_got))
         q, parts = barrier((q, parts))
         ff_got = hop(parts, n, 2)
+    *grads, keep, send = call(
+        back_body,
+        [(row, BF)] * 3 + [((4 * SHARE + 8, 128), F32)] * 2,
+        [SMEM] + [VMEM] * 9,
+        [(whole, F32)] + sums + [((8, 128), F32)] + buffers,
+        1000, 1000, 28,
+    )(place, q, k, v, gctx, lse, x_t, *begun)
+    if direct:
         got = swap(send, n, 1)
-    *parts, keep_a, keep_b, send_a, send_b = back(1, 3, q, before)
-    grads += parts
     (input_grad,) = call(
-        input_body, [(row, F32)], [VMEM] * 8, [], 1000, 1000, 24
+        input_body, [(row, F32)], [VMEM] * 5, [], 32 << 30, 1000, 24
     )(gm, *grads, w)
     if direct:
-        gots = [got, swap(send_a, n, 1), swap(send_b, n, 1)]
-        gots, input_grad, ff_got = barrier((gots, input_grad, ff_got))
-        parts = small(square_xy_body, blocks_of(49), (place, keep, gots[0], keep_a, keep_b, *gots[1:]))
+        got, input_grad, ff_got = barrier((got, input_grad, ff_got))
+        parts = small(square_xy_body, blocks_of(49), (place, keep, got))
         ff_got, parts = barrier((ff_got, parts))
         got = hop(parts, n, 2)
         *ff_parts, wo = small(feed_z_body, blocks_of(G_TILES) + [((16, 16, 128), F32)], (place, *ff_got))
@@ -816,19 +824,18 @@
     def reduce(flat):
         return lax.psum_scatter(flat.reshape(-1), AXES, scatter_dimension=0, tiled=True)
 
-    both = owners(ff_keep, ff_send)
+    mail = ff_send.astype(F32)
+    mail = mail.at[:, F_TILES, 0].add(mail[:, F_TILES, 4])
+    both = owners(ff_keep, mail)
     up = jax.vmap(lambda t: from_columns(t, 2 * D // n))(both[: n // 2, :F_TILES]).reshape(-1)
     down = jax.vmap(lambda t: from_columns(t, 2 * FF // n))(both[n // 2 :, :F_TILES]).reshape(-1)
     ff_grad = reduce(jnp.concatenate([up, down]))
     tail = both[0, F_TILES]
     gate_grad = lax.psum((tail[1] + tail[2] + tail[3])[:2], AXES)
-    bias_grad = owners(keep_b[3 * SHARE : 3 * SHARE + 4], send_b[3 * SHARE : 3 * SHARE + 4])
+    bias_grad = owners(keep[4 * SHARE : 4 * SHARE + 4], send[4 * SHARE : 4 * SHARE + 4])
     bias_grad = jnp.concatenate([bias_grad, both[8:, F_TILES, 0]])
-    both = []
-    for own, x_a, x_b in ((keep, keep_a, keep_b), (send, send_a, send_b)):
-        x_a, x_b = [jnp.concatenate(x).reshape(4, 6, 64, 128) for x in ((own[:SHARE], x_a), (own[SHARE:], x_b[: 3 * SHARE]))]
-        both.append(jnp.concatenate([x_a[:, :4], x_b[:, :4], x_a[:, 4:], x_b[:, 4:]], axis=1))
-    both = jnp.stack(both, axis=2).reshape(4, 24, 4, 16, 128).transpose(1, 0, 2, 3, 4)
+    both = jnp.stack([x[: 4 * SHARE].reshape(4, 12, 4, 16, 128) for x in (keep, send)], axis=2)
+    both = both.reshape(4, 24, 4, 16, 128).transpose(1, 0, 2, 3, 4)
     both = jnp.concatenate([both.reshape(24, 16, 16, 128), owners(wo_keep, wo_send)])
     att_grad = jax.vmap(lambda t: from_columns(t, 4 * D // n))(both)
     return layer, input_grad, reduce(att_grad), ff_grad, reduce(bias_grad), gate_grad

time: 153 us -> 147 us (0.961)
  waiting for transfers between devices: 35.9 us -> 31.5 us
    ppermute x37 -> x35, waiting for transfers between devices: 35.9 us -> 31.5 us  [swap(): return lax.ppermute(x, AXES, [(i, i ^ bit) for i in range(n)])]
    ppermute x37 -> x35, starting transfers between devices: 36.2 us -> 35.3 us  [swap(): return lax.ppermute(x, AXES, [(i, i ^ bit) for i in range(n)])]
    pallas_call x3 -> x4, Pallas kernels: 30.5 us -> 30.7 us  [the longest x1 23.4 us: local(): call(back_body, [(row, BF)] * 3 + [((4 * SHARE + 8, 128), F32)] * 2, [SME...]
  transfers between devices with their start and end apart: 37 -> 35, of which waited for: 15 -> 17; matrix products, arithmetic and copies ran while one was open for 0% -> 0% of each run, Pallas kernels for 34% -> 34%
where the time goes in v1:
time: 147 us; the launch traced here: 146 us
  Pallas kernels  73.5 us (50%)
  starting transfers between devices  35.3 us (24%)
  waiting for transfers between devices  31.5 us (21%)
  local copies, waits for them, and re-layouts  5.03 us (3%)
    ppermute x35, starting transfers between devices, swap(): return lax.ppermute(x, AXES, [(i, i ^ bit) for i in range(n)])  35.3 us
    ppermute x35, waiting for transfers between devices, swap(): return lax.ppermute(x, AXES, [(i, i ^ bit) for i in range(n)])  31.5 us
    pallas_call x1, Pallas kernels, local(): call(back_body, [(row, BF)] * 3 + [((4 * SHARE + 8, 128), F32)] * 2, [SME...  23.4 us
    pallas_call x1, Pallas kernels, local(): call(feed_body, [(row, BF, ANY), (row, F32), (row, BF)] + [((n // 2, G_TI...  20 us
    pallas_call x1, Pallas kernels, local(): call(attend_body, [(row, BF), ((D + 16, ROWS), BF), ((8, ROWS), F32)], [V...  13.4 us
    unnamed x20, local copies, waits for them, and re-layouts  4.95 us
    pallas_call x6, Pallas kernels, small(): return call(body, outs, ins, scratch, 2 * size, 6 * size, 16)(*args)  3.91 us
    pallas_call x1, Pallas kernels, local(): call(input_body, [(row, F32)], [VMEM] * 5, [], 32 << 30, 1000, 24)  3.14 us
  transfers between devices with their start and end apart: 35, of which 17 were waited for; matrix products, arithmetic and copies ran while one was open for 0% of the time, Pallas kernels for 34%

profile of v1, /device:TPU:0, one launch (start us, length us, event | category | flops | bytes accessed | tf_op | source)
XLA Modules:
  0.0 146.5 jit_solution(12843762217093464588)
XLA Ops:
  2.2 5.1 %collective-permute-start.2 = (bf16[17,16,128]{2,1,0:T(8,128)(2,1)S(1)}, bf16[17,16,128]{2,1,0:T(8,128)(2,1)S(1)}, u32[]{:S(2)}, u32[]{:S(2)}) collective-permute-start(bf16[17,16,128]{2,1,0:T(8,128)(2,1)S(1)} %shard_map.127), channel_id=1, source_target_pairs={{0,24},{1,25},{2,26},{3,27},{4,28},{5,29},{6,30},{7,31},{8,16},{9,... | collective-permute-start | bytes 208904 | tf_op jit(solution)/shard_map/ppermute | solution.py:600
  8.0 0.9 copy-done.3
  9.5 3.8 %collective-permute-start.7 = (bf16[32,16,128]{2,1,0:T(8,128)(2,1)S(1)}, bf16[32,16,128]{2,1,0:T(8,128)(2,1)S(1)}, u32[]{:S(2)}, u32[]{:S(2)}) collective-permute-start(bf16[32,16,128]{2,1,0:T(8,128)(2,1)S(1)} %shard_map.129), channel_id=1, source_target_pairs={{0,24},{1,25},{2,26},{3,27},{4,28},{5,29},{6,30},{7,31},{8,16},{9,... | collective-permute-start | bytes 393224 | tf_op jit(solution)/shard_map/ppermute | solution.py:600
  13.3 1.2 copy-done.1
  15.8 1.5 %shard_map.128 = (bf16[2,1024,128]{2,1,0:T(8,128)(2,1)S(1)}, bf16[2,1024,128]{2,1,0:T(8,128)(2,1)S(1)}, bf16[528,1024]{1,0:T(8,128)(2,1)S(1)}) custom-call(s32[1,3]{1,0:T(1,128)S(1)} %copy-done.5, s32[1,8]{1,0:T(1,128)S(1)} %copy-done.6, bf16[1024,512]{1,0:T(8,128)(2,1)S(1)} %copy-done.1), custom_call_target="tpu_custom_call" | custom-call | flops 1048576 | bytes 3145728 | tf_op jit(solution)/shard_map/pallas_call | solution.py:722
  17.4 2.5 %collective-permute-start.5 = (bf16[4,17,16,128]{3,2,1,0:T(8,128)(2,1)S(1)}, bf16[4,17,16,128]{3,2,1,0:T(8,128)(2,1)S(1)}, u32[]{:S(2)}, u32[]{:S(2)}) collective-permute-start(bf16[4,17,16,128]{3,2,1,0:T(8,128)(2,1)S(1)} %pad_maximum_fusion.1.refs_0_), channel_id=1, source_target_pairs={{0,6},{1,7},{2,4},{3,5},{4,2},{5,3},{6,0},{7,1},{8,14},{9,15},{10,... | collective-permute-start | bytes 835592 | tf_op jit(solution)/shard_map/ppermute | solution.py:600
  21.0 3.4 %collective-permute-done.6 = bf16[32,16,128]{2,1,0:T(8,128)(2,1)S(1)} collective-permute-done((bf16[32,16,128]{2,1,0:T(8,128)(2,1)S(1)}, bf16[32,16,128]{2,1,0:T(8,128)(2,1)S(1)}, u32[]{:S(2)}, u32[]{:S(2)}) %collective-permute-start.6) | collective-permute-done | bytes 131104 | tf_op jit(solution)/shard_map/ppermute | solution.py:600
  24.4 1.1 shard_map.130.place
  25.6 2.5 %collective-permute-done.5.refs_3_ = bf16[4,17,16,128]{3,2,1,0:T(8,128)(2,1)S(1)} collective-permute-done((bf16[4,17,16,128]{3,2,1,0:T(8,128)(2,1)S(1)}, bf16[4,17,16,128]{3,2,1,0:T(8,128)(2,1)S(1)}, u32[]{:S(2)}, u32[]{:S(2)}) %collective-permute-start.5) | collective-permute-done | bytes 278560 | tf_op jit(solution)/shard_map/ppermute | solution.py:600
  28.0 3.7 %collective-permute-done.4.refs_2_ = bf16[4,17,16,128]{3,2,1,0:T(8,128)(2,1)S(1)} collective-permute-done((bf16[4,17,16,128]{3,2,1,0:T(8,128)(2,1)S(1)}, bf16[4,17,16,128]{3,2,1,0:T(8,128)(2,1)S(1)}, u32[]{:S(2)}, u32[]{:S(2)}) %collective-permute-start.4) | collective-permute-done | bytes 278560 | tf_op jit(solution)/shard_map/ppermute | solution.py:600
  32.3 2.4 %collective-permute-start.11 = (bf16[4,32,16,128]{3,2,1,0:T(8,128)(2,1)S(1)}, bf16[4,32,16,128]{3,2,1,0:T(8,128)(2,1)S(1)}, u32[]{:S(2)}, u32[]{:S(2)}) collective-permute-start(bf16[4,32,16,128]{3,2,1,0:T(8,128)(2,1)S(1)} %pad_maximum_fusion.refs_0_), channel_id=1, source_target_pairs={{0,6},{1,7},{2,4},{3,5},{4,2},{5,3},{6,0},{7,1},{8,14},{9,15},{10,... | collective-permute-start | bytes 1572872 | tf_op jit(solution)/shard_map/ppermute | solution.py:600
  36.4 1.0 collective-permute-done.14.refs_6_
  37.8 2.6 %shard_map.131 = (bf16[8,1024,128]{2,1,0:T(8,128)(2,1)S(1)}, bf16[8,1024,128]{2,1,0:T(8,128)(2,1)S(1)}, bf16[1024,512]{1,0:T(8,128)(2,1)S(1)}, bf16[32,17,16,128]{3,2,1,0:T(8,128)(2,1)S(1)}, f32[1,4096]{1,0:T(1,128)S(1)}) custom-call(s32[5]{0:T(128)S(1)} %shard_map.130.place, bf16[1024,512]{1,0:T(8,128)(2,1)S(1)} %copy-done.2, ...), custom_call_target="tpu_custom_call" | custom-call | flops 1000 | bytes 1000 | tf_op jit(solution)/shard_map/pallas_call | solution.py:748
  40.4 13.4 %shard_map.132 = (bf16[1024,512]{1,0:T(8,128)(2,1)S(1)}, bf16[528,1024]{1,0:T(8,128)(2,1)S(1)}, f32[8,1024]{1,0:T(8,128)S(1)}) custom-call(bf16[8,1024,128]{2,1,0:T(8,128)(2,1)S(1)} %get-tuple-element.140.q_all, bf16[8,1024,128]{2,1,0:T(8,128)(2,1)S(1)} %get-tuple-element.113.k_all, bf16[1024,512]{1,0:T(8,128)(2,1)S(1)} %get-tuple-element.114.v_all), custom_call_target="tpu_custom_call" | custom-call | flops 1000 | bytes 1000 | tf_op jit(solution)/shard_map/pallas_call | solution.py:753
  53.8 4.5 %collective-permute-done.10.refs_2_ = bf16[4,32,16,128]{3,2,1,0:T(8,128)(2,1)S(1)} collective-permute-done((bf16[4,32,16,128]{3,2,1,0:T(8,128)(2,1)S(1)}, bf16[4,32,16,128]{3,2,1,0:T(8,128)(2,1)S(1)}, u32[]{:S(2)}, u32[]{:S(2)}) %collective-permute-start.10) | collective-permute-done | bytes 524320 | tf_op jit(solution)/shard_map/ppermute | solution.py:600
  62.5 20.0 %shard_map.133 = (bf16[1024,512]{1,0:T(8,128)(2,1)}, f32[1024,512]{1,0:T(8,128)S(1)}, bf16[1024,512]{1,0:T(8,128)(2,1)S(1)}, f32[16,33,16,128]{3,2,1,0:T(8,128)}...) custom-call(s32[5]{0:T(128)S(1)} %shard_map.130.place, ...), custom_call_target="tpu_custom_call" | custom-call | flops 17179869184 | bytes 31457280 | tf_op jit(solution)/shard_map/pallas_call | solution.py:763
  83.1 3.0 %shard_map.134 = (f32[64,1024]{1,0:T(8,128)S(1)}, f32[1024,128]{1,0:T(8,128)S(1)}, f32[1024,128]{1,0:T(8,128)S(1)}) custom-call(bf16[8,1024,128]{2,1,0:T(8,128)(2,1)S(1)} %get-tuple-element.140.q_all, bf16[8,1024,128]{2,1,0:T(8,128)(2,1)S(1)} %get-tuple-element.113.k_all, bf16[1024,512]{1,0:T(8,128)(2,1)S(1)} %get-tuple-element.114.v_all, ...), custom_call_target="tpu_custom_call" | custom-call | flops 1000 | bytes 1000 | tf_op jit(solution)/shard_map/pallas_call | solution.py:782
  86.1 1.5 %collective-permute-done.21.wo_got = f32[4,16,16,128]{3,2,1,0:T(8,128)S(1)} collective-permute-done((f32[4,16,16,128]{3,2,1,0:T(8,128)S(1)}, f32[4,16,16,128]{3,2,1,0:T(8,128)S(1)}, u32[]{:S(2)}, u32[]{:S(2)}) %collective-permute-start.21) | collective-permute-done | bytes 524320 | tf_op jit(solution)/shard_map/ppermute | solution.py:600
  87.6 1.0 shard_map.135
  88.7 1.5 %collective-permute-start.23 = (bf16[148,16,128]{2,1,0:T(8,128)(2,1)S(1)}, bf16[148,16,128]{2,1,0:T(8,128)(2,1)S(1)}, u32[]{:S(2)}, u32[]{:S(2)}) collective-permute-start(bf16[148,16,128]{2,1,0:T(8,128)(2,1)S(1)} %get-tuple-element.151), channel_id=1, source_target_pairs={{0,2},{1,3},{2,0},{3,1},{4,6},{5,7},{6,4},{7,5},{8,10},{9,11},{10,... | collective-permute-start | bytes 1818632 | tf_op jit(solution)/shard_map/ppermute | solution.py:600
  90.1 1.5 %collective-permute-start.24 = (bf16[148,16,128]{2,1,0:T(8,128)(2,1)S(1)}, bf16[148,16,128]{2,1,0:T(8,128)(2,1)S(1)}, u32[]{:S(2)}, u32[]{:S(2)}) collective-permute-start(bf16[148,16,128]{2,1,0:T(8,128)(2,1)S(1)} %get-tuple-element.152), channel_id=1, source_target_pairs={{0,4},{1,5},{2,6},{3,7},{4,0},{5,1},{6,2},{7,3},{8,12},{9,13},{10,... | collective-permute-start | bytes 1818632 | tf_op jit(solution)/shard_map/ppermute | solution.py:600
  92.2 23.4 %shard_map.136 = (bf16[1024,512]{1,0:T(8,128)(2,1)S(1)}, bf16[1024,512]{1,0:T(8,128)(2,1)S(1)}, bf16[1024,512]{1,0:T(8,128)(2,1)S(1)}, f32[3080,128]{1,0:T(8,128)S(1)}, f32[3080,128]{1,0:T(8,128)S(1)}) custom-call(s32[5]{0:T(128)S(1)} %shard_map.130.place, bf16[8,1024,128]{2,1,0:T(8,128)(2,1)S(1)} %get-tuple-element.140.q_all, ...), custom_call_target="tpu_custom_call" | custom-call | flops 1000 | bytes 1000 | tf_op jit(solution)/shard_map/pallas_call | solution.py:790
  115.7 3.1 %shard_map.137 = f32[1024,512]{1,0:T(8,128)} custom-call(f32[1024,512]{1,0:T(8,128)S(1)} %get-tuple-element.146.gm, bf16[1024,512]{1,0:T(8,128)(2,1)S(1)} %get-tuple-element.147.dq, bf16[1024,512]{1,0:T(8,128)(2,1)S(1)} %get-tuple-element.148.dk, bf16[1024,512]{1,0:T(8,128)(2,1)S(1)} %get-tuple-element.149.dv, ...), custom_call_target="tpu_custom_call" | custom-call | flops 34359738368 | bytes 1000 | tf_op jit(solution)/shard_map/pallas_call | solution.py:799
  119.8 1.5 %collective-permute-start.29 = (bf16[49,16,128]{2,1,0:T(8,128)(2,1)S(1)}, bf16[49,16,128]{2,1,0:T(8,128)(2,1)S(1)}, u32[]{:S(2)}, u32[]{:S(2)}) collective-permute-start(bf16[49,16,128]{2,1,0:T(8,128)(2,1)S(1)} %get-tuple-element.174), channel_id=1, source_target_pairs={{0,2},{1,3},{2,0},{3,1},{4,6},{5,7},{6,4},{7,5},{8,10},{9,11},{10,... | collective-permute-start | bytes 602120 | tf_op jit(solution)/shard_map/ppermute | solution.py:600
  121.3 1.5 collective-permute-start.30
  125.0 2.0 %collective-permute-start.27 = (bf16[33,16,128]{2,1,0:T(8,128)(2,1)S(1)}, bf16[33,16,128]{2,1,0:T(8,128)(2,1)S(1)}, u32[]{:S(2)}, u32[]{:S(2)}) collective-permute-start(bf16[33,16,128]{2,1,0:T(8,128)(2,1)S(1)} %get-tuple-element.171), channel_id=1, source_target_pairs={{0,16},{1,17},{2,18},{3,19},{4,20},{5,21},{6,22},{7,23},{8,24},{9,... | collective-permute-start | bytes 405512 | tf_op jit(solution)/shard_map/ppermute | solution.py:600
  127.0 1.6 %collective-permute-start.28 = (bf16[33,16,128]{2,1,0:T(8,128)(2,1)S(1)}, bf16[33,16,128]{2,1,0:T(8,128)(2,1)S(1)}, u32[]{:S(2)}, u32[]{:S(2)}) collective-permute-start(bf16[33,16,128]{2,1,0:T(8,128)(2,1)S(1)} %get-tuple-element.172), channel_id=1, source_target_pairs={{0,24},{1,25},{2,26},{3,27},{4,28},{5,29},{6,30},{7,31},{8,16},{9,... | collective-permute-start | bytes 405512 | tf_op jit(solution)/shard_map/ppermute | solution.py:600
  129.2 3.4 %collective-permute-done.31.g3 = bf16[49,16,128]{2,1,0:T(8,128)(2,1)S(1)} collective-permute-done((bf16[49,16,128]{2,1,0:T(8,128)(2,1)S(1)}, bf16[49,16,128]{2,1,0:T(8,128)(2,1)S(1)}, u32[]{:S(2)}, u32[]{:S(2)}) %collective-permute-start.31) | collective-permute-done | bytes 200736 | tf_op jit(solution)/shard_map/ppermute | solution.py:600
  133.9 2.0 %collective-permute-start.33 = (bf16[17,16,128]{2,1,0:T(8,128)(2,1)S(1)}, bf16[17,16,128]{2,1,0:T(8,128)(2,1)S(1)}, u32[]{:S(2)}, u32[]{:S(2)}) collective-permute-start(bf16[17,16,128]{2,1,0:T(8,128)(2,1)S(1)} %get-tuple-element.184), channel_id=1, source_target_pairs={{0,16},{1,17},{2,18},{3,19},{4,20},{5,21},{6,22},{7,23},{8,24},{9,... | collective-permute-start | bytes 208904 | tf_op jit(solution)/shard_map/ppermute | solution.py:600
  136.0 1.7 %collective-permute-start.34 = (bf16[17,16,128]{2,1,0:T(8,128)(2,1)S(1)}, bf16[17,16,128]{2,1,0:T(8,128)(2,1)S(1)}, u32[]{:S(2)}, u32[]{:S(2)}) collective-permute-start(bf16[17,16,128]{2,1,0:T(8,128)(2,1)S(1)} %get-tuple-element.185), channel_id=1, source_target_pairs={{0,24},{1,25},{2,26},{3,27},{4,28},{5,29},{6,30},{7,31},{8,16},{9,... | collective-permute-start | bytes 208904 | tf_op jit(solution)/shard_map/ppermute | solution.py:600
  138.5 6.3 %collective-permute-done.33.a2 = bf16[17,16,128]{2,1,0:T(8,128)(2,1)S(1)} collective-permute-done((bf16[17,16,128]{2,1,0:T(8,128)(2,1)S(1)}, bf16[17,16,128]{2,1,0:T(8,128)(2,1)S(1)}, u32[]{:S(2)}, u32[]{:S(2)}) %collective-permute-start.33) | collective-permute-done | bytes 69664 | tf_op jit(solution)/shard_map/ppermute | solution.py:600
  144.8 1.5 %shard_map.141 = (f32[256,128]{1,0:T(8,128)}, f32[512,128]{1,0:T(8,128)}, f32[1,128]{1,0:T(1,128)}, f32[2]{0:T(128)}) custom-call(s32[5]{0:T(128)S(1)} %shard_map.130.place, f32[33,16,128]{2,1,0:T(8,128)S(1)} %get-tuple-element.169.keep_f, bf16[33,16,128]{2,1,0:T(8,128)(2,1)S(1)} %collective-permute-done.26.f1, ...), custom_call_target="tpu_custom_call" | custom-call | flops 1048576 | bytes 1048576 | tf_op jit(solution)/shard_map/pallas_call | solution.py:813
  (76 shorter events, 19.3 us)
Async XLA Ops:
  2.2 15.2 %collective-permute-start.2 = (bf16[17,16,128]{2,1,0:T(8,128)(2,1)S(1)}, bf16[17,16,128]{2,1,0:T(8,128)(2,1)S(1)}, u32[]{:S(2)}, u32[]{:S(2)}) collective-permute-start(bf16[17,16,128]{2,1,0:T(8,128)(2,1)S(1)} %shard_map.127), channel_id=1, source_target_pairs={{0,24},{1,25},{2,26},{3,27},{4,28},{5,29},{6,30},{7,31},{8,16},{9,... | collective-permute-start | bytes 208904 | tf_op jit(solution)/shard_map/ppermute | solution.py:600
  7.3 10.1 %collective-permute-start.1 = (bf16[17,16,128]{2,1,0:T(8,128)(2,1)S(1)}, bf16[17,16,128]{2,1,0:T(8,128)(2,1)S(1)}, u32[]{:S(2)}, u32[]{:S(2)}) collective-permute-start(bf16[17,16,128]{2,1,0:T(8,128)(2,1)S(1)} %shard_map.127), channel_id=1, source_target_pairs={{0,16},{1,17},{2,18},{3,19},{4,20},{5,21},{6,22},{7,23},{8,24},{9,... | collective-permute-start | bytes 208904 | tf_op jit(solution)/shard_map/ppermute | solution.py:600
  7.3 10.1 %collective-permute-start = (bf16[17,16,128]{2,1,0:T(8,128)(2,1)S(1)}, bf16[17,16,128]{2,1,0:T(8,128)(2,1)S(1)}, u32[]{:S(2)}, u32[]{:S(2)}) collective-permute-start(bf16[17,16,128]{2,1,0:T(8,128)(2,1)S(1)} %shard_map.127), channel_id=1, source_target_pairs={{0,8},{1,9},{2,10},{3,11},{4,12},{5,13},{6,14},{7,15},{8,0},{9,1},... | collective-permute-start | bytes 208904 | tf_op jit(solution)/shard_map/ppermute | solution.py:600
  9.5 11.4 %collective-permute-start.7 = (bf16[32,16,128]{2,1,0:T(8,128)(2,1)S(1)}, bf16[32,16,128]{2,1,0:T(8,128)(2,1)S(1)}, u32[]{:S(2)}, u32[]{:S(2)}) collective-permute-start(bf16[32,16,128]{2,1,0:T(8,128)(2,1)S(1)} %shard_map.129), channel_id=1, source_target_pairs={{0,24},{1,25},{2,26},{3,27},{4,28},{5,29},{6,30},{7,31},{8,16},{9,... | collective-permute-start | bytes 393224 | tf_op jit(solution)/shard_map/ppermute | solution.py:600
  13.3 11.1 %collective-permute-start.6 = (bf16[32,16,128]{2,1,0:T(8,128)(2,1)S(1)}, bf16[32,16,128]{2,1,0:T(8,128)(2,1)S(1)}, u32[]{:S(2)}, u32[]{:S(2)}) collective-permute-start(bf16[32,16,128]{2,1,0:T(8,128)(2,1)S(1)} %shard_map.129), channel_id=1, source_target_pairs={{0,16},{1,17},{2,18},{3,19},{4,20},{5,21},{6,22},{7,23},{8,24},{9,... | collective-permute-start | bytes 393224 | tf_op jit(solution)/shard_map/ppermute | solution.py:600
  17.4 10.6 %collective-permute-start.5 = (bf16[4,17,16,128]{3,2,1,0:T(8,128)(2,1)S(1)}, bf16[4,17,16,128]{3,2,1,0:T(8,128)(2,1)S(1)}, u32[]{:S(2)}, u32[]{:S(2)}) collective-permute-start(bf16[4,17,16,128]{3,2,1,0:T(8,128)(2,1)S(1)} %pad_maximum_fusion.1.refs_0_), channel_id=1, source_target_pairs={{0,6},{1,7},{2,4},{3,5},{4,2},{5,3},{6,0},{7,1},{8,14},{9,15},{10,... | collective-permute-start | bytes 835592 | tf_op jit(solution)/shard_map/ppermute | solution.py:600
  19.9 11.8 %collective-permute-start.4 = (bf16[4,17,16,128]{3,2,1,0:T(8,128)(2,1)S(1)}, bf16[4,17,16,128]{3,2,1,0:T(8,128)(2,1)S(1)}, u32[]{:S(2)}, u32[]{:S(2)}) collective-permute-start(bf16[4,17,16,128]{3,2,1,0:T(8,128)(2,1)S(1)} %pad_maximum_fusion.1.refs_0_), channel_id=1, source_target_pairs={{0,4},{1,5},{2,6},{3,7},{4,0},{5,1},{6,2},{7,3},{8,12},{9,13},{10,... | collective-permute-start | bytes 835592 | tf_op jit(solution)/shard_map/ppermute | solution.py:600
  20.5 11.3 %collective-permute-start.3 = (bf16[4,17,16,128]{3,2,1,0:T(8,128)(2,1)S(1)}, bf16[4,17,16,128]{3,2,1,0:T(8,128)(2,1)S(1)}, u32[]{:S(2)}, u32[]{:S(2)}) collective-permute-start(bf16[4,17,16,128]{3,2,1,0:T(8,128)(2,1)S(1)} %pad_maximum_fusion.1.refs_0_), channel_id=1, source_target_pairs={{0,2},{1,3},{2,0},{3,1},{4,6},{5,7},{6,4},{7,5},{8,10},{9,11},{10,... | collective-permute-start | bytes 835592 | tf_op jit(solution)/shard_map/ppermute | solution.py:600
  24.4 7.8 %collective-permute-start.8 = (bf16[32,16,128]{2,1,0:T(8,128)(2,1)S(1)}, bf16[32,16,128]{2,1,0:T(8,128)(2,1)S(1)}, u32[]{:S(2)}, u32[]{:S(2)}) collective-permute-start(bf16[32,16,128]{2,1,0:T(8,128)(2,1)S(1)} %shard_map.129), channel_id=1, source_target_pairs={{0,8},{1,9},{2,10},{3,11},{4,12},{5,13},{6,14},{7,15},{8,0},{9,1},... | collective-permute-start | bytes 393224 | tf_op jit(solution)/shard_map/ppermute | solution.py:600
  31.7 4.1 %collective-permute-start.12 = (bf16[4,17,16,128]{3,2,1,0:T(8,128)(2,1)S(1)}, bf16[4,17,16,128]{3,2,1,0:T(8,128)(2,1)S(1)}, u32[]{:S(2)}, u32[]{:S(2)}) collective-permute-start(bf16[4,17,16,128]{3,2,1,0:T(8,128)(2,1)S(1)} %pad_maximum_fusion.1.refs_0_), channel_id=1, source_target_pairs={{0,1},{1,0},{2,3},{3,2},{4,5},{5,4},{6,7},{7,6},{8,9},{9,8},{10,11... | collective-permute-start | bytes 835592 | tf_op jit(solution)/shard_map/ppermute | solution.py:600
  31.7 4.1 %collective-permute-start.13 = (bf16[4,17,16,128]{3,2,1,0:T(8,128)(2,1)S(1)}, bf16[4,17,16,128]{3,2,1,0:T(8,128)(2,1)S(1)}, u32[]{:S(2)}, u32[]{:S(2)}) collective-permute-start(bf16[4,17,16,128]{3,2,1,0:T(8,128)(2,1)S(1)} %collective-permute-done.3.refs_1_), channel_id=1, source_target_pairs={{0,1},{1,0},{2,3},{3,2},{4,5},{5,4},{6,7},{7,6},{8,9},{9,8},{10,11... | collective-permute-start | bytes 835592 | tf_op jit(solution)/shard_map/ppermute | solution.py:600
  32.3 21.5 %collective-permute-start.11 = (bf16[4,32,16,128]{3,2,1,0:T(8,128)(2,1)S(1)}, bf16[4,32,16,128]{3,2,1,0:T(8,128)(2,1)S(1)}, u32[]{:S(2)}, u32[]{:S(2)}) collective-permute-start(bf16[4,32,16,128]{3,2,1,0:T(8,128)(2,1)S(1)} %pad_maximum_fusion.refs_0_), channel_id=1, source_target_pairs={{0,6},{1,7},{2,4},{3,5},{4,2},{5,3},{6,0},{7,1},{8,14},{9,15},{10,... | collective-permute-start | bytes 1572872 | tf_op jit(solution)/shard_map/ppermute | solution.py:600
  34.7 23.6 %collective-permute-start.10 = (bf16[4,32,16,128]{3,2,1,0:T(8,128)(2,1)S(1)}, bf16[4,32,16,128]{3,2,1,0:T(8,128)(2,1)S(1)}, u32[]{:S(2)}, u32[]{:S(2)}) collective-permute-start(bf16[4,32,16,128]{3,2,1,0:T(8,128)(2,1)S(1)} %pad_maximum_fusion.refs_0_), channel_id=1, source_target_pairs={{0,4},{1,5},{2,6},{3,7},{4,0},{5,1},{6,2},{7,3},{8,12},{9,13},{10,... | collective-permute-start | bytes 1572872 | tf_op jit(solution)/shard_map/ppermute | solution.py:600
  35.3 23.1 %collective-permute-start.9 = (bf16[4,32,16,128]{3,2,1,0:T(8,128)(2,1)S(1)}, bf16[4,32,16,128]{3,2,1,0:T(8,128)(2,1)S(1)}, u32[]{:S(2)}, u32[]{:S(2)}) collective-permute-start(bf16[4,32,16,128]{3,2,1,0:T(8,128)(2,1)S(1)} %pad_maximum_fusion.refs_0_), channel_id=1, source_target_pairs={{0,2},{1,3},{2,0},{3,1},{4,6},{5,7},{6,4},{7,5},{8,10},{9,11},{10,... | collective-permute-start | bytes 1572872 | tf_op jit(solution)/shard_map/ppermute | solution.py:600
  58.4 2.7 %collective-permute-start.17 = (bf16[4,32,16,128]{3,2,1,0:T(8,128)(2,1)S(1)}, bf16[4,32,16,128]{3,2,1,0:T(8,128)(2,1)S(1)}, u32[]{:S(2)}, u32[]{:S(2)}) collective-permute-start(bf16[4,32,16,128]{3,2,1,0:T(8,128)(2,1)S(1)} %collective-permute-done.9.refs_1_), channel_id=1, source_target_pairs={{0,1},{1,0},{2,3},{3,2},{4,5},{5,4},{6,7},{7,6},{8,9},{9,8},{10,11... | collective-permute-start | bytes 1572872 | tf_op jit(solution)/shard_map/ppermute | solution.py:600
  58.9 2.9 %collective-permute-start.18 = (bf16[4,32,16,128]{3,2,1,0:T(8,128)(2,1)S(1)}, bf16[4,32,16,128]{3,2,1,0:T(8,128)(2,1)S(1)}, u32[]{:S(2)}, u32[]{:S(2)}) collective-permute-start(bf16[4,32,16,128]{3,2,1,0:T(8,128)(2,1)S(1)} %collective-permute-done.10.refs_2_), channel_id=1, source_target_pairs={{0,1},{1,0},{2,3},{3,2},{4,5},{5,4},{6,7},{7,6},{8,9},{9,8},{10,11... | collective-permute-start | bytes 1572872 | tf_op jit(solution)/shard_map/ppermute | solution.py:600
  58.9 3.6 %collective-permute-start.19 = (bf16[4,32,16,128]{3,2,1,0:T(8,128)(2,1)S(1)}, bf16[4,32,16,128]{3,2,1,0:T(8,128)(2,1)S(1)}, u32[]{:S(2)}, u32[]{:S(2)}) collective-permute-start(bf16[4,32,16,128]{3,2,1,0:T(8,128)(2,1)S(1)} %collective-permute-done.11.refs_3_), channel_id=1, source_target_pairs={{0,1},{1,0},{2,3},{3,2},{4,5},{5,4},{6,7},{7,6},{8,9},{9,8},{10,11... | collective-permute-start | bytes 1572872 | tf_op jit(solution)/shard_map/ppermute | solution.py:600
  82.6 5.1 %collective-permute-start.20 = (bf16[16,33,16,128]{3,2,1,0:T(8,128)(2,1)S(1)}, bf16[16,33,16,128]{3,2,1,0:T(8,128)(2,1)S(1)}, u32[]{:S(2)}, u32[]{:S(2)}) collective-permute-start(bf16[16,33,16,128]{3,2,1,0:T(8,128)(2,1)S(1)} %get-tuple-element.126), channel_id=1, source_target_pairs={{0,1},{1,0},{2,3},{3,2},{4,5},{5,4},{6,7},{7,6},{8,9},{9,8},{10,11... | collective-permute-start | bytes 6488072 | tf_op jit(solution)/shard_map/ppermute | solution.py:600
  82.7 4.9 %collective-permute-start.21 = (f32[4,16,16,128]{3,2,1,0:T(8,128)S(1)}, f32[4,16,16,128]{3,2,1,0:T(8,128)S(1)}, u32[]{:S(2)}, u32[]{:S(2)}) collective-permute-start(f32[4,16,16,128]{3,2,1,0:T(8,128)S(1)} %get-tuple-element.127), channel_id=1, source_target_pairs={{0,1},{1,0},{2,3},{3,2},{4,5},{5,4},{6,7},{7,6},{8,9},{9,8},{10,11... | collective-permute-start | bytes 1572872 | tf_op jit(solution)/shard_map/ppermute | solution.py:600
  88.7 30.2 %collective-permute-start.23 = (bf16[148,16,128]{2,1,0:T(8,128)(2,1)S(1)}, bf16[148,16,128]{2,1,0:T(8,128)(2,1)S(1)}, u32[]{:S(2)}, u32[]{:S(2)}) collective-permute-start(bf16[148,16,128]{2,1,0:T(8,128)(2,1)S(1)} %get-tuple-element.151), channel_id=1, source_target_pairs={{0,2},{1,3},{2,0},{3,1},{4,6},{5,7},{6,4},{7,5},{8,10},{9,11},{10,... | collective-permute-start | bytes 1818632 | tf_op jit(solution)/shard_map/ppermute | solution.py:600
  90.1 28.7 %collective-permute-start.24 = (bf16[148,16,128]{2,1,0:T(8,128)(2,1)S(1)}, bf16[148,16,128]{2,1,0:T(8,128)(2,1)S(1)}, u32[]{:S(2)}, u32[]{:S(2)}) collective-permute-start(bf16[148,16,128]{2,1,0:T(8,128)(2,1)S(1)} %get-tuple-element.152), channel_id=1, source_target_pairs={{0,4},{1,5},{2,6},{3,7},{4,0},{5,1},{6,2},{7,3},{8,12},{9,13},{10,... | collective-permute-start | bytes 1818632 | tf_op jit(solution)/shard_map/ppermute | solution.py:600
  91.6 27.3 %collective-permute-start.25 = (bf16[148,16,128]{2,1,0:T(8,128)(2,1)S(1)}, bf16[148,16,128]{2,1,0:T(8,128)(2,1)S(1)}, u32[]{:S(2)}, u32[]{:S(2)}) collective-permute-start(bf16[148,16,128]{2,1,0:T(8,128)(2,1)S(1)} %get-tuple-element.153), channel_id=1, source_target_pairs={{0,6},{1,7},{2,4},{3,5},{4,2},{5,3},{6,0},{7,1},{8,14},{9,15},{10,... | collective-permute-start | bytes 1818632 | tf_op jit(solution)/shard_map/ppermute | solution.py:600
  115.6 3.5 %collective-permute-start.22 = (f32[3080,128]{1,0:T(8,128)S(1)}, f32[3080,128]{1,0:T(8,128)S(1)}, u32[]{:S(2)}, u32[]{:S(2)}) collective-permute-start(f32[3080,128]{1,0:T(8,128)S(1)} %get-tuple-element.145), channel_id=1, source_target_pairs={{0,1},{1,0},{2,3},{3,2},{4,5},{5,4},{6,7},{7,6},{8,9},{9,8},{10,11... | collective-permute-start | bytes 4730888 | tf_op jit(solution)/shard_map/ppermute | solution.py:600
  119.8 7.2 %collective-permute-start.29 = (bf16[49,16,128]{2,1,0:T(8,128)(2,1)S(1)}, bf16[49,16,128]{2,1,0:T(8,128)(2,1)S(1)}, u32[]{:S(2)}, u32[]{:S(2)}) collective-permute-start(bf16[49,16,128]{2,1,0:T(8,128)(2,1)S(1)} %get-tuple-element.174), channel_id=1, source_target_pairs={{0,2},{1,3},{2,0},{3,1},{4,6},{5,7},{6,4},{7,5},{8,10},{9,11},{10,... | collective-permute-start | bytes 602120 | tf_op jit(solution)/shard_map/ppermute | solution.py:600
  121.3 7.9 %collective-permute-start.30 = (bf16[49,16,128]{2,1,0:T(8,128)(2,1)S(1)}, bf16[49,16,128]{2,1,0:T(8,128)(2,1)S(1)}, u32[]{:S(2)}, u32[]{:S(2)}) collective-permute-start(bf16[49,16,128]{2,1,0:T(8,128)(2,1)S(1)} %get-tuple-element.175), channel_id=1, source_target_pairs={{0,4},{1,5},{2,6},{3,7},{4,0},{5,1},{6,2},{7,3},{8,12},{9,13},{10,... | collective-permute-start | bytes 602120 | tf_op jit(solution)/shard_map/ppermute | solution.py:600
  122.8 9.8 %collective-permute-start.31 = (bf16[49,16,128]{2,1,0:T(8,128)(2,1)S(1)}, bf16[49,16,128]{2,1,0:T(8,128)(2,1)S(1)}, u32[]{:S(2)}, u32[]{:S(2)}) collective-permute-start(bf16[49,16,128]{2,1,0:T(8,128)(2,1)S(1)} %get-tuple-element.176), channel_id=1, source_target_pairs={{0,6},{1,7},{2,4},{3,5},{4,2},{5,3},{6,0},{7,1},{8,14},{9,15},{10,... | collective-permute-start | bytes 602120 | tf_op jit(solution)/shard_map/ppermute | solution.py:600
  124.2 11.7 %collective-permute-start.26 = (bf16[33,16,128]{2,1,0:T(8,128)(2,1)S(1)}, bf16[33,16,128]{2,1,0:T(8,128)(2,1)S(1)}, u32[]{:S(2)}, u32[]{:S(2)}) collective-permute-start(bf16[33,16,128]{2,1,0:T(8,128)(2,1)S(1)} %get-tuple-element.170), channel_id=1, source_target_pairs={{0,8},{1,9},{2,10},{3,11},{4,12},{5,13},{6,14},{7,15},{8,0},{9,1},... | collective-permute-start | bytes 405512 | tf_op jit(solution)/shard_map/ppermute | solution.py:600
  125.0 12.7 %collective-permute-start.27 = (bf16[33,16,128]{2,1,0:T(8,128)(2,1)S(1)}, bf16[33,16,128]{2,1,0:T(8,128)(2,1)S(1)}, u32[]{:S(2)}, u32[]{:S(2)}) collective-permute-start(bf16[33,16,128]{2,1,0:T(8,128)(2,1)S(1)} %get-tuple-element.171), channel_id=1, source_target_pairs={{0,16},{1,17},{2,18},{3,19},{4,20},{5,21},{6,22},{7,23},{8,24},{9,... | collective-permute-start | bytes 405512 | tf_op jit(solution)/shard_map/ppermute | solution.py:600
  127.0 10.7 %collective-permute-start.28 = (bf16[33,16,128]{2,1,0:T(8,128)(2,1)S(1)}, bf16[33,16,128]{2,1,0:T(8,128)(2,1)S(1)}, u32[]{:S(2)}, u32[]{:S(2)}) collective-permute-start(bf16[33,16,128]{2,1,0:T(8,128)(2,1)S(1)} %get-tuple-element.172), channel_id=1, source_target_pairs={{0,24},{1,25},{2,26},{3,27},{4,28},{5,29},{6,30},{7,31},{8,16},{9,... | collective-permute-start | bytes 405512 | tf_op jit(solution)/shard_map/ppermute | solution.py:600
  133.2 5.3 %collective-permute-start.32 = (bf16[17,16,128]{2,1,0:T(8,128)(2,1)S(1)}, bf16[17,16,128]{2,1,0:T(8,128)(2,1)S(1)}, u32[]{:S(2)}, u32[]{:S(2)}) collective-permute-start(bf16[17,16,128]{2,1,0:T(8,128)(2,1)S(1)} %get-tuple-element.183), channel_id=1, source_target_pairs={{0,8},{1,9},{2,10},{3,11},{4,12},{5,13},{6,14},{7,15},{8,0},{9,1},... | collective-permute-start | bytes 208904 | tf_op jit(solution)/shard_map/ppermute | solution.py:600
  133.9 10.8 %collective-permute-start.33 = (bf16[17,16,128]{2,1,0:T(8,128)(2,1)S(1)}, bf16[17,16,128]{2,1,0:T(8,128)(2,1)S(1)}, u32[]{:S(2)}, u32[]{:S(2)}) collective-permute-start(bf16[17,16,128]{2,1,0:T(8,128)(2,1)S(1)} %get-tuple-element.184), channel_id=1, source_target_pairs={{0,16},{1,17},{2,18},{3,19},{4,20},{5,21},{6,22},{7,23},{8,24},{9,... | collective-permute-start | bytes 208904 | tf_op jit(solution)/shard_map/ppermute | solution.py:600
  136.0 8.8 %collective-permute-start.34 = (bf16[17,16,128]{2,1,0:T(8,128)(2,1)S(1)}, bf16[17,16,128]{2,1,0:T(8,128)(2,1)S(1)}, u32[]{:S(2)}, u32[]{:S(2)}) collective-permute-start(bf16[17,16,128]{2,1,0:T(8,128)(2,1)S(1)} %get-tuple-element.185), channel_id=1, source_target_pairs={{0,24},{1,25},{2,26},{3,27},{4,28},{5,29},{6,30},{7,31},{8,16},{9,... | collective-permute-start | bytes 208904 | tf_op jit(solution)/shard_map/ppermute | solution.py:600
  (13 other events, 79.5 us)

commit v2 on v1

--- a/solution.py
+++ b/solution.py
@@ -217,11 +217,23 @@
         task()
 
 
-def feed_body(place, gates, tok, cot, ctx, ctx_t, w_in, bias, *refs):
+def branch_body(gates, tok, cot, ctx, w, bias, branch, low, low_t, gs):
+    wo = square(w, 3)
+    for r in range(4):
+        at = slice(256 * r, 256 * r + 256)
+        out = nn(ctx[at, :], wo) + bias[0:1, 2 * D : 3 * D]
+        branch[at, :] = out
+        low[at, :] = (tok[at, :].astype(F32) + gates[0] * out).astype(BF)
+        gs[at, :] = (gates[1] * cot[at, :].astype(F32)).astype(BF)
+    low_t[:D] = low[...].T
+    low_t[D:] = jnp.ones((16, ROWS), BF)
+
+
+def feed_body(place, gates, tok, cot, branch, low_all, low_t, gs_all, ctx_t, w_in, bias, *refs):
     pieces, refs = refs[:8], refs[8:]
     (layer_out, gm, gctx, keep_out, send_out, wo_keep, wo_send) = refs[:7]
-    (w, low_t, gbr, gs_all, active_t, gh_all, v0, v1, b0, b1, active, second, gmid, sums) = refs[7:21]
-    (layer, keep, send, sems) = refs[21:]
+    (w, gbr, active_t, gh_all, v0, v1, b0, b1, active, second, gmid, sums) = refs[7:19]
+    (layer, keep, send, sems) = refs[19:]
     values, backs = (v0, v1), (b0, b1)
     wo = w_in.at[24:32]
     assemble(pieces, w, place[0])
@@ -232,9 +244,7 @@
     ga, gf = gates[0], gates[1]
     c1 = 0.7978845608028654
     c2 = 0.044715
-    ones = jnp.ones((16, ROWS), BF)
-    low_t[D:] = ones
-    active_t[FF:] = ones
+    active_t[FF:] = jnp.ones((16, ROWS), BF)
 
     def w_up(j):
         return columns(w, slice(0, 16), slice(8 * j, 8 * j + 8), 2)
@@ -245,13 +255,7 @@
     def rows(r, carry):
         attend_sum, feed_sum = carry
         at = rows_of(r)
-        br = nn(ctx[at, :], square(wo, 0)) + bias[0:1, 2 * D : 3 * D]
-        middle = tok[at, :].astype(F32) + ga * br
-        low = middle.astype(BF)
-        low_t[:D, at] = low.T
-        ct = cot[at, :].astype(F32)
-        gs = (gf * ct).astype(BF)
-        gs_all[at, :] = gs
+        low, gs = low_all[at, :], gs_all[at, :]
 
         def first(j):
             up, down = w_up(j), w_down(j)
@@ -301,12 +305,12 @@
         for j in range(5):
             mix(bend(j) if j < 4 else [], (first(j + 1) if j < 3 else []) + (then(j - 1) if j else []))
         out = second[...] + bias[0:1, 3 * D : 4 * D]
-        layer[at, :] = (middle + gf * out).astype(BF)
+        br, ct = branch[at, :], cot[at, :].astype(F32)
+        layer[at, :] = (tok[at, :].astype(F32) + ga * br + gf * out).astype(BF)
         grad = ct + gmid[...]
         gm[at, :] = grad
         gb = (ga * grad).astype(BF)
         gbr[at, :] = gb
-        gctx[at, :] = nt(gb, square(wo, 0)).astype(BF)
         pltpu.make_async_copy(layer.at[at], layer_out.at[at], sems.at[0]).start()
         attend_sum = attend_sum + jnp.sum(br * grad, axis=0, keepdims=True)
         feed_sum = feed_sum + jnp.sum(out * ct, axis=0, keepdims=True)
@@ -330,24 +334,45 @@
             copy.start()
         return copies
 
-    for j in range(4):
-        val = nn(low_t[...], gh_all[:, 512 * j : 512 * j + 512])
+    def up_grad(j):
+        return nn(low_t[...], gh_all[:, 512 * j : 512 * j + 512])
+
+    def up_store(j, val):
         sums[0:1, 4 * D + 512 * j : 4 * D + 512 * j + 512] = val[D : D + 1]
         for o in range(0, 16, 2):
             for jj in range(4):
                 for i in range(2):
                     top, col = 32 * o + 16 * i, slice(128 * jj, 128 * jj + 128)
                     store(o, 2 * (4 * j + jj) + i, val[top : top + 16, col], val[top + 32 : top + 48, col])
-    val = nn(ctx_t[...], gbr[...])
-    sums[0:1, 2 * D : 3 * D] = val[D : D + 1]
-    for o in range(0, 8, 2):
-        for j in range(4):
-            for i in range(4):
-                top, col = 64 * o + 16 * i, slice(128 * j, 128 * j + 128)
-                even, other = val[top : top + 16, col], val[top + 64 : top + 80, col]
-                wo_keep[o // 2, 4 * j + i] = jnp.where(odd, other, even)
-                wo_send[o // 2, 4 * j + i] = jnp.where(odd, even, other)
-    copies = []
+
+    def down_grad(j):
+        return nn(active_t[512 * j : 512 * j + (528 if j == 3 else 512)], gs_all[...])
+
+    def down_store(j, val):
+        if j == 3:
+            sums[0:1, 3 * D : 4 * D] = val[D : D + 1]
+        for o in (0, 2):
+            for jj in range(4):
+                for i in range(8):
+                    top, col = 128 * o + 16 * i, slice(128 * jj, 128 * jj + 128)
+                    store(16 + 4 * j + o, 8 * jj + i, val[top : top + 16, col], val[top + 128 : top + 144, col])
+
+    def out_grad(_):
+        return nn(ctx_t[...], gbr[...])
+
+    def out_store(_, val):
+        sums[0:1, 2 * D : 3 * D] = val[D : D + 1]
+        for o in range(0, 8, 2):
+            for j in range(4):
+                for i in range(4):
+                    top, col = 64 * o + 16 * i, slice(128 * j, 128 * j + 128)
+                    even, other = val[top : top + 16, col], val[top + 64 : top + 80, col]
+                    wo_keep[o // 2, 4 * j + i] = jnp.where(odd, other, even)
+                    wo_send[o // 2, 4 * j + i] = jnp.where(odd, even, other)
+
+    for r in range(4):
+        at = slice(256 * r, 256 * r + 256)
+        gctx[at, :] = nt(gbr[at, :], square(wo, 0)).astype(BF)
     lane = lax.broadcasted_iota(jnp.int32, (1, 128), 1)
     gate = jnp.where(lane == 2 * place[2], jnp.sum(attend_sum), 0.0)
     gate = jnp.where(lane == 2 * place[2] + 1, jnp.sum(feed_sum), gate)
@@ -364,20 +389,22 @@
         other = jnp.where(row == 0, sums[0:1, 128 * o + 128 : 128 * o + 256], base)
         store(o, G_TILES - 1, even, other)
 
-    for j in (3, 2, 1, 0):
-        val = nn(active_t[512 * j : 512 * j + (528 if j == 3 else 512)], gs_all[...])
-        if j == 3:
-            sums[0:1, 3 * D : 4 * D] = val[D : D + 1]
-            for o in range(0, 16, 2):
+    copies, before = [], None
+    blocks = [(up_grad, up_store, j) for j in range(4)] + [(out_grad, out_store, 0)]
+    blocks += [(down_grad, down_store, j) for j in (3, 2, 1, 0)]
+    for index, (product, put, j) in enumerate(blocks):
+        val = product(j)
+        if before:
+            before[0](before[1], before[2])
+        before = (put, j, val)
+        if index == 6:
+            for o in range(0, PARTS, 2):
                 tail(o)
             copies += post(pl.ds(0, 8), 5)
-        for o in (0, 2):
-            tail(16 + 4 * j + o)
-            for jj in range(4):
-                for i in range(8):
-                    top, col = 128 * o + 16 * i, slice(128 * jj, 128 * jj + 128)
-                    store(16 + 4 * j + o, 8 * jj + i, val[top : top + 16, col], val[top + 128 : top + 144, col])
-        copies += post(pl.ds(8 + 2 * j, 2), 7 + 2 * j)
+        if index == 8:
+            copies += post(pl.ds(12, 4), 7)
+    down_store(0, val)
+    copies += post(pl.ds(8, 4), 9)
     pltpu.make_async_copy(layer, layer_out, sems.at[0]).wait()
     for copy in copies:
         copy.wait()
@@ -660,39 +687,44 @@
         out[i] = ref[i]
 
 
-def finish_body(place, keep_f, f1, f2, f3, keep_a, a1, a2, a3, att, ff, bias, gate):
-    def added(keep, gots, at):
-        total = keep[at]
-        for g in gots:
-            total = total + g[at].astype(F32)
-        return total
-
-    def added_tail(keep, gots, at):
-        total = keep[at]
-        for g in gots:
-            total = total + join_row(g[at].astype(F32))
-        return total
-
-    for j in range(4):
-        for i in range(4):
-            att[pl.ds(64 * i + j, 16, stride=4), :] = added(keep_a, (a1, a2, a3), 4 * j + i)
+def added(keep, gots, at):
+    total = keep[at]
+    for g in gots:
+        total = total + g[at].astype(F32)
+    return total
+
+
+def added_tail(keep, gots, at):
+    total = keep[at]
+    for g in gots:
+        total = total + join_row(g[at].astype(F32))
+    return total
+
+
+def finish_feed_body(place, keep, f1, f2, f3, ff, tail):
     gots = (f1, f2, f3)
 
     @pl.when(place[0] < PARTS // 2)
     def _():
         for j in range(16):
             for i in range(2):
-                ff[pl.ds(256 * i + j, 16, stride=16), :] = added(keep_f, gots, 2 * j + i)
+                ff[pl.ds(256 * i + j, 16, stride=16), :] = added(keep, gots, 2 * j + i)
 
     @pl.when(place[0] >= PARTS // 2)
     def _():
         for j in range(4):
             for i in range(8):
-                ff[pl.ds(64 * i + j, 16, stride=4), :] = added(keep_f, gots, 8 * j + i)
-
-    tail = added_tail(keep_f, gots, F_TILES)
-    own = added_tail(keep_a, (a1, a2, a3), 16)
-    bias[...] = jnp.where(place[0] < 8, own[0:1], tail[0:1])
+                ff[pl.ds(64 * i + j, 16, stride=4), :] = added(keep, gots, 8 * j + i)
+
+    tail[...] = added_tail(keep, gots, F_TILES)
+
+
+def finish_square_body(place, keep, a1, a2, a3, tail, att, bias, gate):
+    gots = (a1, a2, a3)
+    for j in range(4):
+        for i in range(4):
+            att[pl.ds(64 * i + j, 16, stride=4), :] = added(keep, gots, 4 * j + i)
+    bias[...] = jnp.where(place[0] < 8, added_tail(keep, gots, 16)[0:1], tail[0:1])
     gates = tail[1:2] + tail[2:3] + tail[3:4]
     lane = lax.broadcasted_iota(jnp.int32, (1, 128), 1)
     for g in range(2):
@@ -719,11 +751,16 @@
 def local(direct, tokens, cotangent, attention, feedforward, biases, gates, counts, lengths):
     me = lax.axis_index(AXES)
     n = PARTS
-    *masks, x_t = call(
-        prepare_body,
-        [((2, ROWS, 128), BF), ((2, ROWS, 128), BF), ((D + 16, ROWS), BF)],
-        [SMEM, SMEM, VMEM], [], 1 << 20, 3 << 20, 16,
-    )(counts, lengths, tokens)
+    row = (ROWS, D)
+
+    def prepare(counts):
+        *masks, x_t = call(
+            prepare_body,
+            [((2, ROWS, 128), BF), ((2, ROWS, 128), BF), ((D + 16, ROWS), BF)],
+            [SMEM, SMEM, VMEM], [], 1000, 1000, 16,
+        )(counts, lengths, tokens)
+        return masks, x_t
+
     if direct:
         place = jnp.stack([me, me % 2, me, (me // 2) % 4, me // 8]).astype(jnp.int32)
         (own_a,) = small(
@@ -732,16 +769,19 @@
         (own_f,) = small(
             pack_feed_body, [((F_TILES, 16, 128), BF)], (place, feedforward.reshape(-1, 128)), [((512, 128), F32)]
         )
-        stack_a, masks = lax.optimization_barrier((along_z(own_a, n), masks))
+        stack_a = along_z(own_a, n)
         far = [swap(own_f, n, 16), swap(own_f, n, 24)]
         chips_a = along_xy(stack_a, n)
-        far, own_f, place = lax.optimization_barrier((far, own_f, place))
         near = swap(own_f, n, 8)
+        far, near, place, counts = lax.optimization_barrier((far, near, place, counts))
+        masks, x_t = prepare(counts)
         (place,) = call(copy_body, [((5,), jnp.int32, SMEM)], [SMEM], [], 8 << 30, 1000, 16)(place)
-        chips_a, place = lax.optimization_barrier((chips_a, place))
+        stack_f = jnp.stack([own_f, near] + far)
+        chips_a, stack_f, place, masks = lax.optimization_barrier((chips_a, stack_f, place, masks))
         ga_all = across(chips_a, n)
-        chips_f = along_xy(jnp.stack([own_f, near] + far), n)
+        chips_f = along_xy(stack_f, n)
     else:
+        masks, x_t = prepare(counts)
         ga_all, gf_all = pieces_any(attention, feedforward, biases)
         place = jnp.zeros((5,), jnp.int32)
     row = (ROWS, D)
@@ -757,21 +797,27 @@
         [((128, ROWS), BF), ((128, ROWS), F32)] + [((ROWS, 256), F32)] * 2 + [((ROWS, 256), BF)] * 2,
         1000, 1000, 20,
     )(q, k, v)
+    branch, low, low_t, gs = call(
+        branch_body,
+        [(row, F32), (row, BF), ((D + 16, ROWS), BF), (row, BF)],
+        [SMEM] + [VMEM] * 5, [], 1000, 1000, 20,
+    )(gates, tokens, cotangent, ctx, w, bias)
     if direct:
-        chips_f, ctx = lax.optimization_barrier((chips_f, ctx))
-        gf_all = across(chips_f, n)
+        other = swap(tie(chips_f[0], ctx), n, 1)
+        chips_f, other, branch = lax.optimization_barrier((chips_f, other, branch))
+        gf_all = chips_f + [other] + [swap(part, n, 1) for part in chips_f[1:]]
     layer, gm, gctx, ff_keep, ff_send, wo_keep, wo_send = call(
         feed_body,
         [(row, BF, ANY), (row, F32), (row, BF)]
         + [((n // 2, G_TILES, 16, 128), F32, ANY), ((n // 2, G_TILES, 16, 128), BF, ANY)]
         + [((4, 16, 16, 128), F32)] * 2,
-        [SMEM, SMEM] + [VMEM] * 14,
-        [((PARTS, F_TILES, 16, 128), BF), ((D + 16, ROWS), BF), (row, BF), (row, BF),
+        [SMEM, SMEM] + [VMEM] * 17,
+        [((PARTS, F_TILES, 16, 128), BF), (row, BF),
          ((FF + 16, ROWS), BF), ((ROWS, FF), BF)]
         + [((256, D), F32)] * 4 + [((256, FF), BF)] + [((256, D), F32)] * 2 + [((1, 8 * D), F32)]
         + [(row, BF), ((n // 2, G_TILES, 16, 128), F32), ((n // 2, G_TILES, 16, 128), BF), DMA((16,))],
-        16 << 30, 30 << 20, 36,
-    )(place, gates, tokens, cotangent, ctx, ctx_t, w, bias, *gf_all)
+        16 << 30, 30 << 20, 32,
+    )(place, gates, tokens, cotangent, branch, low, low_t, gs, ctx_t, w, bias, *gf_all)
 
     half, whole = (ROWS // 16, ROWS), (128, ROWS)
     buffers = [((2, 128, ROWS), BF)] + [((ROWS, 256), F32)] * 4 + [((ROWS, 256), BF)] * 4
@@ -810,11 +856,15 @@
     if direct:
         parts = small(square_z_body, blocks_of(17), (place, *got, wo), [((4, 17, 16, 128), F32)])
         got = hop(parts, n, 8)
-        att_grad, ff_grad, bias_grad, gate_grad = call(
-            finish_body,
-            [((256, 128), F32), ((512, 128), F32), ((1, 128), F32), ((2,), F32, SMEM)],
-            [SMEM] + [VMEM] * 8, [], 1 << 20, 1 << 20, 16,
-        )(place, *ff_got, *got)
+        ff_grad, tail = call(
+            finish_feed_body, [((512, 128), F32), ((16, 128), F32)], [SMEM] + [VMEM] * 4, [], 1000, 1000, 16,
+        )(place, *ff_got)
+        got, tail = barrier((got, tail))
+        att_grad, bias_grad, gate_grad = call(
+            finish_square_body,
+            [((256, 128), F32), ((1, 128), F32), ((2,), F32, SMEM)],
+            [SMEM] + [VMEM] * 5, [], 1000, 1000, 16,
+        )(place, *got, tail)
         att_grad, ff_grad, bias_grad = att_grad.reshape(-1), ff_grad.reshape(-1), bias_grad.reshape(-1)
         return layer, input_grad, att_grad, ff_grad, bias_grad, gate_grad
 

time: 147 us -> 142 us (0.966)
  waiting for transfers between devices: 31.5 us -> 26.5 us
  local copies, waits for them, and re-layouts: 5.03 us -> 2.51 us
  Pallas kernels: 73.5 us -> 76 us
    ppermute x35, waiting for transfers between devices: 31.5 us -> 26.5 us  [swap(): return lax.ppermute(x, AXES, [(i, i ^ bit) for i in range(n)])]
    pallas_call x2 -> x4, Pallas kernels: 2.96 us -> 5.74 us  [the longest x1 1.62 us: local(): call(branch_body, [(row, F32), (row, BF), ((D + 16, ROWS), BF), (row, BF)...]
    unnamed x20 -> x18, local copies, waits for them, and re-layouts: 4.95 us -> 2.43 us
  transfers between devices with their start and end apart: 35 -> 35, of which waited for: 17 -> 14; matrix products, arithmetic and copies ran while one was open for 0% -> 0% of each run, Pallas kernels for 34% -> 37%
where the time goes in v2:
time: 142 us
  Pallas kernels  76 us (54%)
  starting transfers between devices  36 us (25%)
  waiting for transfers between devices  26.5 us (19%)
  local copies, waits for them, and re-layouts  2.51 us (2%)
    ppermute x35, starting transfers between devices, swap(): return lax.ppermute(x, AXES, [(i, i ^ bit) for i in range(n)])  36 us
    ppermute x35, waiting for transfers between devices, swap(): return lax.ppermute(x, AXES, [(i, i ^ bit) for i in range(n)])  26.5 us
    pallas_call x1, Pallas kernels, local(): call(back_body, [(row, BF)] * 3 + [((4 * SHARE + 8, 128), F32)] * 2, [SME...  23.4 us
    pallas_call x1, Pallas kernels, local(): call(feed_body, [(row, BF, ANY), (row, F32), (row, BF)] + [((n // 2, G_TI...  19.7 us
    pallas_call x1, Pallas kernels, local(): call(attend_body, [(row, BF), ((D + 16, ROWS), BF), ((8, ROWS), F32)], [V...  13.4 us
    pallas_call x6, Pallas kernels, small(): return call(body, outs, ins, scratch, 2 * size, 6 * size, 16)(*args)  3.93 us
    pallas_call x1, Pallas kernels, local(): call(input_body, [(row, F32)], [VMEM] * 5, [], 32 << 30, 1000, 24)  3.15 us
    pallas_call x1, Pallas kernels, local(): call(back_first_body, [(half, F32)] + sums, [VMEM] * 5, buffers, 1000, 10...  3.01 us
  transfers between devices with their start and end apart: 35, of which 14 were waited for; matrix products, arithmetic and copies ran while one was open for 0% of the time, Pallas kernels for 37%

profile of v2, /device:TPU:0, one launch (start us, length us, event | category | flops | bytes accessed | tf_op | source)
XLA Modules:
  0.0 142.2 jit_solution(16586223006821400567)
XLA Ops:
  2.2 5.1 %collective-permute-start.2 = (bf16[17,16,128]{2,1,0:T(8,128)(2,1)S(1)}, bf16[17,16,128]{2,1,0:T(8,128)(2,1)S(1)}, u32[]{:S(2)}, u32[]{:S(2)}) collective-permute-start(bf16[17,16,128]{2,1,0:T(8,128)(2,1)S(1)} %shard_map.127), channel_id=1, source_target_pairs={{0,24},{1,25},{2,26},{3,27},{4,28},{5,29},{6,30},{7,31},{8,16},{9,... | collective-permute-start | bytes 208904 | tf_op jit(solution)/shard_map/ppermute | solution.py:627
  9.5 1.5 %collective-permute-start.8 = (bf16[32,16,128]{2,1,0:T(8,128)(2,1)S(1)}, bf16[32,16,128]{2,1,0:T(8,128)(2,1)S(1)}, u32[]{:S(2)}, u32[]{:S(2)}) collective-permute-start(bf16[32,16,128]{2,1,0:T(8,128)(2,1)S(1)} %shard_map.128), channel_id=1, source_target_pairs={{0,8},{1,9},{2,10},{3,11},{4,12},{5,13},{6,14},{7,15},{8,0},{9,1},... | collective-permute-start | bytes 393224 | tf_op jit(solution)/shard_map/ppermute | solution.py:627
  11.0 2.4 %collective-permute-start.7 = (bf16[32,16,128]{2,1,0:T(8,128)(2,1)S(1)}, bf16[32,16,128]{2,1,0:T(8,128)(2,1)S(1)}, u32[]{:S(2)}, u32[]{:S(2)}) collective-permute-start(bf16[32,16,128]{2,1,0:T(8,128)(2,1)S(1)} %shard_map.128), channel_id=1, source_target_pairs={{0,24},{1,25},{2,26},{3,27},{4,28},{5,29},{6,30},{7,31},{8,16},{9,... | collective-permute-start | bytes 393224 | tf_op jit(solution)/shard_map/ppermute | solution.py:627
  14.0 2.5 %collective-permute-start.5 = (bf16[4,17,16,128]{3,2,1,0:T(8,128)(2,1)S(1)}, bf16[4,17,16,128]{3,2,1,0:T(8,128)(2,1)S(1)}, u32[]{:S(2)}, u32[]{:S(2)}) collective-permute-start(bf16[4,17,16,128]{3,2,1,0:T(8,128)(2,1)S(1)} %pad_maximum_fusion.1.refs_0_), channel_id=1, source_target_pairs={{0,6},{1,7},{2,4},{3,5},{4,2},{5,3},{6,0},{7,1},{8,14},{9,15},{10,... | collective-permute-start | bytes 835592 | tf_op jit(solution)/shard_map/ppermute | solution.py:627
  18.0 2.6 %collective-permute-done.7 = bf16[32,16,128]{2,1,0:T(8,128)(2,1)S(1)} collective-permute-done((bf16[32,16,128]{2,1,0:T(8,128)(2,1)S(1)}, bf16[32,16,128]{2,1,0:T(8,128)(2,1)S(1)}, u32[]{:S(2)}, u32[]{:S(2)}) %collective-permute-start.7) | collective-permute-done | bytes 131104 | tf_op jit(solution)/shard_map/ppermute | solution.py:627
  20.6 4.6 %collective-permute-done.6 = bf16[32,16,128]{2,1,0:T(8,128)(2,1)S(1)} collective-permute-done((bf16[32,16,128]{2,1,0:T(8,128)(2,1)S(1)}, bf16[32,16,128]{2,1,0:T(8,128)(2,1)S(1)}, u32[]{:S(2)}, u32[]{:S(2)}) %collective-permute-start.6) | collective-permute-done | bytes 131104 | tf_op jit(solution)/shard_map/ppermute | solution.py:627
  25.2 1.1 shard_map.129.place
  26.4 1.5 %shard_map.130 = (bf16[2,1024,128]{2,1,0:T(8,128)(2,1)S(1)}, bf16[2,1024,128]{2,1,0:T(8,128)(2,1)S(1)}, bf16[528,1024]{1,0:T(8,128)(2,1)S(1)}) custom-call(s32[1,3]{1,0:T(1,128)S(1)} %copy-done.5, s32[1,8]{1,0:T(1,128)S(1)} %copy-done.6, bf16[1024,512]{1,0:T(8,128)(2,1)S(1)} %copy-done), custom_call_target="tpu_custom_call" | custom-call | flops 1000 | bytes 1000 | tf_op jit(solution)/shard_map/pallas_call | solution.py:757
  29.7 2.3 %collective-permute-start.11 = (bf16[4,32,16,128]{3,2,1,0:T(8,128)(2,1)S(1)}, bf16[4,32,16,128]{3,2,1,0:T(8,128)(2,1)S(1)}, u32[]{:S(2)}, u32[]{:S(2)}) collective-permute-start(bf16[4,32,16,128]{3,2,1,0:T(8,128)(2,1)S(1)} %pad_maximum_fusion.refs_0_), channel_id=1, source_target_pairs={{0,6},{1,7},{2,4},{3,5},{4,2},{5,3},{6,0},{7,1},{8,14},{9,15},{10,... | collective-permute-start | bytes 1572872 | tf_op jit(solution)/shard_map/ppermute | solution.py:627
  33.2 2.6 %shard_map.131 = (bf16[8,1024,128]{2,1,0:T(8,128)(2,1)S(1)}, bf16[8,1024,128]{2,1,0:T(8,128)(2,1)S(1)}, bf16[1024,512]{1,0:T(8,128)(2,1)S(1)}, bf16[32,17,16,128]{3,2,1,0:T(8,128)(2,1)S(1)}, f32[1,4096]{1,0:T(1,128)S(1)}) custom-call(s32[5]{0:T(128)S(1)} %shard_map.129.place, bf16[1024,512]{1,0:T(8,128)(2,1)S(1)} %copy-done, ...), custom_call_target="tpu_custom_call" | custom-call | flops 1000 | bytes 1000 | tf_op jit(solution)/shard_map/pallas_call | solution.py:788
  35.8 13.4 %shard_map.132 = (bf16[1024,512]{1,0:T(8,128)(2,1)S(1)}, bf16[528,1024]{1,0:T(8,128)(2,1)S(1)}, f32[8,1024]{1,0:T(8,128)S(1)}) custom-call(bf16[8,1024,128]{2,1,0:T(8,128)(2,1)S(1)} %get-tuple-element.160.q_all, bf16[8,1024,128]{2,1,0:T(8,128)(2,1)S(1)} %get-tuple-element.127.k_all, bf16[1024,512]{1,0:T(8,128)(2,1)S(1)} %get-tuple-element.128.v_all), custom_call_target="tpu_custom_call" | custom-call | flops 1000 | bytes 1000 | tf_op jit(solution)/shard_map/pallas_call | solution.py:793
  49.3 1.6 %shard_map.133 = (f32[1024,512]{1,0:T(8,128)S(1)}, bf16[1024,512]{1,0:T(8,128)(2,1)S(1)}, bf16[528,1024]{1,0:T(8,128)(2,1)S(1)}, bf16[1024,512]{1,0:T(8,128)(2,1)S(1)}) custom-call(f32[2]{0:T(128)S(1)} %copy-done.8, bf16[1024,512]{1,0:T(8,128)(2,1)S(1)} %copy-done, bf16[1024,512]{1,0:T(8,128)(2,1)S(1)} %copy-done.2, ...), custom_call_target="tpu_custom_call" | custom-call | flops 1000 | bytes 1000 | tf_op jit(solution)/shard_map/pallas_call | solution.py:800
  50.9 4.7 %collective-permute-done.10.refs_2_ = bf16[4,32,16,128]{3,2,1,0:T(8,128)(2,1)S(1)} collective-permute-done((bf16[4,32,16,128]{3,2,1,0:T(8,128)(2,1)S(1)}, bf16[4,32,16,128]{3,2,1,0:T(8,128)(2,1)S(1)}, u32[]{:S(2)}, u32[]{:S(2)}) %collective-permute-start.10) | collective-permute-done | bytes 524320 | tf_op jit(solution)/shard_map/ppermute | solution.py:627
  56.3 1.3 collective-permute-done.17.refs_5_
  59.1 19.7 %shard_map.134 = (bf16[1024,512]{1,0:T(8,128)(2,1)}, f32[1024,512]{1,0:T(8,128)S(1)}, bf16[1024,512]{1,0:T(8,128)(2,1)S(1)}, f32[16,33,16,128]{3,2,1,0:T(8,128)}...) custom-call(s32[5]{0:T(128)S(1)} %shard_map.129.place, ...), custom_call_target="tpu_custom_call" | custom-call | flops 17179869184 | bytes 31457280 | tf_op jit(solution)/shard_map/pallas_call | solution.py:809
  79.4 3.0 %shard_map.135 = (f32[64,1024]{1,0:T(8,128)S(1)}, f32[1024,128]{1,0:T(8,128)S(1)}, f32[1024,128]{1,0:T(8,128)S(1)}) custom-call(bf16[8,1024,128]{2,1,0:T(8,128)(2,1)S(1)} %get-tuple-element.160.q_all, bf16[8,1024,128]{2,1,0:T(8,128)(2,1)S(1)} %get-tuple-element.127.k_all, bf16[1024,512]{1,0:T(8,128)(2,1)S(1)} %get-tuple-element.128.v_all, ...), custom_call_target="tpu_custom_call" | custom-call | flops 1000 | bytes 1000 | tf_op jit(solution)/shard_map/pallas_call | solution.py:828
  82.4 1.5 %collective-permute-done.21.wo_got = f32[4,16,16,128]{3,2,1,0:T(8,128)S(1)} collective-permute-done((f32[4,16,16,128]{3,2,1,0:T(8,128)S(1)}, f32[4,16,16,128]{3,2,1,0:T(8,128)S(1)}, u32[]{:S(2)}, u32[]{:S(2)}) %collective-permute-start.21) | collective-permute-done | bytes 524320 | tf_op jit(solution)/shard_map/ppermute | solution.py:627
  83.9 1.0 shard_map.136
  84.9 1.5 %collective-permute-start.23 = (bf16[148,16,128]{2,1,0:T(8,128)(2,1)S(1)}, bf16[148,16,128]{2,1,0:T(8,128)(2,1)S(1)}, u32[]{:S(2)}, u32[]{:S(2)}) collective-permute-start(bf16[148,16,128]{2,1,0:T(8,128)(2,1)S(1)} %get-tuple-element.171), channel_id=1, source_target_pairs={{0,2},{1,3},{2,0},{3,1},{4,6},{5,7},{6,4},{7,5},{8,10},{9,11},{10,... | collective-permute-start | bytes 1818632 | tf_op jit(solution)/shard_map/ppermute | solution.py:627
  86.4 1.5 %collective-permute-start.24 = (bf16[148,16,128]{2,1,0:T(8,128)(2,1)S(1)}, bf16[148,16,128]{2,1,0:T(8,128)(2,1)S(1)}, u32[]{:S(2)}, u32[]{:S(2)}) collective-permute-start(bf16[148,16,128]{2,1,0:T(8,128)(2,1)S(1)} %get-tuple-element.172), channel_id=1, source_target_pairs={{0,4},{1,5},{2,6},{3,7},{4,0},{5,1},{6,2},{7,3},{8,12},{9,13},{10,... | collective-permute-start | bytes 1818632 | tf_op jit(solution)/shard_map/ppermute | solution.py:627
  88.5 23.4 %shard_map.137 = (bf16[1024,512]{1,0:T(8,128)(2,1)S(1)}, bf16[1024,512]{1,0:T(8,128)(2,1)S(1)}, bf16[1024,512]{1,0:T(8,128)(2,1)S(1)}, f32[3080,128]{1,0:T(8,128)S(1)}, f32[3080,128]{1,0:T(8,128)S(1)}) custom-call(s32[5]{0:T(128)S(1)} %shard_map.129.place, bf16[8,1024,128]{2,1,0:T(8,128)(2,1)S(1)} %get-tuple-element.160.q_all, ...), custom_call_target="tpu_custom_call" | custom-call | flops 1000 | bytes 1000 | tf_op jit(solution)/shard_map/pallas_call | solution.py:836
  111.9 3.1 %shard_map.138 = f32[1024,512]{1,0:T(8,128)} custom-call(f32[1024,512]{1,0:T(8,128)S(1)} %get-tuple-element.166.gm, bf16[1024,512]{1,0:T(8,128)(2,1)S(1)} %get-tuple-element.167.dq, bf16[1024,512]{1,0:T(8,128)(2,1)S(1)} %get-tuple-element.168.dk, bf16[1024,512]{1,0:T(8,128)(2,1)S(1)} %get-tuple-element.169.dv, ...), custom_call_target="tpu_custom_call" | custom-call | flops 34359738368 | bytes 1000 | tf_op jit(solution)/shard_map/pallas_call | solution.py:845
  116.0 1.5 %collective-permute-start.26 = (bf16[49,16,128]{2,1,0:T(8,128)(2,1)S(1)}, bf16[49,16,128]{2,1,0:T(8,128)(2,1)S(1)}, u32[]{:S(2)}, u32[]{:S(2)}) collective-permute-start(bf16[49,16,128]{2,1,0:T(8,128)(2,1)S(1)} %get-tuple-element.186), channel_id=1, source_target_pairs={{0,2},{1,3},{2,0},{3,1},{4,6},{5,7},{6,4},{7,5},{8,10},{9,11},{10,... | collective-permute-start | bytes 602120 | tf_op jit(solution)/shard_map/ppermute | solution.py:627
  117.5 1.4 %collective-permute-start.27 = (bf16[49,16,128]{2,1,0:T(8,128)(2,1)S(1)}, bf16[49,16,128]{2,1,0:T(8,128)(2,1)S(1)}, u32[]{:S(2)}, u32[]{:S(2)}) collective-permute-start(bf16[49,16,128]{2,1,0:T(8,128)(2,1)S(1)} %get-tuple-element.187), channel_id=1, source_target_pairs={{0,4},{1,5},{2,6},{3,7},{4,0},{5,1},{6,2},{7,3},{8,12},{9,13},{10,... | collective-permute-start | bytes 602120 | tf_op jit(solution)/shard_map/ppermute | solution.py:627
  121.3 1.7 %collective-permute-start.33 = (bf16[33,16,128]{2,1,0:T(8,128)(2,1)S(1)}, bf16[33,16,128]{2,1,0:T(8,128)(2,1)S(1)}, u32[]{:S(2)}, u32[]{:S(2)}) collective-permute-start(bf16[33,16,128]{2,1,0:T(8,128)(2,1)S(1)} %get-tuple-element.195), channel_id=1, source_target_pairs={{0,16},{1,17},{2,18},{3,19},{4,20},{5,21},{6,22},{7,23},{8,24},{9,... | collective-permute-start | bytes 405512 | tf_op jit(solution)/shard_map/ppermute | solution.py:627
  123.2 1.9 %collective-permute-start.34 = (bf16[33,16,128]{2,1,0:T(8,128)(2,1)S(1)}, bf16[33,16,128]{2,1,0:T(8,128)(2,1)S(1)}, u32[]{:S(2)}, u32[]{:S(2)}) collective-permute-start(bf16[33,16,128]{2,1,0:T(8,128)(2,1)S(1)} %get-tuple-element.196), channel_id=1, source_target_pairs={{0,24},{1,25},{2,26},{3,27},{4,28},{5,29},{6,30},{7,31},{8,16},{9,... | collective-permute-start | bytes 405512 | tf_op jit(solution)/shard_map/ppermute | solution.py:627
  125.4 3.3 %collective-permute-done.28.g3 = bf16[49,16,128]{2,1,0:T(8,128)(2,1)S(1)} collective-permute-done((bf16[49,16,128]{2,1,0:T(8,128)(2,1)S(1)}, bf16[49,16,128]{2,1,0:T(8,128)(2,1)S(1)}, u32[]{:S(2)}, u32[]{:S(2)}) %collective-permute-start.28) | collective-permute-done | bytes 200736 | tf_op jit(solution)/shard_map/ppermute | solution.py:627
  130.3 1.7 %collective-permute-start.30 = (bf16[17,16,128]{2,1,0:T(8,128)(2,1)S(1)}, bf16[17,16,128]{2,1,0:T(8,128)(2,1)S(1)}, u32[]{:S(2)}, u32[]{:S(2)}) collective-permute-start(bf16[17,16,128]{2,1,0:T(8,128)(2,1)S(1)} %get-tuple-element.204), channel_id=1, source_target_pairs={{0,16},{1,17},{2,18},{3,19},{4,20},{5,21},{6,22},{7,23},{8,24},{9,... | collective-permute-start | bytes 208904 | tf_op jit(solution)/shard_map/ppermute | solution.py:627
  132.0 1.9 %collective-permute-start.31 = (bf16[17,16,128]{2,1,0:T(8,128)(2,1)S(1)}, bf16[17,16,128]{2,1,0:T(8,128)(2,1)S(1)}, u32[]{:S(2)}, u32[]{:S(2)}) collective-permute-start(bf16[17,16,128]{2,1,0:T(8,128)(2,1)S(1)} %get-tuple-element.205), channel_id=1, source_target_pairs={{0,24},{1,25},{2,26},{3,27},{4,28},{5,29},{6,30},{7,31},{8,16},{9,... | collective-permute-start | bytes 208904 | tf_op jit(solution)/shard_map/ppermute | solution.py:627
  134.9 1.4 shard_map.142
  136.3 4.5 %collective-permute-done.30.a2 = bf16[17,16,128]{2,1,0:T(8,128)(2,1)S(1)} collective-permute-done((bf16[17,16,128]{2,1,0:T(8,128)(2,1)S(1)}, bf16[17,16,128]{2,1,0:T(8,128)(2,1)S(1)}, u32[]{:S(2)}, u32[]{:S(2)}) %collective-permute-start.30) | collective-permute-done | bytes 69664 | tf_op jit(solution)/shard_map/ppermute | solution.py:627
  140.8 1.2 shard_map.143
  (76 shorter events, 18.5 us)
Async XLA Ops:
  2.2 11.2 %collective-permute-start.2 = (bf16[17,16,128]{2,1,0:T(8,128)(2,1)S(1)}, bf16[17,16,128]{2,1,0:T(8,128)(2,1)S(1)}, u32[]{:S(2)}, u32[]{:S(2)}) collective-permute-start(bf16[17,16,128]{2,1,0:T(8,128)(2,1)S(1)} %shard_map.127), channel_id=1, source_target_pairs={{0,24},{1,25},{2,26},{3,27},{4,28},{5,29},{6,30},{7,31},{8,16},{9,... | collective-permute-start | bytes 208904 | tf_op jit(solution)/shard_map/ppermute | solution.py:627
  7.3 6.6 %collective-permute-start.1 = (bf16[17,16,128]{2,1,0:T(8,128)(2,1)S(1)}, bf16[17,16,128]{2,1,0:T(8,128)(2,1)S(1)}, u32[]{:S(2)}, u32[]{:S(2)}) collective-permute-start(bf16[17,16,128]{2,1,0:T(8,128)(2,1)S(1)} %shard_map.127), channel_id=1, source_target_pairs={{0,16},{1,17},{2,18},{3,19},{4,20},{5,21},{6,22},{7,23},{8,24},{9,... | collective-permute-start | bytes 208904 | tf_op jit(solution)/shard_map/ppermute | solution.py:627
  7.3 6.6 %collective-permute-start = (bf16[17,16,128]{2,1,0:T(8,128)(2,1)S(1)}, bf16[17,16,128]{2,1,0:T(8,128)(2,1)S(1)}, u32[]{:S(2)}, u32[]{:S(2)}) collective-permute-start(bf16[17,16,128]{2,1,0:T(8,128)(2,1)S(1)} %shard_map.127), channel_id=1, source_target_pairs={{0,8},{1,9},{2,10},{3,11},{4,12},{5,13},{6,14},{7,15},{8,0},{9,1},... | collective-permute-start | bytes 208904 | tf_op jit(solution)/shard_map/ppermute | solution.py:627
  9.5 7.5 %collective-permute-start.8 = (bf16[32,16,128]{2,1,0:T(8,128)(2,1)S(1)}, bf16[32,16,128]{2,1,0:T(8,128)(2,1)S(1)}, u32[]{:S(2)}, u32[]{:S(2)}) collective-permute-start(bf16[32,16,128]{2,1,0:T(8,128)(2,1)S(1)} %shard_map.128), channel_id=1, source_target_pairs={{0,8},{1,9},{2,10},{3,11},{4,12},{5,13},{6,14},{7,15},{8,0},{9,1},... | collective-permute-start | bytes 393224 | tf_op jit(solution)/shard_map/ppermute | solution.py:627
  11.0 9.6 %collective-permute-start.7 = (bf16[32,16,128]{2,1,0:T(8,128)(2,1)S(1)}, bf16[32,16,128]{2,1,0:T(8,128)(2,1)S(1)}, u32[]{:S(2)}, u32[]{:S(2)}) collective-permute-start(bf16[32,16,128]{2,1,0:T(8,128)(2,1)S(1)} %shard_map.128), channel_id=1, source_target_pairs={{0,24},{1,25},{2,26},{3,27},{4,28},{5,29},{6,30},{7,31},{8,16},{9,... | collective-permute-start | bytes 393224 | tf_op jit(solution)/shard_map/ppermute | solution.py:627
  13.4 11.9 %collective-permute-start.6 = (bf16[32,16,128]{2,1,0:T(8,128)(2,1)S(1)}, bf16[32,16,128]{2,1,0:T(8,128)(2,1)S(1)}, u32[]{:S(2)}, u32[]{:S(2)}) collective-permute-start(bf16[32,16,128]{2,1,0:T(8,128)(2,1)S(1)} %shard_map.128), channel_id=1, source_target_pairs={{0,16},{1,17},{2,18},{3,19},{4,20},{5,21},{6,22},{7,23},{8,24},{9,... | collective-permute-start | bytes 393224 | tf_op jit(solution)/shard_map/ppermute | solution.py:627
  14.0 14.0 %collective-permute-start.5 = (bf16[4,17,16,128]{3,2,1,0:T(8,128)(2,1)S(1)}, bf16[4,17,16,128]{3,2,1,0:T(8,128)(2,1)S(1)}, u32[]{:S(2)}, u32[]{:S(2)}) collective-permute-start(bf16[4,17,16,128]{3,2,1,0:T(8,128)(2,1)S(1)} %pad_maximum_fusion.1.refs_0_), channel_id=1, source_target_pairs={{0,6},{1,7},{2,4},{3,5},{4,2},{5,3},{6,0},{7,1},{8,14},{9,15},{10,... | collective-permute-start | bytes 835592 | tf_op jit(solution)/shard_map/ppermute | solution.py:627
  16.5 12.2 %collective-permute-start.4 = (bf16[4,17,16,128]{3,2,1,0:T(8,128)(2,1)S(1)}, bf16[4,17,16,128]{3,2,1,0:T(8,128)(2,1)S(1)}, u32[]{:S(2)}, u32[]{:S(2)}) collective-permute-start(bf16[4,17,16,128]{3,2,1,0:T(8,128)(2,1)S(1)} %pad_maximum_fusion.1.refs_0_), channel_id=1, source_target_pairs={{0,4},{1,5},{2,6},{3,7},{4,0},{5,1},{6,2},{7,3},{8,12},{9,13},{10,... | collective-permute-start | bytes 835592 | tf_op jit(solution)/shard_map/ppermute | solution.py:627
  17.0 11.7 %collective-permute-start.3 = (bf16[4,17,16,128]{3,2,1,0:T(8,128)(2,1)S(1)}, bf16[4,17,16,128]{3,2,1,0:T(8,128)(2,1)S(1)}, u32[]{:S(2)}, u32[]{:S(2)}) collective-permute-start(bf16[4,17,16,128]{3,2,1,0:T(8,128)(2,1)S(1)} %pad_maximum_fusion.1.refs_0_), channel_id=1, source_target_pairs={{0,2},{1,3},{2,0},{3,1},{4,6},{5,7},{6,4},{7,5},{8,10},{9,11},{10,... | collective-permute-start | bytes 835592 | tf_op jit(solution)/shard_map/ppermute | solution.py:627
  28.7 3.4 %collective-permute-start.12 = (bf16[4,17,16,128]{3,2,1,0:T(8,128)(2,1)S(1)}, bf16[4,17,16,128]{3,2,1,0:T(8,128)(2,1)S(1)}, u32[]{:S(2)}, u32[]{:S(2)}) collective-permute-start(bf16[4,17,16,128]{3,2,1,0:T(8,128)(2,1)S(1)} %pad_maximum_fusion.1.refs_0_), channel_id=1, source_target_pairs={{0,1},{1,0},{2,3},{3,2},{4,5},{5,4},{6,7},{7,6},{8,9},{9,8},{10,11... | collective-permute-start | bytes 835592 | tf_op jit(solution)/shard_map/ppermute | solution.py:627
  28.7 3.9 %collective-permute-start.13 = (bf16[4,17,16,128]{3,2,1,0:T(8,128)(2,1)S(1)}, bf16[4,17,16,128]{3,2,1,0:T(8,128)(2,1)S(1)}, u32[]{:S(2)}, u32[]{:S(2)}) collective-permute-start(bf16[4,17,16,128]{3,2,1,0:T(8,128)(2,1)S(1)} %collective-permute-done.3.refs_1_), channel_id=1, source_target_pairs={{0,1},{1,0},{2,3},{3,2},{4,5},{5,4},{6,7},{7,6},{8,9},{9,8},{10,11... | collective-permute-start | bytes 835592 | tf_op jit(solution)/shard_map/ppermute | solution.py:627
  29.2 4.0 %collective-permute-start.14 = (bf16[4,17,16,128]{3,2,1,0:T(8,128)(2,1)S(1)}, bf16[4,17,16,128]{3,2,1,0:T(8,128)(2,1)S(1)}, u32[]{:S(2)}, u32[]{:S(2)}) collective-permute-start(bf16[4,17,16,128]{3,2,1,0:T(8,128)(2,1)S(1)} %collective-permute-done.4.refs_2_), channel_id=1, source_target_pairs={{0,1},{1,0},{2,3},{3,2},{4,5},{5,4},{6,7},{7,6},{8,9},{9,8},{10,11... | collective-permute-start | bytes 835592 | tf_op jit(solution)/shard_map/ppermute | solution.py:627
  29.2 4.0 %collective-permute-start.15 = (bf16[4,17,16,128]{3,2,1,0:T(8,128)(2,1)S(1)}, bf16[4,17,16,128]{3,2,1,0:T(8,128)(2,1)S(1)}, u32[]{:S(2)}, u32[]{:S(2)}) collective-permute-start(bf16[4,17,16,128]{3,2,1,0:T(8,128)(2,1)S(1)} %collective-permute-done.5.refs_3_), channel_id=1, source_target_pairs={{0,1},{1,0},{2,3},{3,2},{4,5},{5,4},{6,7},{7,6},{8,9},{9,8},{10,11... | collective-permute-start | bytes 835592 | tf_op jit(solution)/shard_map/ppermute | solution.py:627
  29.7 21.2 %collective-permute-start.11 = (bf16[4,32,16,128]{3,2,1,0:T(8,128)(2,1)S(1)}, bf16[4,32,16,128]{3,2,1,0:T(8,128)(2,1)S(1)}, u32[]{:S(2)}, u32[]{:S(2)}) collective-permute-start(bf16[4,32,16,128]{3,2,1,0:T(8,128)(2,1)S(1)} %pad_maximum_fusion.refs_0_), channel_id=1, source_target_pairs={{0,6},{1,7},{2,4},{3,5},{4,2},{5,3},{6,0},{7,1},{8,14},{9,15},{10,... | collective-permute-start | bytes 1572872 | tf_op jit(solution)/shard_map/ppermute | solution.py:627
  32.0 23.6 %collective-permute-start.10 = (bf16[4,32,16,128]{3,2,1,0:T(8,128)(2,1)S(1)}, bf16[4,32,16,128]{3,2,1,0:T(8,128)(2,1)S(1)}, u32[]{:S(2)}, u32[]{:S(2)}) collective-permute-start(bf16[4,32,16,128]{3,2,1,0:T(8,128)(2,1)S(1)} %pad_maximum_fusion.refs_0_), channel_id=1, source_target_pairs={{0,4},{1,5},{2,6},{3,7},{4,0},{5,1},{6,2},{7,3},{8,12},{9,13},{10,... | collective-permute-start | bytes 1572872 | tf_op jit(solution)/shard_map/ppermute | solution.py:627
  32.6 23.1 %collective-permute-start.9 = (bf16[4,32,16,128]{3,2,1,0:T(8,128)(2,1)S(1)}, bf16[4,32,16,128]{3,2,1,0:T(8,128)(2,1)S(1)}, u32[]{:S(2)}, u32[]{:S(2)}) collective-permute-start(bf16[4,32,16,128]{3,2,1,0:T(8,128)(2,1)S(1)} %pad_maximum_fusion.refs_0_), channel_id=1, source_target_pairs={{0,2},{1,3},{2,0},{3,1},{4,6},{5,7},{6,4},{7,5},{8,10},{9,11},{10,... | collective-permute-start | bytes 1572872 | tf_op jit(solution)/shard_map/ppermute | solution.py:627
  49.2 6.5 %collective-permute-start.16 = (bf16[4,32,16,128]{3,2,1,0:T(8,128)(2,1)S(1)}, bf16[4,32,16,128]{3,2,1,0:T(8,128)(2,1)S(1)}, u32[]{:S(2)}, u32[]{:S(2)}) collective-permute-start(bf16[4,32,16,128]{3,2,1,0:T(8,128)(2,1)S(1)} %pad_maximum_fusion.refs_0_), channel_id=1, source_target_pairs={{0,1},{1,0},{2,3},{3,2},{4,5},{5,4},{6,7},{7,6},{8,9},{9,8},{10,11... | collective-permute-start | bytes 1572872 | tf_op jit(solution)/shard_map/ppermute | solution.py:627
  78.8 5.1 %collective-permute-start.20 = (bf16[16,33,16,128]{3,2,1,0:T(8,128)(2,1)S(1)}, bf16[16,33,16,128]{3,2,1,0:T(8,128)(2,1)S(1)}, u32[]{:S(2)}, u32[]{:S(2)}) collective-permute-start(bf16[16,33,16,128]{3,2,1,0:T(8,128)(2,1)S(1)} %get-tuple-element.146), channel_id=1, source_target_pairs={{0,1},{1,0},{2,3},{3,2},{4,5},{5,4},{6,7},{7,6},{8,9},{9,8},{10,11... | collective-permute-start | bytes 6488072 | tf_op jit(solution)/shard_map/ppermute | solution.py:627
  79.0 4.9 %collective-permute-start.21 = (f32[4,16,16,128]{3,2,1,0:T(8,128)S(1)}, f32[4,16,16,128]{3,2,1,0:T(8,128)S(1)}, u32[]{:S(2)}, u32[]{:S(2)}) collective-permute-start(f32[4,16,16,128]{3,2,1,0:T(8,128)S(1)} %get-tuple-element.147), channel_id=1, source_target_pairs={{0,1},{1,0},{2,3},{3,2},{4,5},{5,4},{6,7},{7,6},{8,9},{9,8},{10,11... | collective-permute-start | bytes 1572872 | tf_op jit(solution)/shard_map/ppermute | solution.py:627
  84.9 30.2 %collective-permute-start.23 = (bf16[148,16,128]{2,1,0:T(8,128)(2,1)S(1)}, bf16[148,16,128]{2,1,0:T(8,128)(2,1)S(1)}, u32[]{:S(2)}, u32[]{:S(2)}) collective-permute-start(bf16[148,16,128]{2,1,0:T(8,128)(2,1)S(1)} %get-tuple-element.171), channel_id=1, source_target_pairs={{0,2},{1,3},{2,0},{3,1},{4,6},{5,7},{6,4},{7,5},{8,10},{9,11},{10,... | collective-permute-start | bytes 1818632 | tf_op jit(solution)/shard_map/ppermute | solution.py:627
  86.4 28.7 %collective-permute-start.24 = (bf16[148,16,128]{2,1,0:T(8,128)(2,1)S(1)}, bf16[148,16,128]{2,1,0:T(8,128)(2,1)S(1)}, u32[]{:S(2)}, u32[]{:S(2)}) collective-permute-start(bf16[148,16,128]{2,1,0:T(8,128)(2,1)S(1)} %get-tuple-element.172), channel_id=1, source_target_pairs={{0,4},{1,5},{2,6},{3,7},{4,0},{5,1},{6,2},{7,3},{8,12},{9,13},{10,... | collective-permute-start | bytes 1818632 | tf_op jit(solution)/shard_map/ppermute | solution.py:627
  87.9 27.2 %collective-permute-start.25 = (bf16[148,16,128]{2,1,0:T(8,128)(2,1)S(1)}, bf16[148,16,128]{2,1,0:T(8,128)(2,1)S(1)}, u32[]{:S(2)}, u32[]{:S(2)}) collective-permute-start(bf16[148,16,128]{2,1,0:T(8,128)(2,1)S(1)} %get-tuple-element.173), channel_id=1, source_target_pairs={{0,6},{1,7},{2,4},{3,5},{4,2},{5,3},{6,0},{7,1},{8,14},{9,15},{10,... | collective-permute-start | bytes 1818632 | tf_op jit(solution)/shard_map/ppermute | solution.py:627
  111.8 3.5 %collective-permute-start.22 = (f32[3080,128]{1,0:T(8,128)S(1)}, f32[3080,128]{1,0:T(8,128)S(1)}, u32[]{:S(2)}, u32[]{:S(2)}) collective-permute-start(f32[3080,128]{1,0:T(8,128)S(1)} %get-tuple-element.165), channel_id=1, source_target_pairs={{0,1},{1,0},{2,3},{3,2},{4,5},{5,4},{6,7},{7,6},{8,9},{9,8},{10,11... | collective-permute-start | bytes 4730888 | tf_op jit(solution)/shard_map/ppermute | solution.py:627
  116.0 7.2 %collective-permute-start.26 = (bf16[49,16,128]{2,1,0:T(8,128)(2,1)S(1)}, bf16[49,16,128]{2,1,0:T(8,128)(2,1)S(1)}, u32[]{:S(2)}, u32[]{:S(2)}) collective-permute-start(bf16[49,16,128]{2,1,0:T(8,128)(2,1)S(1)} %get-tuple-element.186), channel_id=1, source_target_pairs={{0,2},{1,3},{2,0},{3,1},{4,6},{5,7},{6,4},{7,5},{8,10},{9,11},{10,... | collective-permute-start | bytes 602120 | tf_op jit(solution)/shard_map/ppermute | solution.py:627
  117.5 7.9 %collective-permute-start.27 = (bf16[49,16,128]{2,1,0:T(8,128)(2,1)S(1)}, bf16[49,16,128]{2,1,0:T(8,128)(2,1)S(1)}, u32[]{:S(2)}, u32[]{:S(2)}) collective-permute-start(bf16[49,16,128]{2,1,0:T(8,128)(2,1)S(1)} %get-tuple-element.187), channel_id=1, source_target_pairs={{0,4},{1,5},{2,6},{3,7},{4,0},{5,1},{6,2},{7,3},{8,12},{9,13},{10,... | collective-permute-start | bytes 602120 | tf_op jit(solution)/shard_map/ppermute | solution.py:627
  119.0 9.8 %collective-permute-start.28 = (bf16[49,16,128]{2,1,0:T(8,128)(2,1)S(1)}, bf16[49,16,128]{2,1,0:T(8,128)(2,1)S(1)}, u32[]{:S(2)}, u32[]{:S(2)}) collective-permute-start(bf16[49,16,128]{2,1,0:T(8,128)(2,1)S(1)} %get-tuple-element.188), channel_id=1, source_target_pairs={{0,6},{1,7},{2,4},{3,5},{4,2},{5,3},{6,0},{7,1},{8,14},{9,15},{10,... | collective-permute-start | bytes 602120 | tf_op jit(solution)/shard_map/ppermute | solution.py:627
  120.4 11.5 %collective-permute-start.32 = (bf16[33,16,128]{2,1,0:T(8,128)(2,1)S(1)}, bf16[33,16,128]{2,1,0:T(8,128)(2,1)S(1)}, u32[]{:S(2)}, u32[]{:S(2)}) collective-permute-start(bf16[33,16,128]{2,1,0:T(8,128)(2,1)S(1)} %get-tuple-element.194), channel_id=1, source_target_pairs={{0,8},{1,9},{2,10},{3,11},{4,12},{5,13},{6,14},{7,15},{8,0},{9,1},... | collective-permute-start | bytes 405512 | tf_op jit(solution)/shard_map/ppermute | solution.py:627
  121.3 13.6 %collective-permute-start.33 = (bf16[33,16,128]{2,1,0:T(8,128)(2,1)S(1)}, bf16[33,16,128]{2,1,0:T(8,128)(2,1)S(1)}, u32[]{:S(2)}, u32[]{:S(2)}) collective-permute-start(bf16[33,16,128]{2,1,0:T(8,128)(2,1)S(1)} %get-tuple-element.195), channel_id=1, source_target_pairs={{0,16},{1,17},{2,18},{3,19},{4,20},{5,21},{6,22},{7,23},{8,24},{9,... | collective-permute-start | bytes 405512 | tf_op jit(solution)/shard_map/ppermute | solution.py:627
  123.2 11.6 %collective-permute-start.34 = (bf16[33,16,128]{2,1,0:T(8,128)(2,1)S(1)}, bf16[33,16,128]{2,1,0:T(8,128)(2,1)S(1)}, u32[]{:S(2)}, u32[]{:S(2)}) collective-permute-start(bf16[33,16,128]{2,1,0:T(8,128)(2,1)S(1)} %get-tuple-element.196), channel_id=1, source_target_pairs={{0,24},{1,25},{2,26},{3,27},{4,28},{5,29},{6,30},{7,31},{8,16},{9,... | collective-permute-start | bytes 405512 | tf_op jit(solution)/shard_map/ppermute | solution.py:627
  129.4 6.9 %collective-permute-start.29 = (bf16[17,16,128]{2,1,0:T(8,128)(2,1)S(1)}, bf16[17,16,128]{2,1,0:T(8,128)(2,1)S(1)}, u32[]{:S(2)}, u32[]{:S(2)}) collective-permute-start(bf16[17,16,128]{2,1,0:T(8,128)(2,1)S(1)} %get-tuple-element.203), channel_id=1, source_target_pairs={{0,8},{1,9},{2,10},{3,11},{4,12},{5,13},{6,14},{7,15},{8,0},{9,1},... | collective-permute-start | bytes 208904 | tf_op jit(solution)/shard_map/ppermute | solution.py:627
  130.3 10.5 %collective-permute-start.30 = (bf16[17,16,128]{2,1,0:T(8,128)(2,1)S(1)}, bf16[17,16,128]{2,1,0:T(8,128)(2,1)S(1)}, u32[]{:S(2)}, u32[]{:S(2)}) collective-permute-start(bf16[17,16,128]{2,1,0:T(8,128)(2,1)S(1)} %get-tuple-element.204), channel_id=1, source_target_pairs={{0,16},{1,17},{2,18},{3,19},{4,20},{5,21},{6,22},{7,23},{8,24},{9,... | collective-permute-start | bytes 208904 | tf_op jit(solution)/shard_map/ppermute | solution.py:627
  132.0 8.8 %collective-permute-start.31 = (bf16[17,16,128]{2,1,0:T(8,128)(2,1)S(1)}, bf16[17,16,128]{2,1,0:T(8,128)(2,1)S(1)}, u32[]{:S(2)}, u32[]{:S(2)}) collective-permute-start(bf16[17,16,128]{2,1,0:T(8,128)(2,1)S(1)} %get-tuple-element.205), channel_id=1, source_target_pairs={{0,24},{1,25},{2,26},{3,27},{4,28},{5,29},{6,30},{7,31},{8,16},{9,... | collective-permute-start | bytes 208904 | tf_op jit(solution)/shard_map/ppermute | solution.py:627
  (12 other events, 78.8 us)

commit v3 on v2

--- a/solution.py
+++ b/solution.py
@@ -803,9 +803,11 @@
         [SMEM] + [VMEM] * 5, [], 1000, 1000, 20,
     )(gates, tokens, cotangent, ctx, w, bias)
     if direct:
-        other = swap(tie(chips_f[0], ctx), n, 1)
-        chips_f, other, branch = lax.optimization_barrier((chips_f, other, branch))
-        gf_all = chips_f + [other] + [swap(part, n, 1) for part in chips_f[1:]]
+        own, y, x, xy = chips_f
+        xy, branch = lax.optimization_barrier((xy, branch))
+        own_other, xy_other = swap(tie(own, ctx), n, 1), swap(xy, n, 1)
+        y, x, own_other, xy_other = lax.optimization_barrier((y, x, own_other, xy_other))
+        gf_all = [own, y, x, xy, own_other, swap(y, n, 1), swap(x, n, 1), xy_other]
     layer, gm, gctx, ff_keep, ff_send, wo_keep, wo_send = call(
         feed_body,
         [(row, BF, ANY), (row, F32), (row, BF)]

time: 142 us -> 140 us (0.986)
  transfers between devices with their start and end apart: 35 -> 35, of which waited for: 14 -> 14; matrix products, arithmetic and copies ran while one was open for 0% -> 0% of each run, Pallas kernels for 37% -> 38%
where the time goes in v3:
time: 140 us
  Pallas kernels  76 us (54%)
  starting transfers between devices  35.2 us (25%)
  waiting for transfers between devices  25.3 us (18%)
  local copies, waits for them, and re-layouts  2.51 us (2%)
    ppermute x35, starting transfers between devices, swap(): return lax.ppermute(x, AXES, [(i, i ^ bit) for i in range(n)])  35.2 us
    ppermute x35, waiting for transfers between devices, swap(): return lax.ppermute(x, AXES, [(i, i ^ bit) for i in range(n)])  25.3 us
    pallas_call x1, Pallas kernels, local(): call(back_body, [(row, BF)] * 3 + [((4 * SHARE + 8, 128), F32)] * 2, [SME...  23.4 us
    pallas_call x1, Pallas kernels, local(): call(feed_body, [(row, BF, ANY), (row, F32), (row, BF)] + [((n // 2, G_TI...  19.7 us
    pallas_call x1, Pallas kernels, local(): call(attend_body, [(row, BF), ((D + 16, ROWS), BF), ((8, ROWS), F32)], [V...  13.4 us
    pallas_call x6, Pallas kernels, small(): return call(body, outs, ins, scratch, 2 * size, 6 * size, 16)(*args)  3.93 us
    pallas_call x1, Pallas kernels, local(): call(input_body, [(row, F32)], [VMEM] * 5, [], 32 << 30, 1000, 24)  3.15 us
    pallas_call x1, Pallas kernels, local(): call(back_first_body, [(half, F32)] + sums, [VMEM] * 5, buffers, 1000, 10...  3.01 us
  transfers between devices with their start and end apart: 35, of which 14 were waited for; matrix products, arithmetic and copies ran while one was open for 0% of the time, Pallas kernels for 38%

profile of v3, /device:TPU:0, one launch (start us, length us, event | category | flops | bytes accessed | tf_op | source)
XLA Modules:
  0.0 140.1 jit_solution(6852702129933476100)
XLA Ops:
  2.2 5.1 %collective-permute-start.2 = (bf16[17,16,128]{2,1,0:T(8,128)(2,1)S(1)}, bf16[17,16,128]{2,1,0:T(8,128)(2,1)S(1)}, u32[]{:S(2)}, u32[]{:S(2)}) collective-permute-start(bf16[17,16,128]{2,1,0:T(8,128)(2,1)S(1)} %shard_map.127), channel_id=1, source_target_pairs={{0,24},{1,25},{2,26},{3,27},{4,28},{5,29},{6,30},{7,31},{8,16},{9,... | collective-permute-start | bytes 208904 | tf_op jit(solution)/shard_map/ppermute | solution.py:627
  9.5 1.5 %collective-permute-start.8 = (bf16[32,16,128]{2,1,0:T(8,128)(2,1)S(1)}, bf16[32,16,128]{2,1,0:T(8,128)(2,1)S(1)}, u32[]{:S(2)}, u32[]{:S(2)}) collective-permute-start(bf16[32,16,128]{2,1,0:T(8,128)(2,1)S(1)} %shard_map.128), channel_id=1, source_target_pairs={{0,8},{1,9},{2,10},{3,11},{4,12},{5,13},{6,14},{7,15},{8,0},{9,1},... | collective-permute-start | bytes 393224 | tf_op jit(solution)/shard_map/ppermute | solution.py:627
  11.0 2.4 %collective-permute-start.7 = (bf16[32,16,128]{2,1,0:T(8,128)(2,1)S(1)}, bf16[32,16,128]{2,1,0:T(8,128)(2,1)S(1)}, u32[]{:S(2)}, u32[]{:S(2)}) collective-permute-start(bf16[32,16,128]{2,1,0:T(8,128)(2,1)S(1)} %shard_map.128), channel_id=1, source_target_pairs={{0,24},{1,25},{2,26},{3,27},{4,28},{5,29},{6,30},{7,31},{8,16},{9,... | collective-permute-start | bytes 393224 | tf_op jit(solution)/shard_map/ppermute | solution.py:627
  14.0 2.5 %collective-permute-start.5 = (bf16[4,17,16,128]{3,2,1,0:T(8,128)(2,1)S(1)}, bf16[4,17,16,128]{3,2,1,0:T(8,128)(2,1)S(1)}, u32[]{:S(2)}, u32[]{:S(2)}) collective-permute-start(bf16[4,17,16,128]{3,2,1,0:T(8,128)(2,1)S(1)} %pad_maximum_fusion.1.refs_0_), channel_id=1, source_target_pairs={{0,6},{1,7},{2,4},{3,5},{4,2},{5,3},{6,0},{7,1},{8,14},{9,15},{10,... | collective-permute-start | bytes 835592 | tf_op jit(solution)/shard_map/ppermute | solution.py:627
  18.0 2.6 %collective-permute-done.7 = bf16[32,16,128]{2,1,0:T(8,128)(2,1)S(1)} collective-permute-done((bf16[32,16,128]{2,1,0:T(8,128)(2,1)S(1)}, bf16[32,16,128]{2,1,0:T(8,128)(2,1)S(1)}, u32[]{:S(2)}, u32[]{:S(2)}) %collective-permute-start.7) | collective-permute-done | bytes 131104 | tf_op jit(solution)/shard_map/ppermute | solution.py:627
  20.6 4.6 %collective-permute-done.6 = bf16[32,16,128]{2,1,0:T(8,128)(2,1)S(1)} collective-permute-done((bf16[32,16,128]{2,1,0:T(8,128)(2,1)S(1)}, bf16[32,16,128]{2,1,0:T(8,128)(2,1)S(1)}, u32[]{:S(2)}, u32[]{:S(2)}) %collective-permute-start.6) | collective-permute-done | bytes 131104 | tf_op jit(solution)/shard_map/ppermute | solution.py:627
  25.2 1.1 shard_map.129.place
  26.4 1.5 %shard_map.130 = (bf16[2,1024,128]{2,1,0:T(8,128)(2,1)S(1)}, bf16[2,1024,128]{2,1,0:T(8,128)(2,1)S(1)}, bf16[528,1024]{1,0:T(8,128)(2,1)S(1)}) custom-call(s32[1,3]{1,0:T(1,128)S(1)} %copy-done.5, s32[1,8]{1,0:T(1,128)S(1)} %copy-done.6, bf16[1024,512]{1,0:T(8,128)(2,1)S(1)} %copy-done), custom_call_target="tpu_custom_call" | custom-call | flops 1000 | bytes 1000 | tf_op jit(solution)/shard_map/pallas_call | solution.py:757
  28.7 2.3 %collective-permute-start.9 = (bf16[4,32,16,128]{3,2,1,0:T(8,128)(2,1)S(1)}, bf16[4,32,16,128]{3,2,1,0:T(8,128)(2,1)S(1)}, u32[]{:S(2)}, u32[]{:S(2)}) collective-permute-start(bf16[4,32,16,128]{3,2,1,0:T(8,128)(2,1)S(1)} %pad_maximum_fusion.refs_0_), channel_id=1, source_target_pairs={{0,6},{1,7},{2,4},{3,5},{4,2},{5,3},{6,0},{7,1},{8,14},{9,15},{10,... | collective-permute-start | bytes 1572872 | tf_op jit(solution)/shard_map/ppermute | solution.py:627
  33.8 2.6 %shard_map.131 = (bf16[8,1024,128]{2,1,0:T(8,128)(2,1)S(1)}, bf16[8,1024,128]{2,1,0:T(8,128)(2,1)S(1)}, bf16[1024,512]{1,0:T(8,128)(2,1)S(1)}, bf16[32,17,16,128]{3,2,1,0:T(8,128)(2,1)S(1)}, f32[1,4096]{1,0:T(1,128)S(1)}) custom-call(s32[5]{0:T(128)S(1)} %shard_map.129.place, bf16[1024,512]{1,0:T(8,128)(2,1)S(1)} %copy-done, ...), custom_call_target="tpu_custom_call" | custom-call | flops 1000 | bytes 1000 | tf_op jit(solution)/shard_map/pallas_call | solution.py:788
  36.4 13.4 %shard_map.132 = (bf16[1024,512]{1,0:T(8,128)(2,1)S(1)}, bf16[528,1024]{1,0:T(8,128)(2,1)S(1)}, f32[8,1024]{1,0:T(8,128)S(1)}) custom-call(bf16[8,1024,128]{2,1,0:T(8,128)(2,1)S(1)} %get-tuple-element.160.q_all, bf16[8,1024,128]{2,1,0:T(8,128)(2,1)S(1)} %get-tuple-element.127.k_all, bf16[1024,512]{1,0:T(8,128)(2,1)S(1)} %get-tuple-element.128.v_all), custom_call_target="tpu_custom_call" | custom-call | flops 1000 | bytes 1000 | tf_op jit(solution)/shard_map/pallas_call | solution.py:793
  50.0 1.6 %shard_map.133 = (f32[1024,512]{1,0:T(8,128)S(1)}, bf16[1024,512]{1,0:T(8,128)(2,1)S(1)}, bf16[528,1024]{1,0:T(8,128)(2,1)S(1)}, bf16[1024,512]{1,0:T(8,128)(2,1)S(1)}) custom-call(f32[2]{0:T(128)S(1)} %copy-done.8, bf16[1024,512]{1,0:T(8,128)(2,1)S(1)} %copy-done, bf16[1024,512]{1,0:T(8,128)(2,1)S(1)} %copy-done.2, ...), custom_call_target="tpu_custom_call" | custom-call | flops 1000 | bytes 1000 | tf_op jit(solution)/shard_map/pallas_call | solution.py:800
  52.1 2.6 %collective-permute-done.15.refs_2_ = bf16[4,32,16,128]{3,2,1,0:T(8,128)(2,1)S(1)} collective-permute-done((bf16[4,32,16,128]{3,2,1,0:T(8,128)(2,1)S(1)}, bf16[4,32,16,128]{3,2,1,0:T(8,128)(2,1)S(1)}, u32[]{:S(2)}, u32[]{:S(2)}) %collective-permute-start.15) | collective-permute-done | bytes 524320 | tf_op jit(solution)/shard_map/ppermute | solution.py:627
  55.2 1.4 collective-permute-done.18.refs_5_
  57.4 19.7 %shard_map.134 = (bf16[1024,512]{1,0:T(8,128)(2,1)}, f32[1024,512]{1,0:T(8,128)S(1)}, bf16[1024,512]{1,0:T(8,128)(2,1)S(1)}, f32[16,33,16,128]{3,2,1,0:T(8,128)}...) custom-call(s32[5]{0:T(128)S(1)} %shard_map.129.place, ...), custom_call_target="tpu_custom_call" | custom-call | flops 17179869184 | bytes 31457280 | tf_op jit(solution)/shard_map/pallas_call | solution.py:811
  77.7 3.0 %shard_map.135 = (f32[64,1024]{1,0:T(8,128)S(1)}, f32[1024,128]{1,0:T(8,128)S(1)}, f32[1024,128]{1,0:T(8,128)S(1)}) custom-call(bf16[8,1024,128]{2,1,0:T(8,128)(2,1)S(1)} %get-tuple-element.160.q_all, bf16[8,1024,128]{2,1,0:T(8,128)(2,1)S(1)} %get-tuple-element.127.k_all, bf16[1024,512]{1,0:T(8,128)(2,1)S(1)} %get-tuple-element.128.v_all, ...), custom_call_target="tpu_custom_call" | custom-call | flops 1000 | bytes 1000 | tf_op jit(solution)/shard_map/pallas_call | solution.py:830
  80.7 1.5 %collective-permute-done.21.wo_got = f32[4,16,16,128]{3,2,1,0:T(8,128)S(1)} collective-permute-done((f32[4,16,16,128]{3,2,1,0:T(8,128)S(1)}, f32[4,16,16,128]{3,2,1,0:T(8,128)S(1)}, u32[]{:S(2)}, u32[]{:S(2)}) %collective-permute-start.21) | collective-permute-done | bytes 524320 | tf_op jit(solution)/shard_map/ppermute | solution.py:627
  82.2 1.0 shard_map.136
  83.2 1.4 %collective-permute-start.23 = (bf16[148,16,128]{2,1,0:T(8,128)(2,1)S(1)}, bf16[148,16,128]{2,1,0:T(8,128)(2,1)S(1)}, u32[]{:S(2)}, u32[]{:S(2)}) collective-permute-start(bf16[148,16,128]{2,1,0:T(8,128)(2,1)S(1)} %get-tuple-element.171), channel_id=1, source_target_pairs={{0,2},{1,3},{2,0},{3,1},{4,6},{5,7},{6,4},{7,5},{8,10},{9,11},{10,... | collective-permute-start | bytes 1818632 | tf_op jit(solution)/shard_map/ppermute | solution.py:627
  84.6 1.5 %collective-permute-start.24 = (bf16[148,16,128]{2,1,0:T(8,128)(2,1)S(1)}, bf16[148,16,128]{2,1,0:T(8,128)(2,1)S(1)}, u32[]{:S(2)}, u32[]{:S(2)}) collective-permute-start(bf16[148,16,128]{2,1,0:T(8,128)(2,1)S(1)} %get-tuple-element.172), channel_id=1, source_target_pairs={{0,4},{1,5},{2,6},{3,7},{4,0},{5,1},{6,2},{7,3},{8,12},{9,13},{10,... | collective-permute-start | bytes 1818632 | tf_op jit(solution)/shard_map/ppermute | solution.py:627
  86.7 23.4 %shard_map.137 = (bf16[1024,512]{1,0:T(8,128)(2,1)S(1)}, bf16[1024,512]{1,0:T(8,128)(2,1)S(1)}, bf16[1024,512]{1,0:T(8,128)(2,1)S(1)}, f32[3080,128]{1,0:T(8,128)S(1)}, f32[3080,128]{1,0:T(8,128)S(1)}) custom-call(s32[5]{0:T(128)S(1)} %shard_map.129.place, bf16[8,1024,128]{2,1,0:T(8,128)(2,1)S(1)} %get-tuple-element.160.q_all, ...), custom_call_target="tpu_custom_call" | custom-call | flops 1000 | bytes 1000 | tf_op jit(solution)/shard_map/pallas_call | solution.py:838
  110.2 3.1 %shard_map.138 = f32[1024,512]{1,0:T(8,128)} custom-call(f32[1024,512]{1,0:T(8,128)S(1)} %get-tuple-element.166.gm, bf16[1024,512]{1,0:T(8,128)(2,1)S(1)} %get-tuple-element.167.dq, bf16[1024,512]{1,0:T(8,128)(2,1)S(1)} %get-tuple-element.168.dk, bf16[1024,512]{1,0:T(8,128)(2,1)S(1)} %get-tuple-element.169.dv, ...), custom_call_target="tpu_custom_call" | custom-call | flops 34359738368 | bytes 1000 | tf_op jit(solution)/shard_map/pallas_call | solution.py:847
  114.3 1.4 %collective-permute-start.26 = (bf16[49,16,128]{2,1,0:T(8,128)(2,1)S(1)}, bf16[49,16,128]{2,1,0:T(8,128)(2,1)S(1)}, u32[]{:S(2)}, u32[]{:S(2)}) collective-permute-start(bf16[49,16,128]{2,1,0:T(8,128)(2,1)S(1)} %get-tuple-element.186), channel_id=1, source_target_pairs={{0,2},{1,3},{2,0},{3,1},{4,6},{5,7},{6,4},{7,5},{8,10},{9,11},{10,... | collective-permute-start | bytes 602120 | tf_op jit(solution)/shard_map/ppermute | solution.py:627
  115.8 1.5 %collective-permute-start.27 = (bf16[49,16,128]{2,1,0:T(8,128)(2,1)S(1)}, bf16[49,16,128]{2,1,0:T(8,128)(2,1)S(1)}, u32[]{:S(2)}, u32[]{:S(2)}) collective-permute-start(bf16[49,16,128]{2,1,0:T(8,128)(2,1)S(1)} %get-tuple-element.187), channel_id=1, source_target_pairs={{0,4},{1,5},{2,6},{3,7},{4,0},{5,1},{6,2},{7,3},{8,12},{9,13},{10,... | collective-permute-start | bytes 602120 | tf_op jit(solution)/shard_map/ppermute | solution.py:627
  119.2 1.0 collective-permute-start.33
  120.2 1.3 collective-permute-done.26.g1
  121.5 1.7 %collective-permute-start.34 = (bf16[33,16,128]{2,1,0:T(8,128)(2,1)S(1)}, bf16[33,16,128]{2,1,0:T(8,128)(2,1)S(1)}, u32[]{:S(2)}, u32[]{:S(2)}) collective-permute-start(bf16[33,16,128]{2,1,0:T(8,128)(2,1)S(1)} %get-tuple-element.196), channel_id=1, source_target_pairs={{0,24},{1,25},{2,26},{3,27},{4,28},{5,29},{6,30},{7,31},{8,16},{9,... | collective-permute-start | bytes 405512 | tf_op jit(solution)/shard_map/ppermute | solution.py:627
  123.6 3.4 %collective-permute-done.28.g3 = bf16[49,16,128]{2,1,0:T(8,128)(2,1)S(1)} collective-permute-done((bf16[49,16,128]{2,1,0:T(8,128)(2,1)S(1)}, bf16[49,16,128]{2,1,0:T(8,128)(2,1)S(1)}, u32[]{:S(2)}, u32[]{:S(2)}) %collective-permute-start.28) | collective-permute-done | bytes 200736 | tf_op jit(solution)/shard_map/ppermute | solution.py:627
  129.2 3.0 %collective-permute-start.31 = (bf16[17,16,128]{2,1,0:T(8,128)(2,1)S(1)}, bf16[17,16,128]{2,1,0:T(8,128)(2,1)S(1)}, u32[]{:S(2)}, u32[]{:S(2)}) collective-permute-start(bf16[17,16,128]{2,1,0:T(8,128)(2,1)S(1)} %get-tuple-element.205), channel_id=1, source_target_pairs={{0,24},{1,25},{2,26},{3,27},{4,28},{5,29},{6,30},{7,31},{8,16},{9,... | collective-permute-start | bytes 208904 | tf_op jit(solution)/shard_map/ppermute | solution.py:627
  132.8 1.4 shard_map.142
  134.2 4.5 %collective-permute-done.30.a2 = bf16[17,16,128]{2,1,0:T(8,128)(2,1)S(1)} collective-permute-done((bf16[17,16,128]{2,1,0:T(8,128)(2,1)S(1)}, bf16[17,16,128]{2,1,0:T(8,128)(2,1)S(1)}, u32[]{:S(2)}, u32[]{:S(2)}) %collective-permute-start.30) | collective-permute-done | bytes 69664 | tf_op jit(solution)/shard_map/ppermute | solution.py:627
  138.7 1.2 shard_map.143
  (76 shorter events, 18.8 us)
Async XLA Ops:
  2.2 11.2 %collective-permute-start.2 = (bf16[17,16,128]{2,1,0:T(8,128)(2,1)S(1)}, bf16[17,16,128]{2,1,0:T(8,128)(2,1)S(1)}, u32[]{:S(2)}, u32[]{:S(2)}) collective-permute-start(bf16[17,16,128]{2,1,0:T(8,128)(2,1)S(1)} %shard_map.127), channel_id=1, source_target_pairs={{0,24},{1,25},{2,26},{3,27},{4,28},{5,29},{6,30},{7,31},{8,16},{9,... | collective-permute-start | bytes 208904 | tf_op jit(solution)/shard_map/ppermute | solution.py:627
  7.3 6.6 %collective-permute-start.1 = (bf16[17,16,128]{2,1,0:T(8,128)(2,1)S(1)}, bf16[17,16,128]{2,1,0:T(8,128)(2,1)S(1)}, u32[]{:S(2)}, u32[]{:S(2)}) collective-permute-start(bf16[17,16,128]{2,1,0:T(8,128)(2,1)S(1)} %shard_map.127), channel_id=1, source_target_pairs={{0,16},{1,17},{2,18},{3,19},{4,20},{5,21},{6,22},{7,23},{8,24},{9,... | collective-permute-start | bytes 208904 | tf_op jit(solution)/shard_map/ppermute | solution.py:627
  7.3 6.6 %collective-permute-start = (bf16[17,16,128]{2,1,0:T(8,128)(2,1)S(1)}, bf16[17,16,128]{2,1,0:T(8,128)(2,1)S(1)}, u32[]{:S(2)}, u32[]{:S(2)}) collective-permute-start(bf16[17,16,128]{2,1,0:T(8,128)(2,1)S(1)} %shard_map.127), channel_id=1, source_target_pairs={{0,8},{1,9},{2,10},{3,11},{4,12},{5,13},{6,14},{7,15},{8,0},{9,1},... | collective-permute-start | bytes 208904 | tf_op jit(solution)/shard_map/ppermute | solution.py:627
  9.5 7.5 %collective-permute-start.8 = (bf16[32,16,128]{2,1,0:T(8,128)(2,1)S(1)}, bf16[32,16,128]{2,1,0:T(8,128)(2,1)S(1)}, u32[]{:S(2)}, u32[]{:S(2)}) collective-permute-start(bf16[32,16,128]{2,1,0:T(8,128)(2,1)S(1)} %shard_map.128), channel_id=1, source_target_pairs={{0,8},{1,9},{2,10},{3,11},{4,12},{5,13},{6,14},{7,15},{8,0},{9,1},... | collective-permute-start | bytes 393224 | tf_op jit(solution)/shard_map/ppermute | solution.py:627
  11.0 9.6 %collective-permute-start.7 = (bf16[32,16,128]{2,1,0:T(8,128)(2,1)S(1)}, bf16[32,16,128]{2,1,0:T(8,128)(2,1)S(1)}, u32[]{:S(2)}, u32[]{:S(2)}) collective-permute-start(bf16[32,16,128]{2,1,0:T(8,128)(2,1)S(1)} %shard_map.128), channel_id=1, source_target_pairs={{0,24},{1,25},{2,26},{3,27},{4,28},{5,29},{6,30},{7,31},{8,16},{9,... | collective-permute-start | bytes 393224 | tf_op jit(solution)/shard_map/ppermute | solution.py:627
  13.4 11.9 %collective-permute-start.6 = (bf16[32,16,128]{2,1,0:T(8,128)(2,1)S(1)}, bf16[32,16,128]{2,1,0:T(8,128)(2,1)S(1)}, u32[]{:S(2)}, u32[]{:S(2)}) collective-permute-start(bf16[32,16,128]{2,1,0:T(8,128)(2,1)S(1)} %shard_map.128), channel_id=1, source_target_pairs={{0,16},{1,17},{2,18},{3,19},{4,20},{5,21},{6,22},{7,23},{8,24},{9,... | collective-permute-start | bytes 393224 | tf_op jit(solution)/shard_map/ppermute | solution.py:627
  14.0 14.0 %collective-permute-start.5 = (bf16[4,17,16,128]{3,2,1,0:T(8,128)(2,1)S(1)}, bf16[4,17,16,128]{3,2,1,0:T(8,128)(2,1)S(1)}, u32[]{:S(2)}, u32[]{:S(2)}) collective-permute-start(bf16[4,17,16,128]{3,2,1,0:T(8,128)(2,1)S(1)} %pad_maximum_fusion.1.refs_0_), channel_id=1, source_target_pairs={{0,6},{1,7},{2,4},{3,5},{4,2},{5,3},{6,0},{7,1},{8,14},{9,15},{10,... | collective-permute-start | bytes 835592 | tf_op jit(solution)/shard_map/ppermute | solution.py:627
  16.5 12.2 %collective-permute-start.4 = (bf16[4,17,16,128]{3,2,1,0:T(8,128)(2,1)S(1)}, bf16[4,17,16,128]{3,2,1,0:T(8,128)(2,1)S(1)}, u32[]{:S(2)}, u32[]{:S(2)}) collective-permute-start(bf16[4,17,16,128]{3,2,1,0:T(8,128)(2,1)S(1)} %pad_maximum_fusion.1.refs_0_), channel_id=1, source_target_pairs={{0,4},{1,5},{2,6},{3,7},{4,0},{5,1},{6,2},{7,3},{8,12},{9,13},{10,... | collective-permute-start | bytes 835592 | tf_op jit(solution)/shard_map/ppermute | solution.py:627
  17.0 11.7 %collective-permute-start.3 = (bf16[4,17,16,128]{3,2,1,0:T(8,128)(2,1)S(1)}, bf16[4,17,16,128]{3,2,1,0:T(8,128)(2,1)S(1)}, u32[]{:S(2)}, u32[]{:S(2)}) collective-permute-start(bf16[4,17,16,128]{3,2,1,0:T(8,128)(2,1)S(1)} %pad_maximum_fusion.1.refs_0_), channel_id=1, source_target_pairs={{0,2},{1,3},{2,0},{3,1},{4,6},{5,7},{6,4},{7,5},{8,10},{9,11},{10,... | collective-permute-start | bytes 835592 | tf_op jit(solution)/shard_map/ppermute | solution.py:627
  28.7 22.9 %collective-permute-start.9 = (bf16[4,32,16,128]{3,2,1,0:T(8,128)(2,1)S(1)}, bf16[4,32,16,128]{3,2,1,0:T(8,128)(2,1)S(1)}, u32[]{:S(2)}, u32[]{:S(2)}) collective-permute-start(bf16[4,32,16,128]{3,2,1,0:T(8,128)(2,1)S(1)} %pad_maximum_fusion.refs_0_), channel_id=1, source_target_pairs={{0,6},{1,7},{2,4},{3,5},{4,2},{5,3},{6,0},{7,1},{8,14},{9,15},{10,... | collective-permute-start | bytes 1572872 | tf_op jit(solution)/shard_map/ppermute | solution.py:627
  31.5 2.2 %collective-permute-start.12 = (bf16[4,17,16,128]{3,2,1,0:T(8,128)(2,1)S(1)}, bf16[4,17,16,128]{3,2,1,0:T(8,128)(2,1)S(1)}, u32[]{:S(2)}, u32[]{:S(2)}) collective-permute-start(bf16[4,17,16,128]{3,2,1,0:T(8,128)(2,1)S(1)} %collective-permute-done.4.refs_2_), channel_id=1, source_target_pairs={{0,1},{1,0},{2,3},{3,2},{4,5},{5,4},{6,7},{7,6},{8,9},{9,8},{10,11... | collective-permute-start | bytes 835592 | tf_op jit(solution)/shard_map/ppermute | solution.py:627
  31.5 2.2 %collective-permute-start.13 = (bf16[4,17,16,128]{3,2,1,0:T(8,128)(2,1)S(1)}, bf16[4,17,16,128]{3,2,1,0:T(8,128)(2,1)S(1)}, u32[]{:S(2)}, u32[]{:S(2)}) collective-permute-start(bf16[4,17,16,128]{3,2,1,0:T(8,128)(2,1)S(1)} %collective-permute-done.5.refs_3_), channel_id=1, source_target_pairs={{0,1},{1,0},{2,3},{3,2},{4,5},{5,4},{6,7},{7,6},{8,9},{9,8},{10,11... | collective-permute-start | bytes 835592 | tf_op jit(solution)/shard_map/ppermute | solution.py:627
  32.6 22.1 %collective-permute-start.15 = (bf16[4,32,16,128]{3,2,1,0:T(8,128)(2,1)S(1)}, bf16[4,32,16,128]{3,2,1,0:T(8,128)(2,1)S(1)}, u32[]{:S(2)}, u32[]{:S(2)}) collective-permute-start(bf16[4,32,16,128]{3,2,1,0:T(8,128)(2,1)S(1)} %pad_maximum_fusion.refs_0_), channel_id=1, source_target_pairs={{0,4},{1,5},{2,6},{3,7},{4,0},{5,1},{6,2},{7,3},{8,12},{9,13},{10,... | collective-permute-start | bytes 1572872 | tf_op jit(solution)/shard_map/ppermute | solution.py:627
  33.1 21.5 %collective-permute-start.14 = (bf16[4,32,16,128]{3,2,1,0:T(8,128)(2,1)S(1)}, bf16[4,32,16,128]{3,2,1,0:T(8,128)(2,1)S(1)}, u32[]{:S(2)}, u32[]{:S(2)}) collective-permute-start(bf16[4,32,16,128]{3,2,1,0:T(8,128)(2,1)S(1)} %pad_maximum_fusion.refs_0_), channel_id=1, source_target_pairs={{0,2},{1,3},{2,0},{3,1},{4,6},{5,7},{6,4},{7,5},{8,10},{9,11},{10,... | collective-permute-start | bytes 1572872 | tf_op jit(solution)/shard_map/ppermute | solution.py:627
  49.8 4.9 %collective-permute-start.16 = (bf16[4,32,16,128]{3,2,1,0:T(8,128)(2,1)S(1)}, bf16[4,32,16,128]{3,2,1,0:T(8,128)(2,1)S(1)}, u32[]{:S(2)}, u32[]{:S(2)}) collective-permute-start(bf16[4,32,16,128]{3,2,1,0:T(8,128)(2,1)S(1)} %pad_maximum_fusion.refs_0_), channel_id=1, source_target_pairs={{0,1},{1,0},{2,3},{3,2},{4,5},{5,4},{6,7},{7,6},{8,9},{9,8},{10,11... | collective-permute-start | bytes 1572872 | tf_op jit(solution)/shard_map/ppermute | solution.py:627
  51.6 3.0 %collective-permute-start.17 = (bf16[4,32,16,128]{3,2,1,0:T(8,128)(2,1)S(1)}, bf16[4,32,16,128]{3,2,1,0:T(8,128)(2,1)S(1)}, u32[]{:S(2)}, u32[]{:S(2)}) collective-permute-start(bf16[4,32,16,128]{3,2,1,0:T(8,128)(2,1)S(1)} %collective-permute-done.9.refs_3_), channel_id=1, source_target_pairs={{0,1},{1,0},{2,3},{3,2},{4,5},{5,4},{6,7},{7,6},{8,9},{9,8},{10,11... | collective-permute-start | bytes 1572872 | tf_op jit(solution)/shard_map/ppermute | solution.py:627
  54.7 2.6 %collective-permute-start.19 = (bf16[4,32,16,128]{3,2,1,0:T(8,128)(2,1)S(1)}, bf16[4,32,16,128]{3,2,1,0:T(8,128)(2,1)S(1)}, u32[]{:S(2)}, u32[]{:S(2)}) collective-permute-start(bf16[4,32,16,128]{3,2,1,0:T(8,128)(2,1)S(1)} %collective-permute-done.15.refs_2_), channel_id=1, source_target_pairs={{0,1},{1,0},{2,3},{3,2},{4,5},{5,4},{6,7},{7,6},{8,9},{9,8},{10,11... | collective-permute-start | bytes 1572872 | tf_op jit(solution)/shard_map/ppermute | solution.py:627
  77.1 5.1 %collective-permute-start.20 = (bf16[16,33,16,128]{3,2,1,0:T(8,128)(2,1)S(1)}, bf16[16,33,16,128]{3,2,1,0:T(8,128)(2,1)S(1)}, u32[]{:S(2)}, u32[]{:S(2)}) collective-permute-start(bf16[16,33,16,128]{3,2,1,0:T(8,128)(2,1)S(1)} %get-tuple-element.146), channel_id=1, source_target_pairs={{0,1},{1,0},{2,3},{3,2},{4,5},{5,4},{6,7},{7,6},{8,9},{9,8},{10,11... | collective-permute-start | bytes 6488072 | tf_op jit(solution)/shard_map/ppermute | solution.py:627
  77.3 4.9 %collective-permute-start.21 = (f32[4,16,16,128]{3,2,1,0:T(8,128)S(1)}, f32[4,16,16,128]{3,2,1,0:T(8,128)S(1)}, u32[]{:S(2)}, u32[]{:S(2)}) collective-permute-start(f32[4,16,16,128]{3,2,1,0:T(8,128)S(1)} %get-tuple-element.147), channel_id=1, source_target_pairs={{0,1},{1,0},{2,3},{3,2},{4,5},{5,4},{6,7},{7,6},{8,9},{9,8},{10,11... | collective-permute-start | bytes 1572872 | tf_op jit(solution)/shard_map/ppermute | solution.py:627
  83.2 30.2 %collective-permute-start.23 = (bf16[148,16,128]{2,1,0:T(8,128)(2,1)S(1)}, bf16[148,16,128]{2,1,0:T(8,128)(2,1)S(1)}, u32[]{:S(2)}, u32[]{:S(2)}) collective-permute-start(bf16[148,16,128]{2,1,0:T(8,128)(2,1)S(1)} %get-tuple-element.171), channel_id=1, source_target_pairs={{0,2},{1,3},{2,0},{3,1},{4,6},{5,7},{6,4},{7,5},{8,10},{9,11},{10,... | collective-permute-start | bytes 1818632 | tf_op jit(solution)/shard_map/ppermute | solution.py:627
  84.6 28.7 %collective-permute-start.24 = (bf16[148,16,128]{2,1,0:T(8,128)(2,1)S(1)}, bf16[148,16,128]{2,1,0:T(8,128)(2,1)S(1)}, u32[]{:S(2)}, u32[]{:S(2)}) collective-permute-start(bf16[148,16,128]{2,1,0:T(8,128)(2,1)S(1)} %get-tuple-element.172), channel_id=1, source_target_pairs={{0,4},{1,5},{2,6},{3,7},{4,0},{5,1},{6,2},{7,3},{8,12},{9,13},{10,... | collective-permute-start | bytes 1818632 | tf_op jit(solution)/shard_map/ppermute | solution.py:627
  86.1 27.3 %collective-permute-start.25 = (bf16[148,16,128]{2,1,0:T(8,128)(2,1)S(1)}, bf16[148,16,128]{2,1,0:T(8,128)(2,1)S(1)}, u32[]{:S(2)}, u32[]{:S(2)}) collective-permute-start(bf16[148,16,128]{2,1,0:T(8,128)(2,1)S(1)} %get-tuple-element.173), channel_id=1, source_target_pairs={{0,6},{1,7},{2,4},{3,5},{4,2},{5,3},{6,0},{7,1},{8,14},{9,15},{10,... | collective-permute-start | bytes 1818632 | tf_op jit(solution)/shard_map/ppermute | solution.py:627
  110.1 3.5 %collective-permute-start.22 = (f32[3080,128]{1,0:T(8,128)S(1)}, f32[3080,128]{1,0:T(8,128)S(1)}, u32[]{:S(2)}, u32[]{:S(2)}) collective-permute-start(f32[3080,128]{1,0:T(8,128)S(1)} %get-tuple-element.165), channel_id=1, source_target_pairs={{0,1},{1,0},{2,3},{3,2},{4,5},{5,4},{6,7},{7,6},{8,9},{9,8},{10,11... | collective-permute-start | bytes 4730888 | tf_op jit(solution)/shard_map/ppermute | solution.py:627
  114.3 7.2 %collective-permute-start.26 = (bf16[49,16,128]{2,1,0:T(8,128)(2,1)S(1)}, bf16[49,16,128]{2,1,0:T(8,128)(2,1)S(1)}, u32[]{:S(2)}, u32[]{:S(2)}) collective-permute-start(bf16[49,16,128]{2,1,0:T(8,128)(2,1)S(1)} %get-tuple-element.186), channel_id=1, source_target_pairs={{0,2},{1,3},{2,0},{3,1},{4,6},{5,7},{6,4},{7,5},{8,10},{9,11},{10,... | collective-permute-start | bytes 602120 | tf_op jit(solution)/shard_map/ppermute | solution.py:627
  115.8 7.9 %collective-permute-start.27 = (bf16[49,16,128]{2,1,0:T(8,128)(2,1)S(1)}, bf16[49,16,128]{2,1,0:T(8,128)(2,1)S(1)}, u32[]{:S(2)}, u32[]{:S(2)}) collective-permute-start(bf16[49,16,128]{2,1,0:T(8,128)(2,1)S(1)} %get-tuple-element.187), channel_id=1, source_target_pairs={{0,4},{1,5},{2,6},{3,7},{4,0},{5,1},{6,2},{7,3},{8,12},{9,13},{10,... | collective-permute-start | bytes 602120 | tf_op jit(solution)/shard_map/ppermute | solution.py:627
  117.2 9.8 %collective-permute-start.28 = (bf16[49,16,128]{2,1,0:T(8,128)(2,1)S(1)}, bf16[49,16,128]{2,1,0:T(8,128)(2,1)S(1)}, u32[]{:S(2)}, u32[]{:S(2)}) collective-permute-start(bf16[49,16,128]{2,1,0:T(8,128)(2,1)S(1)} %get-tuple-element.188), channel_id=1, source_target_pairs={{0,6},{1,7},{2,4},{3,5},{4,2},{5,3},{6,0},{7,1},{8,14},{9,15},{10,... | collective-permute-start | bytes 602120 | tf_op jit(solution)/shard_map/ppermute | solution.py:627
  118.7 10.5 %collective-permute-start.32 = (bf16[33,16,128]{2,1,0:T(8,128)(2,1)S(1)}, bf16[33,16,128]{2,1,0:T(8,128)(2,1)S(1)}, u32[]{:S(2)}, u32[]{:S(2)}) collective-permute-start(bf16[33,16,128]{2,1,0:T(8,128)(2,1)S(1)} %get-tuple-element.194), channel_id=1, source_target_pairs={{0,8},{1,9},{2,10},{3,11},{4,12},{5,13},{6,14},{7,15},{8,0},{9,1},... | collective-permute-start | bytes 405512 | tf_op jit(solution)/shard_map/ppermute | solution.py:627
  119.2 13.6 %collective-permute-start.33 = (bf16[33,16,128]{2,1,0:T(8,128)(2,1)S(1)}, bf16[33,16,128]{2,1,0:T(8,128)(2,1)S(1)}, u32[]{:S(2)}, u32[]{:S(2)}) collective-permute-start(bf16[33,16,128]{2,1,0:T(8,128)(2,1)S(1)} %get-tuple-element.195), channel_id=1, source_target_pairs={{0,16},{1,17},{2,18},{3,19},{4,20},{5,21},{6,22},{7,23},{8,24},{9,... | collective-permute-start | bytes 405512 | tf_op jit(solution)/shard_map/ppermute | solution.py:627
  121.5 11.3 %collective-permute-start.34 = (bf16[33,16,128]{2,1,0:T(8,128)(2,1)S(1)}, bf16[33,16,128]{2,1,0:T(8,128)(2,1)S(1)}, u32[]{:S(2)}, u32[]{:S(2)}) collective-permute-start(bf16[33,16,128]{2,1,0:T(8,128)(2,1)S(1)} %get-tuple-element.196), channel_id=1, source_target_pairs={{0,24},{1,25},{2,26},{3,27},{4,28},{5,29},{6,30},{7,31},{8,16},{9,... | collective-permute-start | bytes 405512 | tf_op jit(solution)/shard_map/ppermute | solution.py:627
  127.7 6.5 %collective-permute-start.29 = (bf16[17,16,128]{2,1,0:T(8,128)(2,1)S(1)}, bf16[17,16,128]{2,1,0:T(8,128)(2,1)S(1)}, u32[]{:S(2)}, u32[]{:S(2)}) collective-permute-start(bf16[17,16,128]{2,1,0:T(8,128)(2,1)S(1)} %get-tuple-element.203), channel_id=1, source_target_pairs={{0,8},{1,9},{2,10},{3,11},{4,12},{5,13},{6,14},{7,15},{8,0},{9,1},... | collective-permute-start | bytes 208904 | tf_op jit(solution)/shard_map/ppermute | solution.py:627
  128.2 10.5 %collective-permute-start.30 = (bf16[17,16,128]{2,1,0:T(8,128)(2,1)S(1)}, bf16[17,16,128]{2,1,0:T(8,128)(2,1)S(1)}, u32[]{:S(2)}, u32[]{:S(2)}) collective-permute-start(bf16[17,16,128]{2,1,0:T(8,128)(2,1)S(1)} %get-tuple-element.204), channel_id=1, source_target_pairs={{0,16},{1,17},{2,18},{3,19},{4,20},{5,21},{6,22},{7,23},{8,24},{9,... | collective-permute-start | bytes 208904 | tf_op jit(solution)/shard_map/ppermute | solution.py:627
  129.2 9.5 %collective-permute-start.31 = (bf16[17,16,128]{2,1,0:T(8,128)(2,1)S(1)}, bf16[17,16,128]{2,1,0:T(8,128)(2,1)S(1)}, u32[]{:S(2)}, u32[]{:S(2)}) collective-permute-start(bf16[17,16,128]{2,1,0:T(8,128)(2,1)S(1)} %get-tuple-element.205), channel_id=1, source_target_pairs={{0,24},{1,25},{2,26},{3,27},{4,28},{5,29},{6,30},{7,31},{8,16},{9,... | collective-permute-start | bytes 208904 | tf_op jit(solution)/shard_map/ppermute | solution.py:627
  (12 other events, 77.2 us)

commit v4 on v3

--- a/solution.py
+++ b/solution.py
@@ -25,7 +25,7 @@
 F32 = jnp.float32
 CHUNK = 64
 SHARE = 12 * 64
-BIG = 512
+BIG = 1024
 VMEM = pl.BlockSpec(memory_space=pltpu.VMEM)
 SMEM = pl.BlockSpec(memory_space=pltpu.SMEM)
 ANY = pl.BlockSpec(memory_space=pl.ANY)

time: 140 us -> 140 us (level)
  transfers between devices with their start and end apart: 35 -> 35, of which waited for: 14 -> 15; matrix products, arithmetic and copies ran while one was open for 0% -> 0% of each run, Pallas kernels for 38% -> 38%
where the time goes in v4:
time: 140 us
  Pallas kernels  75.7 us (54%)
  starting transfers between devices  35.3 us (25%)
  waiting for transfers between devices  25.1 us (18%)
  local copies, waits for them, and re-layouts  2.51 us (2%)
    ppermute x35, starting transfers between devices, swap(): return lax.ppermute(x, AXES, [(i, i ^ bit) for i in range(n)])  35.3 us
    ppermute x35, waiting for transfers between devices, swap(): return lax.ppermute(x, AXES, [(i, i ^ bit) for i in range(n)])  25.1 us
    pallas_call x1, Pallas kernels, local(): call(back_body, [(row, BF)] * 3 + [((4 * SHARE + 8, 128), F32)] * 2, [SME...  23 us
    pallas_call x1, Pallas kernels, local(): call(feed_body, [(row, BF, ANY), (row, F32), (row, BF)] + [((n // 2, G_TI...  19.7 us
    pallas_call x1, Pallas kernels, local(): call(attend_body, [(row, BF), ((D + 16, ROWS), BF), ((8, ROWS), F32)], [V...  13.4 us
    pallas_call x6, Pallas kernels, small(): return call(body, outs, ins, scratch, 2 * size, 6 * size, 16)(*args)  3.93 us
    pallas_call x1, Pallas kernels, local(): call(input_body, [(row, F32)], [VMEM] * 5, [], 32 << 30, 1000, 24)  3.15 us
    pallas_call x1, Pallas kernels, local(): call(back_first_body, [(half, F32)] + sums, [VMEM] * 5, buffers, 1000, 10...  3.09 us
  transfers between devices with their start and end apart: 35, of which 15 were waited for; matrix products, arithmetic and copies ran while one was open for 0% of the time, Pallas kernels for 38%

profile of v4, /device:TPU:0, one launch (start us, length us, event | category | flops | bytes accessed | tf_op | source)
XLA Modules:
  0.0 139.8 jit_solution(669799904702785956)
XLA Ops:
  2.2 5.1 %collective-permute-start.2 = (bf16[17,16,128]{2,1,0:T(8,128)(2,1)S(1)}, bf16[17,16,128]{2,1,0:T(8,128)(2,1)S(1)}, u32[]{:S(2)}, u32[]{:S(2)}) collective-permute-start(bf16[17,16,128]{2,1,0:T(8,128)(2,1)S(1)} %shard_map.127), channel_id=1, source_target_pairs={{0,24},{1,25},{2,26},{3,27},{4,28},{5,29},{6,30},{7,31},{8,16},{9,... | collective-permute-start | bytes 208904 | tf_op jit(solution)/shard_map/ppermute | solution.py:627
  9.5 1.5 %collective-permute-start.8 = (bf16[32,16,128]{2,1,0:T(8,128)(2,1)S(1)}, bf16[32,16,128]{2,1,0:T(8,128)(2,1)S(1)}, u32[]{:S(2)}, u32[]{:S(2)}) collective-permute-start(bf16[32,16,128]{2,1,0:T(8,128)(2,1)S(1)} %shard_map.128), channel_id=1, source_target_pairs={{0,8},{1,9},{2,10},{3,11},{4,12},{5,13},{6,14},{7,15},{8,0},{9,1},... | collective-permute-start | bytes 393224 | tf_op jit(solution)/shard_map/ppermute | solution.py:627
  11.0 2.4 %collective-permute-start.7 = (bf16[32,16,128]{2,1,0:T(8,128)(2,1)S(1)}, bf16[32,16,128]{2,1,0:T(8,128)(2,1)S(1)}, u32[]{:S(2)}, u32[]{:S(2)}) collective-permute-start(bf16[32,16,128]{2,1,0:T(8,128)(2,1)S(1)} %shard_map.128), channel_id=1, source_target_pairs={{0,24},{1,25},{2,26},{3,27},{4,28},{5,29},{6,30},{7,31},{8,16},{9,... | collective-permute-start | bytes 393224 | tf_op jit(solution)/shard_map/ppermute | solution.py:627
  14.0 2.5 %collective-permute-start.5 = (bf16[4,17,16,128]{3,2,1,0:T(8,128)(2,1)S(1)}, bf16[4,17,16,128]{3,2,1,0:T(8,128)(2,1)S(1)}, u32[]{:S(2)}, u32[]{:S(2)}) collective-permute-start(bf16[4,17,16,128]{3,2,1,0:T(8,128)(2,1)S(1)} %pad_maximum_fusion.1.refs_0_), channel_id=1, source_target_pairs={{0,6},{1,7},{2,4},{3,5},{4,2},{5,3},{6,0},{7,1},{8,14},{9,15},{10,... | collective-permute-start | bytes 835592 | tf_op jit(solution)/shard_map/ppermute | solution.py:627
  18.0 2.6 %collective-permute-done.7 = bf16[32,16,128]{2,1,0:T(8,128)(2,1)S(1)} collective-permute-done((bf16[32,16,128]{2,1,0:T(8,128)(2,1)S(1)}, bf16[32,16,128]{2,1,0:T(8,128)(2,1)S(1)}, u32[]{:S(2)}, u32[]{:S(2)}) %collective-permute-start.7) | collective-permute-done | bytes 131104 | tf_op jit(solution)/shard_map/ppermute | solution.py:627
  20.6 4.6 %collective-permute-done.6 = bf16[32,16,128]{2,1,0:T(8,128)(2,1)S(1)} collective-permute-done((bf16[32,16,128]{2,1,0:T(8,128)(2,1)S(1)}, bf16[32,16,128]{2,1,0:T(8,128)(2,1)S(1)}, u32[]{:S(2)}, u32[]{:S(2)}) %collective-permute-start.6) | collective-permute-done | bytes 131104 | tf_op jit(solution)/shard_map/ppermute | solution.py:627
  25.2 1.1 shard_map.129.place
  26.4 1.5 %shard_map.130 = (bf16[2,1024,128]{2,1,0:T(8,128)(2,1)S(1)}, bf16[2,1024,128]{2,1,0:T(8,128)(2,1)S(1)}, bf16[528,1024]{1,0:T(8,128)(2,1)S(1)}) custom-call(s32[1,3]{1,0:T(1,128)S(1)} %copy-done.5, s32[1,8]{1,0:T(1,128)S(1)} %copy-done.6, bf16[1024,512]{1,0:T(8,128)(2,1)S(1)} %copy-done), custom_call_target="tpu_custom_call" | custom-call | flops 1000 | bytes 1000 | tf_op jit(solution)/shard_map/pallas_call | solution.py:757
  28.7 2.3 %collective-permute-start.9 = (bf16[4,32,16,128]{3,2,1,0:T(8,128)(2,1)S(1)}, bf16[4,32,16,128]{3,2,1,0:T(8,128)(2,1)S(1)}, u32[]{:S(2)}, u32[]{:S(2)}) collective-permute-start(bf16[4,32,16,128]{3,2,1,0:T(8,128)(2,1)S(1)} %pad_maximum_fusion.refs_0_), channel_id=1, source_target_pairs={{0,6},{1,7},{2,4},{3,5},{4,2},{5,3},{6,0},{7,1},{8,14},{9,15},{10,... | collective-permute-start | bytes 1572872 | tf_op jit(solution)/shard_map/ppermute | solution.py:627
  33.8 2.6 %shard_map.131 = (bf16[8,1024,128]{2,1,0:T(8,128)(2,1)S(1)}, bf16[8,1024,128]{2,1,0:T(8,128)(2,1)S(1)}, bf16[1024,512]{1,0:T(8,128)(2,1)S(1)}, bf16[32,17,16,128]{3,2,1,0:T(8,128)(2,1)S(1)}, f32[1,4096]{1,0:T(1,128)S(1)}) custom-call(s32[5]{0:T(128)S(1)} %shard_map.129.place, bf16[1024,512]{1,0:T(8,128)(2,1)S(1)} %copy-done, ...), custom_call_target="tpu_custom_call" | custom-call | flops 1000 | bytes 1000 | tf_op jit(solution)/shard_map/pallas_call | solution.py:788
  36.4 13.4 %shard_map.132 = (bf16[1024,512]{1,0:T(8,128)(2,1)S(1)}, bf16[528,1024]{1,0:T(8,128)(2,1)S(1)}, f32[8,1024]{1,0:T(8,128)S(1)}) custom-call(bf16[8,1024,128]{2,1,0:T(8,128)(2,1)S(1)} %get-tuple-element.160.q_all, bf16[8,1024,128]{2,1,0:T(8,128)(2,1)S(1)} %get-tuple-element.127.k_all, bf16[1024,512]{1,0:T(8,128)(2,1)S(1)} %get-tuple-element.128.v_all), custom_call_target="tpu_custom_call" | custom-call | flops 1000 | bytes 1000 | tf_op jit(solution)/shard_map/pallas_call | solution.py:793
  50.0 1.6 %shard_map.133 = (f32[1024,512]{1,0:T(8,128)S(1)}, bf16[1024,512]{1,0:T(8,128)(2,1)S(1)}, bf16[528,1024]{1,0:T(8,128)(2,1)S(1)}, bf16[1024,512]{1,0:T(8,128)(2,1)S(1)}) custom-call(f32[2]{0:T(128)S(1)} %copy-done.8, bf16[1024,512]{1,0:T(8,128)(2,1)S(1)} %copy-done, bf16[1024,512]{1,0:T(8,128)(2,1)S(1)} %copy-done.2, ...), custom_call_target="tpu_custom_call" | custom-call | flops 1000 | bytes 1000 | tf_op jit(solution)/shard_map/pallas_call | solution.py:800
  52.1 2.6 %collective-permute-done.15.refs_2_ = bf16[4,32,16,128]{3,2,1,0:T(8,128)(2,1)S(1)} collective-permute-done((bf16[4,32,16,128]{3,2,1,0:T(8,128)(2,1)S(1)}, bf16[4,32,16,128]{3,2,1,0:T(8,128)(2,1)S(1)}, u32[]{:S(2)}, u32[]{:S(2)}) %collective-permute-start.15) | collective-permute-done | bytes 524320 | tf_op jit(solution)/shard_map/ppermute | solution.py:627
  55.2 1.4 %collective-permute-done.18.refs_5_ = bf16[4,32,16,128]{3,2,1,0:T(8,128)(2,1)S(1)} collective-permute-done((bf16[4,32,16,128]{3,2,1,0:T(8,128)(2,1)S(1)}, bf16[4,32,16,128]{3,2,1,0:T(8,128)(2,1)S(1)}, u32[]{:S(2)}, u32[]{:S(2)}) %collective-permute-start.18) | collective-permute-done | bytes 524320 | tf_op jit(solution)/shard_map/ppermute | solution.py:627
  57.4 19.7 %shard_map.134 = (bf16[1024,512]{1,0:T(8,128)(2,1)}, f32[1024,512]{1,0:T(8,128)S(1)}, bf16[1024,512]{1,0:T(8,128)(2,1)S(1)}, f32[16,33,16,128]{3,2,1,0:T(8,128)}...) custom-call(s32[5]{0:T(128)S(1)} %shard_map.129.place, ...), custom_call_target="tpu_custom_call" | custom-call | flops 17179869184 | bytes 31457280 | tf_op jit(solution)/shard_map/pallas_call | solution.py:811
  77.7 3.1 %shard_map.135 = (f32[64,1024]{1,0:T(8,128)S(1)}, f32[1024,128]{1,0:T(8,128)S(1)}, f32[1024,128]{1,0:T(8,128)S(1)}) custom-call(bf16[8,1024,128]{2,1,0:T(8,128)(2,1)S(1)} %get-tuple-element.160.q_all, bf16[8,1024,128]{2,1,0:T(8,128)(2,1)S(1)} %get-tuple-element.127.k_all, bf16[1024,512]{1,0:T(8,128)(2,1)S(1)} %get-tuple-element.128.v_all, ...), custom_call_target="tpu_custom_call" | custom-call | flops 1000 | bytes 1000 | tf_op jit(solution)/shard_map/pallas_call | solution.py:830
  80.8 1.4 collective-permute-done.21.wo_got
  82.2 1.0 shard_map.136
  83.2 1.4 %collective-permute-start.23 = (bf16[148,16,128]{2,1,0:T(8,128)(2,1)S(1)}, bf16[148,16,128]{2,1,0:T(8,128)(2,1)S(1)}, u32[]{:S(2)}, u32[]{:S(2)}) collective-permute-start(bf16[148,16,128]{2,1,0:T(8,128)(2,1)S(1)} %get-tuple-element.171), channel_id=1, source_target_pairs={{0,2},{1,3},{2,0},{3,1},{4,6},{5,7},{6,4},{7,5},{8,10},{9,11},{10,... | collective-permute-start | bytes 1818632 | tf_op jit(solution)/shard_map/ppermute | solution.py:627
  84.6 1.5 %collective-permute-start.24 = (bf16[148,16,128]{2,1,0:T(8,128)(2,1)S(1)}, bf16[148,16,128]{2,1,0:T(8,128)(2,1)S(1)}, u32[]{:S(2)}, u32[]{:S(2)}) collective-permute-start(bf16[148,16,128]{2,1,0:T(8,128)(2,1)S(1)} %get-tuple-element.172), channel_id=1, source_target_pairs={{0,4},{1,5},{2,6},{3,7},{4,0},{5,1},{6,2},{7,3},{8,12},{9,13},{10,... | collective-permute-start | bytes 1818632 | tf_op jit(solution)/shard_map/ppermute | solution.py:627
  86.7 23.0 %shard_map.137 = (bf16[1024,512]{1,0:T(8,128)(2,1)S(1)}, bf16[1024,512]{1,0:T(8,128)(2,1)S(1)}, bf16[1024,512]{1,0:T(8,128)(2,1)S(1)}, f32[3080,128]{1,0:T(8,128)S(1)}, f32[3080,128]{1,0:T(8,128)S(1)}) custom-call(s32[5]{0:T(128)S(1)} %shard_map.129.place, bf16[8,1024,128]{2,1,0:T(8,128)(2,1)S(1)} %get-tuple-element.160.q_all, ...), custom_call_target="tpu_custom_call" | custom-call | flops 1000 | bytes 1000 | tf_op jit(solution)/shard_map/pallas_call | solution.py:838
  109.9 3.1 %shard_map.138 = f32[1024,512]{1,0:T(8,128)} custom-call(f32[1024,512]{1,0:T(8,128)S(1)} %get-tuple-element.166.gm, bf16[1024,512]{1,0:T(8,128)(2,1)S(1)} %get-tuple-element.167.dq, bf16[1024,512]{1,0:T(8,128)(2,1)S(1)} %get-tuple-element.168.dk, bf16[1024,512]{1,0:T(8,128)(2,1)S(1)} %get-tuple-element.169.dv, ...), custom_call_target="tpu_custom_call" | custom-call | flops 34359738368 | bytes 1000 | tf_op jit(solution)/shard_map/pallas_call | solution.py:847
  114.0 1.4 %collective-permute-start.26 = (bf16[49,16,128]{2,1,0:T(8,128)(2,1)S(1)}, bf16[49,16,128]{2,1,0:T(8,128)(2,1)S(1)}, u32[]{:S(2)}, u32[]{:S(2)}) collective-permute-start(bf16[49,16,128]{2,1,0:T(8,128)(2,1)S(1)} %get-tuple-element.186), channel_id=1, source_target_pairs={{0,2},{1,3},{2,0},{3,1},{4,6},{5,7},{6,4},{7,5},{8,10},{9,11},{10,... | collective-permute-start | bytes 602120 | tf_op jit(solution)/shard_map/ppermute | solution.py:627
  115.4 1.5 %collective-permute-start.27 = (bf16[49,16,128]{2,1,0:T(8,128)(2,1)S(1)}, bf16[49,16,128]{2,1,0:T(8,128)(2,1)S(1)}, u32[]{:S(2)}, u32[]{:S(2)}) collective-permute-start(bf16[49,16,128]{2,1,0:T(8,128)(2,1)S(1)} %get-tuple-element.187), channel_id=1, source_target_pairs={{0,4},{1,5},{2,6},{3,7},{4,0},{5,1},{6,2},{7,3},{8,12},{9,13},{10,... | collective-permute-start | bytes 602120 | tf_op jit(solution)/shard_map/ppermute | solution.py:627
  118.9 1.1 collective-permute-start.33
  120.0 1.2 collective-permute-done.26.g1
  121.2 1.7 %collective-permute-start.34 = (bf16[33,16,128]{2,1,0:T(8,128)(2,1)S(1)}, bf16[33,16,128]{2,1,0:T(8,128)(2,1)S(1)}, u32[]{:S(2)}, u32[]{:S(2)}) collective-permute-start(bf16[33,16,128]{2,1,0:T(8,128)(2,1)S(1)} %get-tuple-element.196), channel_id=1, source_target_pairs={{0,24},{1,25},{2,26},{3,27},{4,28},{5,29},{6,30},{7,31},{8,16},{9,... | collective-permute-start | bytes 405512 | tf_op jit(solution)/shard_map/ppermute | solution.py:627
  123.3 3.4 %collective-permute-done.28.g3 = bf16[49,16,128]{2,1,0:T(8,128)(2,1)S(1)} collective-permute-done((bf16[49,16,128]{2,1,0:T(8,128)(2,1)S(1)}, bf16[49,16,128]{2,1,0:T(8,128)(2,1)S(1)}, u32[]{:S(2)}, u32[]{:S(2)}) %collective-permute-start.28) | collective-permute-done | bytes 200736 | tf_op jit(solution)/shard_map/ppermute | solution.py:627
  128.8 3.0 %collective-permute-start.31 = (bf16[17,16,128]{2,1,0:T(8,128)(2,1)S(1)}, bf16[17,16,128]{2,1,0:T(8,128)(2,1)S(1)}, u32[]{:S(2)}, u32[]{:S(2)}) collective-permute-start(bf16[17,16,128]{2,1,0:T(8,128)(2,1)S(1)} %get-tuple-element.205), channel_id=1, source_target_pairs={{0,24},{1,25},{2,26},{3,27},{4,28},{5,29},{6,30},{7,31},{8,16},{9,... | collective-permute-start | bytes 208904 | tf_op jit(solution)/shard_map/ppermute | solution.py:627
  132.5 1.4 shard_map.142
  133.9 4.5 %collective-permute-done.30.a2 = bf16[17,16,128]{2,1,0:T(8,128)(2,1)S(1)} collective-permute-done((bf16[17,16,128]{2,1,0:T(8,128)(2,1)S(1)}, bf16[17,16,128]{2,1,0:T(8,128)(2,1)S(1)}, u32[]{:S(2)}, u32[]{:S(2)}) %collective-permute-start.30) | collective-permute-done | bytes 69664 | tf_op jit(solution)/shard_map/ppermute | solution.py:627
  138.3 1.2 shard_map.143
  (76 shorter events, 18.8 us)
Async XLA Ops:
  2.2 11.2 %collective-permute-start.2 = (bf16[17,16,128]{2,1,0:T(8,128)(2,1)S(1)}, bf16[17,16,128]{2,1,0:T(8,128)(2,1)S(1)}, u32[]{:S(2)}, u32[]{:S(2)}) collective-permute-start(bf16[17,16,128]{2,1,0:T(8,128)(2,1)S(1)} %shard_map.127), channel_id=1, source_target_pairs={{0,24},{1,25},{2,26},{3,27},{4,28},{5,29},{6,30},{7,31},{8,16},{9,... | collective-permute-start | bytes 208904 | tf_op jit(solution)/shard_map/ppermute | solution.py:627
  7.3 6.6 %collective-permute-start.1 = (bf16[17,16,128]{2,1,0:T(8,128)(2,1)S(1)}, bf16[17,16,128]{2,1,0:T(8,128)(2,1)S(1)}, u32[]{:S(2)}, u32[]{:S(2)}) collective-permute-start(bf16[17,16,128]{2,1,0:T(8,128)(2,1)S(1)} %shard_map.127), channel_id=1, source_target_pairs={{0,16},{1,17},{2,18},{3,19},{4,20},{5,21},{6,22},{7,23},{8,24},{9,... | collective-permute-start | bytes 208904 | tf_op jit(solution)/shard_map/ppermute | solution.py:627
  7.3 6.6 %collective-permute-start = (bf16[17,16,128]{2,1,0:T(8,128)(2,1)S(1)}, bf16[17,16,128]{2,1,0:T(8,128)(2,1)S(1)}, u32[]{:S(2)}, u32[]{:S(2)}) collective-permute-start(bf16[17,16,128]{2,1,0:T(8,128)(2,1)S(1)} %shard_map.127), channel_id=1, source_target_pairs={{0,8},{1,9},{2,10},{3,11},{4,12},{5,13},{6,14},{7,15},{8,0},{9,1},... | collective-permute-start | bytes 208904 | tf_op jit(solution)/shard_map/ppermute | solution.py:627
  9.5 7.5 %collective-permute-start.8 = (bf16[32,16,128]{2,1,0:T(8,128)(2,1)S(1)}, bf16[32,16,128]{2,1,0:T(8,128)(2,1)S(1)}, u32[]{:S(2)}, u32[]{:S(2)}) collective-permute-start(bf16[32,16,128]{2,1,0:T(8,128)(2,1)S(1)} %shard_map.128), channel_id=1, source_target_pairs={{0,8},{1,9},{2,10},{3,11},{4,12},{5,13},{6,14},{7,15},{8,0},{9,1},... | collective-permute-start | bytes 393224 | tf_op jit(solution)/shard_map/ppermute | solution.py:627
  11.0 9.6 %collective-permute-start.7 = (bf16[32,16,128]{2,1,0:T(8,128)(2,1)S(1)}, bf16[32,16,128]{2,1,0:T(8,128)(2,1)S(1)}, u32[]{:S(2)}, u32[]{:S(2)}) collective-permute-start(bf16[32,16,128]{2,1,0:T(8,128)(2,1)S(1)} %shard_map.128), channel_id=1, source_target_pairs={{0,24},{1,25},{2,26},{3,27},{4,28},{5,29},{6,30},{7,31},{8,16},{9,... | collective-permute-start | bytes 393224 | tf_op jit(solution)/shard_map/ppermute | solution.py:627
  13.4 11.9 %collective-permute-start.6 = (bf16[32,16,128]{2,1,0:T(8,128)(2,1)S(1)}, bf16[32,16,128]{2,1,0:T(8,128)(2,1)S(1)}, u32[]{:S(2)}, u32[]{:S(2)}) collective-permute-start(bf16[32,16,128]{2,1,0:T(8,128)(2,1)S(1)} %shard_map.128), channel_id=1, source_target_pairs={{0,16},{1,17},{2,18},{3,19},{4,20},{5,21},{6,22},{7,23},{8,24},{9,... | collective-permute-start | bytes 393224 | tf_op jit(solution)/shard_map/ppermute | solution.py:627
  14.0 14.0 %collective-permute-start.5 = (bf16[4,17,16,128]{3,2,1,0:T(8,128)(2,1)S(1)}, bf16[4,17,16,128]{3,2,1,0:T(8,128)(2,1)S(1)}, u32[]{:S(2)}, u32[]{:S(2)}) collective-permute-start(bf16[4,17,16,128]{3,2,1,0:T(8,128)(2,1)S(1)} %pad_maximum_fusion.1.refs_0_), channel_id=1, source_target_pairs={{0,6},{1,7},{2,4},{3,5},{4,2},{5,3},{6,0},{7,1},{8,14},{9,15},{10,... | collective-permute-start | bytes 835592 | tf_op jit(solution)/shard_map/ppermute | solution.py:627
  16.5 12.2 %collective-permute-start.4 = (bf16[4,17,16,128]{3,2,1,0:T(8,128)(2,1)S(1)}, bf16[4,17,16,128]{3,2,1,0:T(8,128)(2,1)S(1)}, u32[]{:S(2)}, u32[]{:S(2)}) collective-permute-start(bf16[4,17,16,128]{3,2,1,0:T(8,128)(2,1)S(1)} %pad_maximum_fusion.1.refs_0_), channel_id=1, source_target_pairs={{0,4},{1,5},{2,6},{3,7},{4,0},{5,1},{6,2},{7,3},{8,12},{9,13},{10,... | collective-permute-start | bytes 835592 | tf_op jit(solution)/shard_map/ppermute | solution.py:627
  17.0 11.7 %collective-permute-start.3 = (bf16[4,17,16,128]{3,2,1,0:T(8,128)(2,1)S(1)}, bf16[4,17,16,128]{3,2,1,0:T(8,128)(2,1)S(1)}, u32[]{:S(2)}, u32[]{:S(2)}) collective-permute-start(bf16[4,17,16,128]{3,2,1,0:T(8,128)(2,1)S(1)} %pad_maximum_fusion.1.refs_0_), channel_id=1, source_target_pairs={{0,2},{1,3},{2,0},{3,1},{4,6},{5,7},{6,4},{7,5},{8,10},{9,11},{10,... | collective-permute-start | bytes 835592 | tf_op jit(solution)/shard_map/ppermute | solution.py:627
  28.7 22.9 %collective-permute-start.9 = (bf16[4,32,16,128]{3,2,1,0:T(8,128)(2,1)S(1)}, bf16[4,32,16,128]{3,2,1,0:T(8,128)(2,1)S(1)}, u32[]{:S(2)}, u32[]{:S(2)}) collective-permute-start(bf16[4,32,16,128]{3,2,1,0:T(8,128)(2,1)S(1)} %pad_maximum_fusion.refs_0_), channel_id=1, source_target_pairs={{0,6},{1,7},{2,4},{3,5},{4,2},{5,3},{6,0},{7,1},{8,14},{9,15},{10,... | collective-permute-start | bytes 1572872 | tf_op jit(solution)/shard_map/ppermute | solution.py:627
  31.5 2.2 %collective-permute-start.12 = (bf16[4,17,16,128]{3,2,1,0:T(8,128)(2,1)S(1)}, bf16[4,17,16,128]{3,2,1,0:T(8,128)(2,1)S(1)}, u32[]{:S(2)}, u32[]{:S(2)}) collective-permute-start(bf16[4,17,16,128]{3,2,1,0:T(8,128)(2,1)S(1)} %collective-permute-done.4.refs_2_), channel_id=1, source_target_pairs={{0,1},{1,0},{2,3},{3,2},{4,5},{5,4},{6,7},{7,6},{8,9},{9,8},{10,11... | collective-permute-start | bytes 835592 | tf_op jit(solution)/shard_map/ppermute | solution.py:627
  31.5 2.2 %collective-permute-start.13 = (bf16[4,17,16,128]{3,2,1,0:T(8,128)(2,1)S(1)}, bf16[4,17,16,128]{3,2,1,0:T(8,128)(2,1)S(1)}, u32[]{:S(2)}, u32[]{:S(2)}) collective-permute-start(bf16[4,17,16,128]{3,2,1,0:T(8,128)(2,1)S(1)} %collective-permute-done.5.refs_3_), channel_id=1, source_target_pairs={{0,1},{1,0},{2,3},{3,2},{4,5},{5,4},{6,7},{7,6},{8,9},{9,8},{10,11... | collective-permute-start | bytes 835592 | tf_op jit(solution)/shard_map/ppermute | solution.py:627
  32.6 22.1 %collective-permute-start.15 = (bf16[4,32,16,128]{3,2,1,0:T(8,128)(2,1)S(1)}, bf16[4,32,16,128]{3,2,1,0:T(8,128)(2,1)S(1)}, u32[]{:S(2)}, u32[]{:S(2)}) collective-permute-start(bf16[4,32,16,128]{3,2,1,0:T(8,128)(2,1)S(1)} %pad_maximum_fusion.refs_0_), channel_id=1, source_target_pairs={{0,4},{1,5},{2,6},{3,7},{4,0},{5,1},{6,2},{7,3},{8,12},{9,13},{10,... | collective-permute-start | bytes 1572872 | tf_op jit(solution)/shard_map/ppermute | solution.py:627
  33.1 21.5 %collective-permute-start.14 = (bf16[4,32,16,128]{3,2,1,0:T(8,128)(2,1)S(1)}, bf16[4,32,16,128]{3,2,1,0:T(8,128)(2,1)S(1)}, u32[]{:S(2)}, u32[]{:S(2)}) collective-permute-start(bf16[4,32,16,128]{3,2,1,0:T(8,128)(2,1)S(1)} %pad_maximum_fusion.refs_0_), channel_id=1, source_target_pairs={{0,2},{1,3},{2,0},{3,1},{4,6},{5,7},{6,4},{7,5},{8,10},{9,11},{10,... | collective-permute-start | bytes 1572872 | tf_op jit(solution)/shard_map/ppermute | solution.py:627
  49.8 4.9 %collective-permute-start.16 = (bf16[4,32,16,128]{3,2,1,0:T(8,128)(2,1)S(1)}, bf16[4,32,16,128]{3,2,1,0:T(8,128)(2,1)S(1)}, u32[]{:S(2)}, u32[]{:S(2)}) collective-permute-start(bf16[4,32,16,128]{3,2,1,0:T(8,128)(2,1)S(1)} %pad_maximum_fusion.refs_0_), channel_id=1, source_target_pairs={{0,1},{1,0},{2,3},{3,2},{4,5},{5,4},{6,7},{7,6},{8,9},{9,8},{10,11... | collective-permute-start | bytes 1572872 | tf_op jit(solution)/shard_map/ppermute | solution.py:627
  51.6 3.0 %collective-permute-start.17 = (bf16[4,32,16,128]{3,2,1,0:T(8,128)(2,1)S(1)}, bf16[4,32,16,128]{3,2,1,0:T(8,128)(2,1)S(1)}, u32[]{:S(2)}, u32[]{:S(2)}) collective-permute-start(bf16[4,32,16,128]{3,2,1,0:T(8,128)(2,1)S(1)} %collective-permute-done.9.refs_3_), channel_id=1, source_target_pairs={{0,1},{1,0},{2,3},{3,2},{4,5},{5,4},{6,7},{7,6},{8,9},{9,8},{10,11... | collective-permute-start | bytes 1572872 | tf_op jit(solution)/shard_map/ppermute | solution.py:627
  54.7 2.6 %collective-permute-start.19 = (bf16[4,32,16,128]{3,2,1,0:T(8,128)(2,1)S(1)}, bf16[4,32,16,128]{3,2,1,0:T(8,128)(2,1)S(1)}, u32[]{:S(2)}, u32[]{:S(2)}) collective-permute-start(bf16[4,32,16,128]{3,2,1,0:T(8,128)(2,1)S(1)} %collective-permute-done.15.refs_2_), channel_id=1, source_target_pairs={{0,1},{1,0},{2,3},{3,2},{4,5},{5,4},{6,7},{7,6},{8,9},{9,8},{10,11... | collective-permute-start | bytes 1572872 | tf_op jit(solution)/shard_map/ppermute | solution.py:627
  77.1 5.1 %collective-permute-start.20 = (bf16[16,33,16,128]{3,2,1,0:T(8,128)(2,1)S(1)}, bf16[16,33,16,128]{3,2,1,0:T(8,128)(2,1)S(1)}, u32[]{:S(2)}, u32[]{:S(2)}) collective-permute-start(bf16[16,33,16,128]{3,2,1,0:T(8,128)(2,1)S(1)} %get-tuple-element.146), channel_id=1, source_target_pairs={{0,1},{1,0},{2,3},{3,2},{4,5},{5,4},{6,7},{7,6},{8,9},{9,8},{10,11... | collective-permute-start | bytes 6488072 | tf_op jit(solution)/shard_map/ppermute | solution.py:627
  77.3 4.9 %collective-permute-start.21 = (f32[4,16,16,128]{3,2,1,0:T(8,128)S(1)}, f32[4,16,16,128]{3,2,1,0:T(8,128)S(1)}, u32[]{:S(2)}, u32[]{:S(2)}) collective-permute-start(f32[4,16,16,128]{3,2,1,0:T(8,128)S(1)} %get-tuple-element.147), channel_id=1, source_target_pairs={{0,1},{1,0},{2,3},{3,2},{4,5},{5,4},{6,7},{7,6},{8,9},{9,8},{10,11... | collective-permute-start | bytes 1572872 | tf_op jit(solution)/shard_map/ppermute | solution.py:627
  83.2 29.8 %collective-permute-start.23 = (bf16[148,16,128]{2,1,0:T(8,128)(2,1)S(1)}, bf16[148,16,128]{2,1,0:T(8,128)(2,1)S(1)}, u32[]{:S(2)}, u32[]{:S(2)}) collective-permute-start(bf16[148,16,128]{2,1,0:T(8,128)(2,1)S(1)} %get-tuple-element.171), channel_id=1, source_target_pairs={{0,2},{1,3},{2,0},{3,1},{4,6},{5,7},{6,4},{7,5},{8,10},{9,11},{10,... | collective-permute-start | bytes 1818632 | tf_op jit(solution)/shard_map/ppermute | solution.py:627
  84.6 28.4 %collective-permute-start.24 = (bf16[148,16,128]{2,1,0:T(8,128)(2,1)S(1)}, bf16[148,16,128]{2,1,0:T(8,128)(2,1)S(1)}, u32[]{:S(2)}, u32[]{:S(2)}) collective-permute-start(bf16[148,16,128]{2,1,0:T(8,128)(2,1)S(1)} %get-tuple-element.172), channel_id=1, source_target_pairs={{0,4},{1,5},{2,6},{3,7},{4,0},{5,1},{6,2},{7,3},{8,12},{9,13},{10,... | collective-permute-start | bytes 1818632 | tf_op jit(solution)/shard_map/ppermute | solution.py:627
  86.1 27.1 %collective-permute-start.25 = (bf16[148,16,128]{2,1,0:T(8,128)(2,1)S(1)}, bf16[148,16,128]{2,1,0:T(8,128)(2,1)S(1)}, u32[]{:S(2)}, u32[]{:S(2)}) collective-permute-start(bf16[148,16,128]{2,1,0:T(8,128)(2,1)S(1)} %get-tuple-element.173), channel_id=1, source_target_pairs={{0,6},{1,7},{2,4},{3,5},{4,2},{5,3},{6,0},{7,1},{8,14},{9,15},{10,... | collective-permute-start | bytes 1818632 | tf_op jit(solution)/shard_map/ppermute | solution.py:627
  109.8 3.5 %collective-permute-start.22 = (f32[3080,128]{1,0:T(8,128)S(1)}, f32[3080,128]{1,0:T(8,128)S(1)}, u32[]{:S(2)}, u32[]{:S(2)}) collective-permute-start(f32[3080,128]{1,0:T(8,128)S(1)} %get-tuple-element.165), channel_id=1, source_target_pairs={{0,1},{1,0},{2,3},{3,2},{4,5},{5,4},{6,7},{7,6},{8,9},{9,8},{10,11... | collective-permute-start | bytes 4730888 | tf_op jit(solution)/shard_map/ppermute | solution.py:627
  114.0 7.2 %collective-permute-start.26 = (bf16[49,16,128]{2,1,0:T(8,128)(2,1)S(1)}, bf16[49,16,128]{2,1,0:T(8,128)(2,1)S(1)}, u32[]{:S(2)}, u32[]{:S(2)}) collective-permute-start(bf16[49,16,128]{2,1,0:T(8,128)(2,1)S(1)} %get-tuple-element.186), channel_id=1, source_target_pairs={{0,2},{1,3},{2,0},{3,1},{4,6},{5,7},{6,4},{7,5},{8,10},{9,11},{10,... | collective-permute-start | bytes 602120 | tf_op jit(solution)/shard_map/ppermute | solution.py:627
  115.4 7.9 %collective-permute-start.27 = (bf16[49,16,128]{2,1,0:T(8,128)(2,1)S(1)}, bf16[49,16,128]{2,1,0:T(8,128)(2,1)S(1)}, u32[]{:S(2)}, u32[]{:S(2)}) collective-permute-start(bf16[49,16,128]{2,1,0:T(8,128)(2,1)S(1)} %get-tuple-element.187), channel_id=1, source_target_pairs={{0,4},{1,5},{2,6},{3,7},{4,0},{5,1},{6,2},{7,3},{8,12},{9,13},{10,... | collective-permute-start | bytes 602120 | tf_op jit(solution)/shard_map/ppermute | solution.py:627
  116.9 9.8 %collective-permute-start.28 = (bf16[49,16,128]{2,1,0:T(8,128)(2,1)S(1)}, bf16[49,16,128]{2,1,0:T(8,128)(2,1)S(1)}, u32[]{:S(2)}, u32[]{:S(2)}) collective-permute-start(bf16[49,16,128]{2,1,0:T(8,128)(2,1)S(1)} %get-tuple-element.188), channel_id=1, source_target_pairs={{0,6},{1,7},{2,4},{3,5},{4,2},{5,3},{6,0},{7,1},{8,14},{9,15},{10,... | collective-permute-start | bytes 602120 | tf_op jit(solution)/shard_map/ppermute | solution.py:627
  118.4 10.4 %collective-permute-start.32 = (bf16[33,16,128]{2,1,0:T(8,128)(2,1)S(1)}, bf16[33,16,128]{2,1,0:T(8,128)(2,1)S(1)}, u32[]{:S(2)}, u32[]{:S(2)}) collective-permute-start(bf16[33,16,128]{2,1,0:T(8,128)(2,1)S(1)} %get-tuple-element.194), channel_id=1, source_target_pairs={{0,8},{1,9},{2,10},{3,11},{4,12},{5,13},{6,14},{7,15},{8,0},{9,1},... | collective-permute-start | bytes 405512 | tf_op jit(solution)/shard_map/ppermute | solution.py:627
  118.9 13.6 %collective-permute-start.33 = (bf16[33,16,128]{2,1,0:T(8,128)(2,1)S(1)}, bf16[33,16,128]{2,1,0:T(8,128)(2,1)S(1)}, u32[]{:S(2)}, u32[]{:S(2)}) collective-permute-start(bf16[33,16,128]{2,1,0:T(8,128)(2,1)S(1)} %get-tuple-element.195), channel_id=1, source_target_pairs={{0,16},{1,17},{2,18},{3,19},{4,20},{5,21},{6,22},{7,23},{8,24},{9,... | collective-permute-start | bytes 405512 | tf_op jit(solution)/shard_map/ppermute | solution.py:627
  121.2 11.3 %collective-permute-start.34 = (bf16[33,16,128]{2,1,0:T(8,128)(2,1)S(1)}, bf16[33,16,128]{2,1,0:T(8,128)(2,1)S(1)}, u32[]{:S(2)}, u32[]{:S(2)}) collective-permute-start(bf16[33,16,128]{2,1,0:T(8,128)(2,1)S(1)} %get-tuple-element.196), channel_id=1, source_target_pairs={{0,24},{1,25},{2,26},{3,27},{4,28},{5,29},{6,30},{7,31},{8,16},{9,... | collective-permute-start | bytes 405512 | tf_op jit(solution)/shard_map/ppermute | solution.py:627
  127.3 6.5 %collective-permute-start.29 = (bf16[17,16,128]{2,1,0:T(8,128)(2,1)S(1)}, bf16[17,16,128]{2,1,0:T(8,128)(2,1)S(1)}, u32[]{:S(2)}, u32[]{:S(2)}) collective-permute-start(bf16[17,16,128]{2,1,0:T(8,128)(2,1)S(1)} %get-tuple-element.203), channel_id=1, source_target_pairs={{0,8},{1,9},{2,10},{3,11},{4,12},{5,13},{6,14},{7,15},{8,0},{9,1},... | collective-permute-start | bytes 208904 | tf_op jit(solution)/shard_map/ppermute | solution.py:627
  127.8 10.5 %collective-permute-start.30 = (bf16[17,16,128]{2,1,0:T(8,128)(2,1)S(1)}, bf16[17,16,128]{2,1,0:T(8,128)(2,1)S(1)}, u32[]{:S(2)}, u32[]{:S(2)}) collective-permute-start(bf16[17,16,128]{2,1,0:T(8,128)(2,1)S(1)} %get-tuple-element.204), channel_id=1, source_target_pairs={{0,16},{1,17},{2,18},{3,19},{4,20},{5,21},{6,22},{7,23},{8,24},{9,... | collective-permute-start | bytes 208904 | tf_op jit(solution)/shard_map/ppermute | solution.py:627
  128.8 9.5 %collective-permute-start.31 = (bf16[17,16,128]{2,1,0:T(8,128)(2,1)S(1)}, bf16[17,16,128]{2,1,0:T(8,128)(2,1)S(1)}, u32[]{:S(2)}, u32[]{:S(2)}) collective-permute-start(bf16[17,16,128]{2,1,0:T(8,128)(2,1)S(1)} %get-tuple-element.205), channel_id=1, source_target_pairs={{0,24},{1,25},{2,26},{3,27},{4,28},{5,29},{6,30},{7,31},{8,16},{9,... | collective-permute-start | bytes 208904 | tf_op jit(solution)/shard_map/ppermute | solution.py:627
  (12 other events, 77.2 us)
